TPU v7x, 256 devices: a whole 4x4x8 slice. The times are simulated.
256 devices in a mesh: span: 64 (over z, y, core), plane: 4 (over x).
Axes of the slice: x: 4, y: 4, z: 8, core: 2. Of those that a mesh axis runs over, the one named last changes fastest.
Arguments:
- adjoint: float32 [3, 256, 81, 512], P(None, 'span', None, 'plane'), may hold values from -6 to 6
- checkpoints: bfloat16 [8, 2, 256, 81, 512], P(None, None, 'span', None, 'plane'), may hold values from -4 to 4
- checkpoint_step: int32 [3], replicated, may hold values from 0 to 7
- metric: float32 [2, 512], P(None, 'plane'), may hold values from 0.004 to 0.016
- helmholtz_inverse: float32 [256, 81, 81], P('span'), may hold values from -0.08 to 0.8
- wall_element: int32 [1024, 2], replicated, may hold values from 0 to 511
- wall_local: int32 [1024, 2], replicated, may hold values from 0 to 80
- wall_weight: float32 [256, 1024], P('span'), may hold values from 0.7 to 140
Outputs:
- adjoint_next: float32 [3, 256, 81, 512], P(None, 'span', None, 'plane')
- control_gradient: float32 [256, 1024], P('span', 'plane')
All inputs are finite; a program needn't handle non-finite values.
Results may differ from a plain program's by a relative error of at most 0.00065.
Values may be sent and summed in bfloat16 or wider, within the bound.
No kernel may reach another device: no remote copies, remote signals or barrier semaphores. Data moves between devices by JAX's collectives and lax.ppermute only.
A program may use at most 128 MiB of HBM per device.

v0:
```python
import jax
import jax.numpy as jnp
import numpy as np
from jax import lax
from jax.experimental import pallas as pl
from jax.experimental.pallas import tpu as pltpu
from jax.sharding import PartitionSpec as P

P_SIZE = 8
Q = 81
QP = 88
NSTEP = 3
HIGHEST = lax.Precision.HIGHEST
F32 = jnp.float32
VMEM_BYTES = 56 * 1024 * 1024


def chebyshev_matrix(degree):
    points = np.arange(degree + 1)
    abscissa = np.cos(np.pi * points / degree)
    signed = np.where((points == 0) | (points == degree), 2.0, 1.0) * (-1.0) ** points
    spacing = abscissa[:, None] - abscissa[None, :] + np.eye(degree + 1)
    matrix = signed[:, None] / signed[None, :] / spacing
    return matrix - np.eye(degree + 1) * np.sum(matrix, axis=1)[:, None]


def fourier_table(length):
    row_index = np.arange(length)[:, None]
    column = np.arange(length)[None, :]
    wavenumber = (row_index + 1) // 2
    phase_angle = 2.0 * np.pi * wavenumber * column / length
    parity = row_index % 2
    base_rows = np.where(
        row_index == 0, 1.0, np.where(parity == 1, np.cos(phase_angle), np.sin(phase_angle))
    )
    row_scale = np.where(
        (row_index == 0) | (row_index == length - 1), 1.0 / np.sqrt(length), np.sqrt(2.0 / length)
    )
    return base_rows * row_scale


def tables():
    zl = np.arange(256)
    z_of = 4 * (zl % 64) + zl // 64
    jl = np.arange(256)
    j_of = (jl % 128) // 4 * 8 + jl // 128 * 4 + jl % 4
    f = fourier_table(256).astype(np.float32)
    back = f[j_of][:, z_of]
    d = chebyshev_matrix(P_SIZE)
    eye = np.eye(P_SIZE + 1)
    both = np.zeros((2 * QP, QP), np.float32)
    both[:Q, :Q] = np.kron(d, eye)
    both[QP : QP + Q, :Q] = np.kron(eye, d)
    return np.ascontiguousarray(back.T), back, both


def vmem_spec():
    return pl.BlockSpec(memory_space=pltpu.VMEM)


def smem_spec():
    return pl.BlockSpec(memory_space=pltpu.SMEM)


def params():
    return pltpu.CompilerParams(vmem_limit_bytes=VMEM_BYTES)


def pack_inverse_kernel(h_ref, o_ref, t_ref):
    o_ref[...] = jnp.zeros_like(o_ref)
    for j in range(4):
        t_ref[j] = h_ref[j].T
        for r in range(Q):
            start = r * QP
            row, lane = divmod(start, 128)
            first = min(Q, 128 - lane)
            o_ref[j, row, lane : lane + first] = t_ref[j, r, 0:first]
            if first < Q:
                o_ref[j, row + 1, 0 : Q - first] = t_ref[j, r, first:Q]


def pack_inverse(inverse):
    return pl.pallas_call(
        pack_inverse_kernel,
        out_shape=jax.ShapeDtypeStruct((4, 56, 128), F32),
        in_specs=[vmem_spec()],
        out_specs=vmem_spec(),
        scratch_shapes=[pltpu.VMEM((4, Q, Q), F32)],
        compiler_params=params(),
    )(inverse)


def pack_points_kernel(step_ref, adj_ref, c0_ref, c1_ref, c2_ref, o_ref, t_ref):
    stored = (c0_ref, c1_ref, c2_ref)
    for z in range(4):
        for g in range(3):
            t_ref[g, z, 3 * Q : 256, :] = jnp.zeros((256 - 3 * Q, 128), F32)
            for i in range(3):
                if g == 0:
                    block = adj_ref[i, z]
                else:
                    block = stored[i][0, g - 1, z].astype(F32)
                t_ref[g, z, i * Q : (i + 1) * Q, :] = block
            turned = t_ref[g, z].T
            for e in range(2):
                o_ref[:, z * 2 + e, g * 256 : (g + 1) * 256] = turned[e * 64 : (e + 1) * 64, :]


def pack_points(adjoint, checkpoints, checkpoint_step):
    def slot(k):
        return pl.BlockSpec((1, 2, 4, Q, 128), lambda i, st: (st[k], 0, 0, 0, 0))

    return pl.pallas_call(
        pack_points_kernel,
        out_shape=jax.ShapeDtypeStruct((64, 8, 768), F32),
        grid_spec=pltpu.PrefetchScalarGridSpec(
            num_scalar_prefetch=1,
            grid=(1,),
            in_specs=[
                pl.BlockSpec((3, 4, Q, 128), lambda i, st: (0, 0, 0, 0)),
                slot(0),
                slot(1),
                slot(2),
            ],
            out_specs=pl.BlockSpec((64, 8, 768), lambda i, st: (0, 0, 0)),
            scratch_shapes=[pltpu.VMEM((3, 4, 256, 128), F32)],
        ),
        compiler_params=params(),
    )(checkpoint_step, adjoint, checkpoints, checkpoints, checkpoints)


def steps_kernel(
    place_ref, metric_ref, r_ref, own_ref, other_ref, fwd_ref, back_ref, both_ref,
    adj_ref, wall_ref,
    ht, x, v, coef, solved, wall, turn,
):
    chip = place_ref[0]
    core = place_ref[1]

    def turn_inverse(k, carry):
        row = pl.multiple_of(k * 128, 128)
        ht[core, pl.ds(row, 128), :] = own_ref[:, k, :].T
        ht[1 - core, pl.ds(row, 128), :] = other_ref[:, k, :].T
        return carry

    lax.fori_loop(0, 56, turn_inverse, 0)

    x[...] = jnp.zeros_like(x)
    v[...] = jnp.zeros_like(v)
    for e in range(2):
        for g in range(3):
            stack = jnp.concatenate(
                [r_ref[:, z * 2 + e, g * 256 : (g + 1) * 256] for z in range(4)], axis=0
            )
            turn[...] = stack.T
            for i in range(3):
                part = turn[i * Q : (i + 1) * Q, :]
                if g == 0:
                    x[e * 3 + i, 0:Q, :] = part
                else:
                    v[(g - 1), e, i, 0:Q, :] = part

    for step in range(NSTEP):
        for e in range(2):
            m0 = metric_ref[0, chip + 64 * e]
            m1 = metric_ref[1, chip + 64 * e]
            for c in range(3):
                field = x[e * 3 + c]
                slopes = jnp.dot(both_ref[...], field, precision=HIGHEST, preferred_element_type=F32)
                x[e * 3 + c] = (
                    field
                    + v[0, e, step] * (m0 * slopes[0:QP])
                    + v[1, e, step] * (m1 * slopes[QP : 2 * QP])
                )
        modes = jnp.dot(
            x[...].reshape(6 * QP, 256), fwd_ref[...], precision=HIGHEST, preferred_element_type=F32
        )
        coef[0] = modes[:, 0:128]
        coef[1] = modes[:, 128:256]
        for half in range(2):
            for e in range(2):

                def column(r, sums, half=half, e=e):
                    h = ht[half, pl.ds(pl.multiple_of(r * QP, 8), QP), :]
                    return tuple(
                        sums[c] + h * coef[half, pl.ds((e * 3 + c) * QP + r, 1), :] for c in range(3)
                    )

                zero = jnp.zeros((QP, 128), F32)
                sums = lax.fori_loop(0, Q, column, (zero, zero, zero), unroll=3)
                for c in range(3):
                    solved[e * 3 + c, :, half * 128 : (half + 1) * 128] = sums[c]
        planes = jnp.dot(
            solved[...].reshape(6 * QP, 256), back_ref[...], precision=HIGHEST, preferred_element_type=F32
        )
        x[...] = planes.reshape(6, QP, 256)
        for e in range(2):
            product = x[e * 3 + 1] * v[1, e, step]
            if step == 0:
                wall[e, 0:QP] = product
            else:
                wall[e, 0:QP] = wall[e, 0:QP] + product

    for e in range(2):
        wall[e, QP:128, :] = jnp.zeros((128 - QP, 256), F32)
        turned = wall[e].T
        for z in range(4):
            wall_ref[:, z * 2 + e, :] = turned[z * 64 : (z + 1) * 64, :]
        turn[3 * Q : 256, :] = jnp.zeros((256 - 3 * Q, 256), F32)
        for c in range(3):
            turn[c * Q : (c + 1) * Q, :] = x[e * 3 + c, 0:Q, :]
        turned = turn[...].T
        for z in range(4):
            adj_ref[:, z * 2 + e, :] = turned[z * 64 : (z + 1) * 64, :]


def steps(place, metric, points, own, other):
    fwd, back, both = tables()
    return pl.pallas_call(
        steps_kernel,
        out_shape=(
            jax.ShapeDtypeStruct((64, 8, 256), F32),
            jax.ShapeDtypeStruct((64, 8, 128), F32),
        ),
        in_specs=[smem_spec(), smem_spec()] + [vmem_spec()] * 6,
        out_specs=(vmem_spec(), vmem_spec()),
        scratch_shapes=[
            pltpu.VMEM((2, 56 * 128, 128), F32),
            pltpu.VMEM((6, QP, 256), F32),
            pltpu.VMEM((2, 2, 3, QP, 256), F32),
            pltpu.VMEM((2, 6 * QP, 128), F32),
            pltpu.VMEM((6, QP, 256), F32),
            pltpu.VMEM((2, 128, 256), F32),
            pltpu.VMEM((256, 256), F32),
        ],
        compiler_params=params(),
    )(place, metric, points, own, other, jnp.asarray(fwd), jnp.asarray(back), jnp.asarray(both))


def wall_kernel(r_ref, local_ref, element_ref, o_ref):
    points = local_ref.shape[1]
    mode = lax.broadcasted_iota(jnp.int32, (128, points), 0)
    pick = jnp.where(mode == local_ref[...], 1.0, 0.0).astype(jnp.bfloat16)
    here = mode == element_ref[...]
    for z in range(4):
        field = jnp.concatenate([r_ref[:, z * 2, :], r_ref[:, z * 2 + 1, :]], axis=0)
        high = field.astype(jnp.bfloat16)
        rest = field - high.astype(F32)
        middle = rest.astype(jnp.bfloat16)
        low = (rest - middle.astype(F32)).astype(jnp.bfloat16)
        values = (
            jnp.dot(low, pick, preferred_element_type=F32)
            + jnp.dot(middle, pick, preferred_element_type=F32)
            + jnp.dot(high, pick, preferred_element_type=F32)
        )
        total = jnp.sum(jnp.where(here, values, 0.0), axis=0, keepdims=True)
        o_ref[z : z + 1, :] = total[:, 0 : points // 2] + total[:, points // 2 :]


def wall_sums(received, local, element):
    return pl.pallas_call(
        wall_kernel,
        out_shape=jax.ShapeDtypeStruct((4, local.shape[1] // 2), F32),
        in_specs=[vmem_spec()] * 3,
        out_specs=vmem_spec(),
        compiler_params=params(),
    )(received, local, element)


def unpack_kernel(r_ref, o_ref, t_ref):
    for z in range(4):
        stack = jnp.concatenate([r_ref[:, z * 2, :], r_ref[:, z * 2 + 1, :]], axis=0)
        t_ref[z] = stack.T
        for c in range(3):
            o_ref[c, z] = t_ref[z, c * Q : (c + 1) * Q, :]


def unpack(received):
    return pl.pallas_call(
        unpack_kernel,
        out_shape=jax.ShapeDtypeStruct((3, 4, Q, 128), F32),
        in_specs=[vmem_spec()],
        out_specs=vmem_spec(),
        scratch_shapes=[pltpu.VMEM((4, 256, 128), F32)],
        compiler_params=params(),
    )(received)


def on_device(
    adjoint,
    checkpoints,
    checkpoint_step,
    metric,
    helmholtz_inverse,
    wall_element,
    wall_local,
    wall_weight,
):
    span = lax.axis_index("span")
    plane = lax.axis_index("plane")
    span_count = lax.axis_size("span")
    plane_count = lax.axis_size("plane")
    wall_count = wall_element.shape[0]
    place = jnp.stack([span, span % 2]).astype(jnp.int32)

    packed = pack_inverse(helmholtz_inverse)
    same_core = [list(range(core, span_count, 2)) for core in range(2)]
    own = lax.all_gather(packed, "span", axis=0, tiled=True, axis_index_groups=same_core)
    other = lax.ppermute(own, "span", [(i, i ^ 1) for i in range(span_count)])

    sent = pack_points(adjoint, checkpoints, checkpoint_step)
    points = lax.all_to_all(sent, "span", 0, 0, tiled=True)
    adj_out, wall_out = steps(place, metric, points, own, other)

    wall_in = lax.all_to_all(wall_out, "span", 0, 0, tiled=True)
    adj_in = lax.all_to_all(adj_out, "span", 0, 0, tiled=True)

    local = wall_local.T.reshape(1, 2 * wall_count)
    element = wall_element.T.reshape(1, 2 * wall_count) - plane * adjoint.shape[3]
    partial_sum = wall_sums(wall_in, local, element)
    gradient = partial_sum
    for k in range(1, plane_count):
        gradient = gradient + lax.ppermute(
            partial_sum, "plane", [(i, (i + k) % plane_count) for i in range(plane_count)]
        )
    weighted = wall_weight * gradient
    square = jnp.sum(weighted * weighted)
    squares = lax.all_to_all(
        jnp.broadcast_to(square, (span_count, 1, 128)), "span", 0, 0, tiled=True
    )
    total = jnp.sum(squares[:, 0, 0])
    share_width = wall_count // plane_count
    share = lax.dynamic_slice_in_dim(weighted, plane * share_width, share_width, 1)
    inverse_rms = lax.rsqrt(total / (adjoint.shape[1] * span_count * wall_count) + 1e-06)
    return (unpack(adj_in), share * inverse_rms)


def solution(mesh):
    placed = (
        P(None, "span", None, "plane"),
        P(None, None, "span", None, "plane"),
        P(),
        P(None, "plane"),
        P("span", None, None),
        P(),
        P(),
        P("span", None),
    )
    return jax.shard_map(
        on_device,
        mesh=mesh,
        in_specs=placed,
        out_specs=(P(None, "span", None, "plane"), P("span", "plane")),
        check_vma=False,
    )
```

profile of v0, /device:TPU:1, one launch (start us, length us, event | category | flops | bytes accessed | tf_op | source)
XLA Modules:
  0.0 266.4 jit_solution(7919288858451454722)
XLA Ops:
  7.2 0.0 copy-start.2
  7.2 0.0 all-gather.2.cloned.1.call-start
  7.2 1.7 copy.35.h_ref
  8.9 2.3 shard_map.123
  11.2 0.0 all-gather.2.cloned.1.call-update
  11.2 81.7 %all-gather.2.cloned.1.call-done.own_ref = f32[128,56,128]{2,1,0:T(8,128)} async-done(((f32[4,56,128]{2,1,0:T(8,128)}), f32[128,56,128]{2,1,0:T(8,128)}) %all-gather.2.cloned.1.call-update) | async-done | bytes 3670032 | tf_op jit(solution)/shard_map/all_gather | solution.py:308
  92.9 3.9 %collective-permute-start = (f32[128,56,128]{2,1,0:T(8,128)}, f32[128,56,128]{2,1,0:T(8,128)}, u32[]{:S(2)}, u32[]{:S(2)}) collective-permute-start(f32[128,56,128]{2,1,0:T(8,128)} %all-gather.2.cloned.1.call-done.own_ref), channel_id=1, source_target_pairs={{0,4},{4,0},{8,12},{12,8},{16,20},{20,16},{24,28},{28,24},{32,36},... | collective-permute-start | bytes 11010056 | tf_op jit(solution)/shard_map/ppermute | solution.py:309
  96.8 1.9 copy.31.adj_ref
  98.7 0.0 copy-done.2
  98.7 1.3 copy.32.c0_ref.c1_ref.c2_ref
  100.1 3.7 %shard_map.122 = f32[64,8,768]{2,1,0:T(8,128)} custom-call(s32[3]{0:T(128)} %step_ref.1, f32[3,4,81,128]{3,2,1,0:T(8,128)} %copy.31.adj_ref, bf16[8,2,4,81,128]{4,3,2,1,0:T(8,128)(2,1)} %copy.32.c0_ref.c1_ref.c2_ref, bf16[8,2,4,81,128]{4,3,2,1,0:T(8,128)(2,1)} %copy.32.c0_ref.c1_ref.c2_ref, bf16[8,2,4,81,128]{4,3,2,1,0:T(8,128)(2,1)} %copy.32.c0_ref.c1_ref.c2_ref), custom_call_target="tpu_custom_call" | custom-call | tf_op jit(solution)/shard_map/pallas_call | solution.py:113
  103.8 5.7 %all-to-all-start = ((f32[64,8,768]{2,1,0:T(8,128)}), f32[64,8,768]{2,1,0:T(8,128)S(1)}, u32[]{:S(2)}, u32[]{:S(2)}) async-start(f32[64,8,768]{2,1,0:T(8,128)} %shard_map.122), calls=%async_computation | async-start | bytes 3145728 | tf_op jit(solution)/shard_map/all_to_all | solution.py:312
  109.5 0.6 pad_add_fusion.place_ref
  110.1 0.0 copy-start.5
  110.1 0.0 copy-start.6
  110.1 0.0 copy-start.4
  110.1 38.3 %all-to-all-done.r_ref = f32[64,8,768]{2,1,0:T(8,128)S(1)} async-done(((f32[64,8,768]{2,1,0:T(8,128)}), f32[64,8,768]{2,1,0:T(8,128)S(1)}, u32[]{:S(2)}, u32[]{:S(2)}) %all-to-all-start) | async-done | bytes 1572896 | tf_op jit(solution)/shard_map/all_to_all | solution.py:312
  148.5 0.0 copy-start
  148.5 0.0 collective-permute-done.other_ref
  148.5 1.2 copy-done
  149.7 33.8 %shard_map.124 = (f32[64,8,256]{2,1,0:T(8,128)}, f32[64,8,128]{2,1,0:T(8,128)}) custom-call(s32[2]{0:T(128)} %pad_add_fusion.place_ref, f32[2,128]{1,0:T(2,128)} %metric_ref.1, f32[64,8,768]{2,1,0:T(8,128)} %copy-done, f32[128,56,128]{2,1,0:T(8,128)} %all-gather.2.cloned.1.call-done.own_ref, f32[128,56,128]{2,1,0:T(8,128)} %collective-permute-done.other_ref, ...), custom_call_target="tpu_custom_call" | custom-call | tf_op jit(solution)/shard_map/pallas_call | solution.py:219
  183.5 6.5 %all-to-all-start.2 = ((f32[64,8,128]{2,1,0:T(8,128)}), f32[64,8,128]{2,1,0:T(8,128)S(1)}, u32[]{:S(2)}, u32[]{:S(2)}) async-start(f32[64,8,128]{2,1,0:T(8,128)} %get-tuple-element.5), calls=%async_computation.2 | async-start | bytes 524288 | tf_op jit(solution)/shard_map/all_to_all | solution.py:315
  190.0 0.0 copy-done.5
  190.0 0.6 copy.39
  190.6 0.0 copy-done.6
  190.6 0.6 copy.40
  191.2 11.9 %all-to-all-done.2.r_ref = f32[64,8,128]{2,1,0:T(8,128)S(1)} async-done(((f32[64,8,128]{2,1,0:T(8,128)}), f32[64,8,128]{2,1,0:T(8,128)S(1)}, u32[]{:S(2)}, u32[]{:S(2)}) %all-to-all-start.2) | async-done | bytes 262176 | tf_op jit(solution)/shard_map/all_to_all | solution.py:315
  203.1 0.0 copy-start.3
  203.1 0.7 copy-done.3
  203.8 3.7 %shard_map.126 = f32[4,1024]{1,0:T(4,128)} custom-call(f32[64,8,128]{2,1,0:T(8,128)} %copy-done.3, s32[1,2048]{1,0:T(1,128)} %bitcast.11, s32[1,2048]{1,0:T(1,128)} %bitcast.12), custom_call_target="tpu_custom_call" | custom-call | tf_op jit(solution)/shard_map/pallas_call | solution.py:261
  207.5 2.4 collective-permute-start.3
  209.9 0.6 collective-permute-start.2
  210.5 0.6 collective-permute-start.1
  211.1 0.0 collective-permute-done.3
  211.1 3.2 %collective-permute-done.2 = f32[4,1024]{1,0:T(4,128)S(1)} collective-permute-done((f32[4,1024]{1,0:T(4,128)}, f32[4,1024]{1,0:T(4,128)S(1)}, u32[]{:S(2)}, u32[]{:S(2)}) %collective-permute-start.2) | collective-permute-done | bytes 16416 | tf_op jit(solution)/shard_map/ppermute | solution.py:323
  214.2 0.3 collective-permute-done.1
  214.5 0.0 copy-done.4
  214.5 1.3 multiply_reduce_fusion
  215.9 0.7 broadcast_in_dim.3
  216.5 15.6 %all_to_all.20 = f32[64,1,128]{2,1,0:T(1,128)S(1)} all-to-all(f32[64,1,128]{2,1,0:T(1,128)S(1)} %broadcast_in_dim.3), channel_id=1, replica_groups=mesh['span'=64,'plane'=4] {'span'}, dimensions={0} | all-to-all | bytes 65536 | tf_op jit(solution)/shard_map/all_to_all | solution.py:328
  232.1 4.7 %all-to-all-start.1 = ((f32[64,8,256]{2,1,0:T(8,128)}), f32[64,8,256]{2,1,0:T(8,128)S(1)}, u32[]{:S(2)}, u32[]{:S(2)}) async-start(f32[64,8,256]{2,1,0:T(8,128)} %get-tuple-element.4), calls=%async_computation.1 | async-start | bytes 1048576 | tf_op jit(solution)/shard_map/all_to_all | solution.py:316
  236.9 0.7 slice_reduce_fusion
  238.2 0.6 dynamic-slice_multiply_fusion
  238.8 15.9 %all-to-all-done.1.r_ref = f32[64,8,256]{2,1,0:T(8,128)S(1)} async-done(((f32[64,8,256]{2,1,0:T(8,128)}), f32[64,8,256]{2,1,0:T(8,128)S(1)}, u32[]{:S(2)}, u32[]{:S(2)}) %all-to-all-start.1) | async-done | bytes 524320 | tf_op jit(solution)/shard_map/all_to_all | solution.py:316
  254.7 0.0 copy-start.1
  254.7 0.8 copy-done.1
  255.5 2.1 shard_map.125
  257.6 2.0 copy.37
  (1 shorter events, 0.0 us)
Async XLA Ops:
  7.2 91.5 %copy-start.2 = (bf16[8,2,4,81,128]{4,2,3,1,0:T(4,128)(2,1)S(1)}, bf16[8,2,4,81,128]{4,2,3,1,0:T(4,128)(2,1)}, u32[]{:S(2)}) copy-start(bf16[8,2,4,81,128]{4,2,3,1,0:T(4,128)(2,1)} %param.12) | copy-start | bytes 3981316
  7.2 85.7 %all-gather.2.cloned.1.call-start = ((), (), s32[]{:S(2)}) async-start(), calls=%async_computation.4 | async-start | bytes 3784704 | tf_op jit(solution)/shard_map/all_gather | solution.py:308
  92.9 55.6 %collective-permute-start = (f32[128,56,128]{2,1,0:T(8,128)}, f32[128,56,128]{2,1,0:T(8,128)}, u32[]{:S(2)}, u32[]{:S(2)}) collective-permute-start(f32[128,56,128]{2,1,0:T(8,128)} %all-gather.2.cloned.1.call-done.own_ref), channel_id=1, source_target_pairs={{0,4},{4,0},{8,12},{12,8},{16,20},{20,16},{24,28},{28,24},{32,36},... | collective-permute-start | bytes 11010056 | tf_op jit(solution)/shard_map/ppermute | solution.py:309
  103.8 44.7 %all-to-all-start = ((f32[64,8,768]{2,1,0:T(8,128)}), f32[64,8,768]{2,1,0:T(8,128)S(1)}, u32[]{:S(2)}, u32[]{:S(2)}) async-start(f32[64,8,768]{2,1,0:T(8,128)} %shard_map.122), calls=%async_computation | async-start | bytes 3145728 | tf_op jit(solution)/shard_map/all_to_all | solution.py:312
  110.1 79.9 %copy-start.5 = (s32[1024,2]{0,1:T(2,128)S(1)}, s32[1024,2]{0,1:T(2,128)}, u32[]{:S(2)}) copy-start(s32[1024,2]{0,1:T(2,128)} %param.17) | copy-start | bytes 24580
  110.1 80.5 %copy-start.6 = (s32[1024,2]{0,1:T(2,128)S(1)}, s32[1024,2]{0,1:T(2,128)}, u32[]{:S(2)}) copy-start(s32[1024,2]{0,1:T(2,128)} %param.16) | copy-start | bytes 24580
  110.1 104.4 %copy-start.4 = (f32[4,1024]{1,0:T(4,128)S(1)}, f32[4,1024]{1,0:T(4,128)}, u32[]{:S(2)}) copy-start(f32[4,1024]{1,0:T(4,128)} %param.18) | copy-start | bytes 49156
  148.5 1.2 copy-start
  183.5 19.6 %all-to-all-start.2 = ((f32[64,8,128]{2,1,0:T(8,128)}), f32[64,8,128]{2,1,0:T(8,128)S(1)}, u32[]{:S(2)}, u32[]{:S(2)}) async-start(f32[64,8,128]{2,1,0:T(8,128)} %get-tuple-element.5), calls=%async_computation.2 | async-start | bytes 524288 | tf_op jit(solution)/shard_map/all_to_all | solution.py:315
  203.1 0.7 copy-start.3
  207.5 3.5 %collective-permute-start.3 = (f32[4,1024]{1,0:T(4,128)}, f32[4,1024]{1,0:T(4,128)S(1)}, u32[]{:S(2)}, u32[]{:S(2)}) collective-permute-start(f32[4,1024]{1,0:T(4,128)} %shard_map.126), channel_id=1, source_target_pairs={{0,3},{1,0},{2,1},{3,2},{4,7},{5,4},{6,5},{7,6},{8,11},{9,8},{10,9... | collective-permute-start | bytes 49160 | tf_op jit(solution)/shard_map/ppermute | solution.py:323
  209.9 4.3 %collective-permute-start.2 = (f32[4,1024]{1,0:T(4,128)}, f32[4,1024]{1,0:T(4,128)S(1)}, u32[]{:S(2)}, u32[]{:S(2)}) collective-permute-start(f32[4,1024]{1,0:T(4,128)} %shard_map.126), channel_id=1, source_target_pairs={{0,2},{1,3},{2,0},{3,1},{4,6},{5,7},{6,4},{7,5},{8,10},{9,11},{10,... | collective-permute-start | bytes 49160 | tf_op jit(solution)/shard_map/ppermute | solution.py:323
  210.5 4.0 %collective-permute-start.1 = (f32[4,1024]{1,0:T(4,128)}, f32[4,1024]{1,0:T(4,128)S(1)}, u32[]{:S(2)}, u32[]{:S(2)}) collective-permute-start(f32[4,1024]{1,0:T(4,128)} %shard_map.126), channel_id=1, source_target_pairs={{0,1},{1,2},{2,3},{3,0},{4,5},{5,6},{6,7},{7,4},{8,9},{9,10},{10,1... | collective-permute-start | bytes 49160 | tf_op jit(solution)/shard_map/ppermute | solution.py:323
  232.1 22.6 %all-to-all-start.1 = ((f32[64,8,256]{2,1,0:T(8,128)}), f32[64,8,256]{2,1,0:T(8,128)S(1)}, u32[]{:S(2)}, u32[]{:S(2)}) async-start(f32[64,8,256]{2,1,0:T(8,128)} %get-tuple-element.4), calls=%async_computation.1 | async-start | bytes 1048576 | tf_op jit(solution)/shard_map/all_to_all | solution.py:316
  254.7 0.8 copy-start.1
Sparse Core Ops, SparseCore 0:
  11.3 81.4 all-gather.1
where the time goes:
time: 267 us; the launch traced here: 266 us
  waiting for transfers between devices  151 us (57%)
  Pallas kernels  45.6 us (17%)
  starting transfers between devices  24.4 us (9%)
  blocking collectives  15.6 us (6%)
  between operations  14.8 us (6%)
  local copies, waits for them, and re-layouts  11.5 us (4%)
  other arithmetic  3.25 us (1%)
    all_gather x1, waiting for transfers between devices, on_device(): lax.all_gather(packed, 'span', axis=0, tiled=True, axis_index_groups=same...  81.7 us
    all_to_all x1, waiting for transfers between devices, on_device(): points = lax.all_to_all(sent, 'span', 0, 0, tiled=True)  38.3 us
    pallas_call x1, Pallas kernels, steps(): pl.pallas_call(steps_kernel, out_shape=(jax.ShapeDtypeStruct((64, 8, 256)...  33.8 us
    all_to_all x1, waiting for transfers between devices, on_device(): adj_in = lax.all_to_all(adj_out, 'span', 0, 0, tiled=True)  15.9 us
    all_to_all x1, blocking collectives, on_device(): lax.all_to_all(jnp.broadcast_to(square, (span_count, 1, 128)), 'span', 0,...  15.6 us
    all_to_all x1, waiting for transfers between devices, on_device(): wall_in = lax.all_to_all(wall_out, 'span', 0, 0, tiled=True)  11.9 us
    unnamed x20, local copies, waits for them, and re-layouts  10.9 us
    all_to_all x1, starting transfers between devices, on_device(): wall_in = lax.all_to_all(wall_out, 'span', 0, 0, tiled=True)  6.46 us
  transfers between devices with their start and end apart: 8, of which 6 were waited for; matrix products, arithmetic and copies ran while one was open for 2% of the time, Pallas kernels for 1%

commit v1 on v0

--- a/solution.py
+++ b/solution.py
@@ -13,6 +13,8 @@
 HIGHEST = lax.Precision.HIGHEST
 F32 = jnp.float32
 VMEM_BYTES = 56 * 1024 * 1024
+LEVELS = 32767.0
+SCALE_LANE = 250
 
 
 def chebyshev_matrix(degree):
@@ -39,19 +41,38 @@
     return base_rows * row_scale
 
 
-def tables():
+def lane_order():
+    chips = np.arange(32)
+    pieces = [(np.arange(64) // 2, np.arange(64) % 2, 0, 0)]
+    for part, shift in ((chips, 3), (chips, 1), (chips[:16], 2), (chips[16:], 2)):
+        for core in range(2):
+            pieces.append((part, np.full(part.shape, core), 1, shift))
+    chip = np.concatenate([p[0] for p in pieces])
+    core = np.concatenate([p[1] for p in pieces])
+    relative = np.concatenate([np.full(p[0].shape, p[2]) for p in pieces])
+    shift = np.concatenate([np.full(p[0].shape, p[3]) for p in pieces])
+    return [v.astype(np.int32) for v in (chip, core, relative, shift)]
+
+
+def transforms(core, plane):
     zl = np.arange(256)
     z_of = 4 * (zl % 64) + zl // 64
-    jl = np.arange(256)
-    j_of = (jl % 128) // 4 * 8 + jl // 128 * 4 + jl % 4
-    f = fourier_table(256).astype(np.float32)
-    back = f[j_of][:, z_of]
+    table = jnp.asarray(fourier_table(256).astype(np.float32)[:, z_of])
+    chip, lane_core, relative, shift = (jnp.asarray(v) for v in lane_order())
+    span_of = 2 * chip + lane_core + relative * core * (1 - 2 * lane_core)
+    order = 4 * span_of + (plane + shift) % 4
+    pick = jnp.where(order[:, None] == jnp.arange(256)[None, :], 1.0, 0.0).astype(F32)
+    back = jnp.dot(pick, table, precision=HIGHEST)
+    return back.T, back
+
+
+def slope_table():
     d = chebyshev_matrix(P_SIZE)
     eye = np.eye(P_SIZE + 1)
     both = np.zeros((2 * QP, QP), np.float32)
     both[:Q, :Q] = np.kron(d, eye)
     both[QP : QP + Q, :Q] = np.kron(eye, d)
-    return np.ascontiguousarray(back.T), back, both
+    return jnp.asarray(both)
 
 
 def vmem_spec():
@@ -66,32 +87,56 @@
     return pltpu.CompilerParams(vmem_limit_bytes=VMEM_BYTES)
 
 
-def pack_inverse_kernel(h_ref, o_ref, t_ref):
-    o_ref[...] = jnp.zeros_like(o_ref)
-    for j in range(4):
-        t_ref[j] = h_ref[j].T
-        for r in range(Q):
-            start = r * QP
-            row, lane = divmod(start, 128)
-            first = min(Q, 128 - lane)
-            o_ref[j, row, lane : lane + first] = t_ref[j, r, 0:first]
-            if first < Q:
-                o_ref[j, row + 1, 0 : Q - first] = t_ref[j, r, first:Q]
-
-
-def pack_inverse(inverse):
+def pair_up(low, high):
+    return (high.astype(jnp.int32) << 16) | (low.astype(jnp.int32) & 0xFFFF)
+
+
+def low_of(pair):
+    return ((pair << 16) >> 16).astype(F32)
+
+
+def high_of(pair):
+    return (pair >> 16).astype(F32)
+
+
+def pack_inverse_kernel(h_ref, o_ref, w_ref, f_ref):
+    h = h_ref[...]
+    largest = jnp.max(jnp.abs(h), axis=1, keepdims=True)
+    code = jnp.floor(largest * 2.0**30) + 1.0
+    upper = jnp.floor(code * 2.0**-15)
+    lower = code - upper * 2.0**15
+    w_ref[...] = jnp.zeros_like(w_ref)
+    w_ref[0:Q, 0:Q] = jnp.round(h * (LEVELS / (code * 2.0**-30)))
+    w_ref[0:Q, Q : Q + 1] = upper
+    w_ref[0:Q, Q + 1 : Q + 2] = lower
+    turned = w_ref[...].T
+    w_ref[...] = turned
+    f_ref[...] = jnp.zeros_like(f_ref)
+    for r in range(Q):
+        line, lane = divmod(r * QP, 128)
+        first = min(Q, 128 - lane)
+        f_ref[line, lane : lane + first] = w_ref[r, 0:first]
+        if first < Q:
+            f_ref[line + 1, 0 : Q - first] = w_ref[r, first:Q]
+    f_ref[56, 0:Q] = w_ref[Q, 0:Q]
+    f_ref[57, 0:Q] = w_ref[Q + 1, 0:Q]
+    o_ref[...] = jnp.broadcast_to(pair_up(f_ref[0:32, :], f_ref[32:64, :])[None], o_ref.shape)
+
+
+def pack_inverse(matrix, targets):
     return pl.pallas_call(
         pack_inverse_kernel,
-        out_shape=jax.ShapeDtypeStruct((4, 56, 128), F32),
+        out_shape=jax.ShapeDtypeStruct((targets, 32, 128), jnp.int32),
         in_specs=[vmem_spec()],
         out_specs=vmem_spec(),
-        scratch_shapes=[pltpu.VMEM((4, Q, Q), F32)],
+        scratch_shapes=[pltpu.VMEM((128, 128), F32), pltpu.VMEM((64, 128), F32)],
         compiler_params=params(),
-    )(inverse)
+    )(matrix)
 
 
 def pack_points_kernel(step_ref, adj_ref, c0_ref, c1_ref, c2_ref, o_ref, t_ref):
     stored = (c0_ref, c1_ref, c2_ref)
+    lane = lax.broadcasted_iota(jnp.int32, (64, 256), 1)
     for z in range(4):
         for g in range(3):
             t_ref[g, z, 3 * Q : 256, :] = jnp.zeros((256 - 3 * Q, 128), F32)
@@ -101,9 +146,19 @@
                 else:
                     block = stored[i][0, g - 1, z].astype(F32)
                 t_ref[g, z, i * Q : (i + 1) * Q, :] = block
-            turned = t_ref[g, z].T
-            for e in range(2):
-                o_ref[:, z * 2 + e, g * 256 : (g + 1) * 256] = turned[e * 64 : (e + 1) * 64, :]
+            block = t_ref[g, z]
+            largest = jnp.max(jnp.max(jnp.abs(block), axis=0, keepdims=True), axis=1, keepdims=True)
+            code = jnp.floor(largest * 2.0**27) + 1.0
+            turned = jnp.round(block * (LEVELS / (code * 2.0**-27))).T
+            pair = pair_up(turned[0:64, :], turned[64:128, :])
+            pair = jnp.where(lane == SCALE_LANE, code.astype(jnp.int32), pair)
+            if g == 0:
+                o_ref[:, z * 2, 0:256] = pair
+            elif g == 1:
+                o_ref[:, z * 2, 256:384] = pair[:, 0:128]
+                o_ref[:, z * 2 + 1, 0:128] = pair[:, 128:256]
+            else:
+                o_ref[:, z * 2 + 1, 128:384] = pair
 
 
 def pack_points(adjoint, checkpoints, checkpoint_step):
@@ -112,7 +167,7 @@
 
     return pl.pallas_call(
         pack_points_kernel,
-        out_shape=jax.ShapeDtypeStruct((64, 8, 768), F32),
+        out_shape=jax.ShapeDtypeStruct((64, 8, 384), jnp.int32),
         grid_spec=pltpu.PrefetchScalarGridSpec(
             num_scalar_prefetch=1,
             grid=(1,),
@@ -122,7 +177,7 @@
                 slot(1),
                 slot(2),
             ],
-            out_specs=pl.BlockSpec((64, 8, 768), lambda i, st: (0, 0, 0)),
+            out_specs=pl.BlockSpec((64, 8, 384), lambda i, st: (0, 0, 0)),
             scratch_shapes=[pltpu.VMEM((3, 4, 256, 128), F32)],
         ),
         compiler_params=params(),
@@ -130,29 +185,50 @@
 
 
 def steps_kernel(
-    place_ref, metric_ref, r_ref, own_ref, other_ref, fwd_ref, back_ref, both_ref,
-    adj_ref, wall_ref,
-    ht, x, v, coef, solved, wall, turn,
+    place_ref, metric_ref, r_ref, own_ref, left_ref, left2_ref, right_ref, right2_ref,
+    oa_ref, oa2_ref, ob_ref, ob2_ref, fwd_ref, back_ref, both_ref,
+    out_ref,
+    ht, rows, x, v, coef, solved, wall, turn,
 ):
     chip = place_ref[0]
-    core = place_ref[1]
+    lanes = (
+        (own_ref, left_ref, left2_ref),
+        (right_ref, right2_ref, oa_ref, oa2_ref, ob_ref, ob2_ref),
+    )
 
     def turn_inverse(k, carry):
         row = pl.multiple_of(k * 128, 128)
-        ht[core, pl.ds(row, 128), :] = own_ref[:, k, :].T
-        ht[1 - core, pl.ds(row, 128), :] = other_ref[:, k, :].T
+        for half in range(2):
+            pair = jnp.concatenate([ref[:, k, :] for ref in lanes[half]], axis=0).T
+            ht[half, pl.ds(row, 128), :] = low_of(pair)
+            ht[half, pl.ds(row + 4096, 128), :] = high_of(pair)
         return carry
 
-    lax.fori_loop(0, 56, turn_inverse, 0)
+    lax.fori_loop(0, 32, turn_inverse, 0)
+    for half in range(2):
+        rows[half] = (
+            ht[half, 7168 : 7168 + QP, :] * 2.0**15 + ht[half, 7296 : 7296 + QP, :]
+        ) * (2.0**-30 / LEVELS)
 
     x[...] = jnp.zeros_like(x)
     v[...] = jnp.zeros_like(v)
-    for e in range(2):
-        for g in range(3):
-            stack = jnp.concatenate(
-                [r_ref[:, z * 2 + e, g * 256 : (g + 1) * 256] for z in range(4)], axis=0
-            )
-            turn[...] = stack.T
+    for g in range(3):
+        stack = []
+        for z in range(4):
+            if g == 0:
+                stack.append(r_ref[:, z * 2, 0:256])
+            elif g == 1:
+                stack.append(
+                    jnp.concatenate(
+                        [r_ref[:, z * 2, 256:384], r_ref[:, z * 2 + 1, 0:128]], axis=1
+                    )
+                )
+            else:
+                stack.append(r_ref[:, z * 2 + 1, 128:384])
+        pair = jnp.concatenate(stack, axis=0).T
+        unit = pair[SCALE_LANE : SCALE_LANE + 1, :].astype(F32) * (2.0**-27 / LEVELS)
+        for e in range(2):
+            turn[...] = (low_of(pair) if e == 0 else high_of(pair)) * unit
             for i in range(3):
                 part = turn[i * Q : (i + 1) * Q, :]
                 if g == 0:
@@ -189,7 +265,7 @@
                 zero = jnp.zeros((QP, 128), F32)
                 sums = lax.fori_loop(0, Q, column, (zero, zero, zero), unroll=3)
                 for c in range(3):
-                    solved[e * 3 + c, :, half * 128 : (half + 1) * 128] = sums[c]
+                    solved[e * 3 + c, :, half * 128 : (half + 1) * 128] = sums[c] * rows[half]
         planes = jnp.dot(
             solved[...].reshape(6 * QP, 256), back_ref[...], precision=HIGHEST, preferred_element_type=F32
         )
@@ -205,27 +281,24 @@
         wall[e, QP:128, :] = jnp.zeros((128 - QP, 256), F32)
         turned = wall[e].T
         for z in range(4):
-            wall_ref[:, z * 2 + e, :] = turned[z * 64 : (z + 1) * 64, :]
+            out_ref[:, z * 2 + e, 256:384] = turned[z * 64 : (z + 1) * 64, :]
         turn[3 * Q : 256, :] = jnp.zeros((256 - 3 * Q, 256), F32)
         for c in range(3):
             turn[c * Q : (c + 1) * Q, :] = x[e * 3 + c, 0:Q, :]
         turned = turn[...].T
         for z in range(4):
-            adj_ref[:, z * 2 + e, :] = turned[z * 64 : (z + 1) * 64, :]
-
-
-def steps(place, metric, points, own, other):
-    fwd, back, both = tables()
+            out_ref[:, z * 2 + e, 0:256] = turned[z * 64 : (z + 1) * 64, :]
+
+
+def steps(place, metric, points, inverse, fwd, back):
     return pl.pallas_call(
         steps_kernel,
-        out_shape=(
-            jax.ShapeDtypeStruct((64, 8, 256), F32),
-            jax.ShapeDtypeStruct((64, 8, 128), F32),
-        ),
-        in_specs=[smem_spec(), smem_spec()] + [vmem_spec()] * 6,
-        out_specs=(vmem_spec(), vmem_spec()),
+        out_shape=jax.ShapeDtypeStruct((64, 8, 384), F32),
+        in_specs=[smem_spec(), smem_spec()] + [vmem_spec()] * (len(inverse) + 4),
+        out_specs=vmem_spec(),
         scratch_shapes=[
-            pltpu.VMEM((2, 56 * 128, 128), F32),
+            pltpu.VMEM((2, 64 * 128, 128), F32),
+            pltpu.VMEM((2, QP, 128), F32),
             pltpu.VMEM((6, QP, 256), F32),
             pltpu.VMEM((2, 2, 3, QP, 256), F32),
             pltpu.VMEM((2, 6 * QP, 128), F32),
@@ -234,7 +307,7 @@
             pltpu.VMEM((256, 256), F32),
         ],
         compiler_params=params(),
-    )(place, metric, points, own, other, jnp.asarray(fwd), jnp.asarray(back), jnp.asarray(both))
+    )(place, metric, points, *inverse, fwd, back, slope_table())
 
 
 def wall_kernel(r_ref, local_ref, element_ref, o_ref):
@@ -261,8 +334,13 @@
     return pl.pallas_call(
         wall_kernel,
         out_shape=jax.ShapeDtypeStruct((4, local.shape[1] // 2), F32),
-        in_specs=[vmem_spec()] * 3,
-        out_specs=vmem_spec(),
+        grid=(1,),
+        in_specs=[
+            pl.BlockSpec((64, 8, 128), lambda i: (0, 0, 2)),
+            pl.BlockSpec(local.shape, lambda i: (0, 0)),
+            pl.BlockSpec(element.shape, lambda i: (0, 0)),
+        ],
+        out_specs=pl.BlockSpec((4, local.shape[1] // 2), lambda i: (0, 0)),
         compiler_params=params(),
     )(received, local, element)
 
@@ -279,8 +357,9 @@
     return pl.pallas_call(
         unpack_kernel,
         out_shape=jax.ShapeDtypeStruct((3, 4, Q, 128), F32),
-        in_specs=[vmem_spec()],
-        out_specs=vmem_spec(),
+        grid=(1,),
+        in_specs=[pl.BlockSpec((64, 8, 256), lambda i: (0, 0, 0))],
+        out_specs=pl.BlockSpec((3, 4, Q, 128), lambda i: (0, 0, 0, 0)),
         scratch_shapes=[pltpu.VMEM((4, 256, 128), F32)],
         compiler_params=params(),
     )(received)
@@ -301,23 +380,37 @@
     span_count = lax.axis_size("span")
     plane_count = lax.axis_size("plane")
     wall_count = wall_element.shape[0]
-    place = jnp.stack([span, span % 2]).astype(jnp.int32)
-
-    packed = pack_inverse(helmholtz_inverse)
-    same_core = [list(range(core, span_count, 2)) for core in range(2)]
-    own = lax.all_gather(packed, "span", axis=0, tiled=True, axis_index_groups=same_core)
-    other = lax.ppermute(own, "span", [(i, i ^ 1) for i in range(span_count)])
-
+    core = span % 2
+    place = jnp.stack([span, core]).astype(jnp.int32)
+    fwd, back = transforms(core, plane)
+
+    def around(block, step):
+        return lax.ppermute(
+            block, "plane", [(i, (i + step) % plane_count) for i in range(plane_count)]
+        )
+
+    def across(block):
+        return lax.ppermute(block, "span", [(i, i ^ 1) for i in range(span_count)])
+
+    matrix = lax.dynamic_index_in_dim(helmholtz_inverse, plane, 0, keepdims=False)
+    every = lax.all_to_all(pack_inverse(matrix, span_count), "span", 0, 0, tiled=True)
     sent = pack_points(adjoint, checkpoints, checkpoint_step)
+    every, sent = lax.optimization_barrier((every, sent))
+    mine = lax.dynamic_index_in_dim(
+        every.reshape(span_count // 2, 2, 32, 128), core, 1, keepdims=False
+    )
+    left = around(mine, 1)
+    right = around(mine, 3)
+    oa = around(left[:16], 1)
+    ob = around(right[16:], 3)
+    inverse = (every, left, across(left), right, across(right), oa, across(oa), ob, across(ob))
     points = lax.all_to_all(sent, "span", 0, 0, tiled=True)
-    adj_out, wall_out = steps(place, metric, points, own, other)
-
-    wall_in = lax.all_to_all(wall_out, "span", 0, 0, tiled=True)
-    adj_in = lax.all_to_all(adj_out, "span", 0, 0, tiled=True)
+    out = steps(place, metric, points, inverse, fwd, back)
+    received = lax.all_to_all(out, "span", 0, 0, tiled=True)
 
     local = wall_local.T.reshape(1, 2 * wall_count)
     element = wall_element.T.reshape(1, 2 * wall_count) - plane * adjoint.shape[3]
-    partial_sum = wall_sums(wall_in, local, element)
+    partial_sum = wall_sums(received, local, element)
     gradient = partial_sum
     for k in range(1, plane_count):
         gradient = gradient + lax.ppermute(
@@ -332,7 +425,7 @@
     share_width = wall_count // plane_count
     share = lax.dynamic_slice_in_dim(weighted, plane * share_width, share_width, 1)
     inverse_rms = lax.rsqrt(total / (adjoint.shape[1] * span_count * wall_count) + 1e-06)
-    return (unpack(adj_in), share * inverse_rms)
+    return (unpack(received), share * inverse_rms)
 
 
 def solution(mesh):

time: 267 us -> 179 us (0.67)
  waiting for transfers between devices: 151 us -> 67.4 us
  starting transfers between devices: 24.4 us -> 50.7 us
  blocking collectives: 15.6 us -> 0 us
  between operations: 14.8 us -> 1.62 us
    all_gather x1 -> x0, waiting for transfers between devices: 81.7 us -> none  [on_device(): lax.all_gather(packed, 'span', axis=0, tiled=True, axis_index_groups=same...]
    all_to_all x1, waiting for transfers between devices: 38.3 us -> 0.01 us  [on_device(): points = lax.all_to_all(sent, 'span', 0, 0, tiled=True)]
    all_to_all x2 -> x3, waiting for transfers between devices: 27.8 us -> 49 us  [the longest x1 22.2 us: on_device(): lax.all_to_all(pack_inverse(matrix, span_count), 'span', 0, 0, tiled=True)]
    all_to_all x2 -> x3, starting transfers between devices: 11.2 us -> 31.4 us  [the longest x1 13.3 us: on_device(): lax.all_to_all(pack_inverse(matrix, span_count), 'span', 0, 0, tiled=True)]
    all_to_all x1 -> x0, blocking collectives: 15.6 us -> none  [on_device(): lax.all_to_all(jnp.broadcast_to(square, (span_count, 1, 128)), 'span', 0,...]
    ppermute x1 -> x8, waiting for transfers between devices: 0.01 us -> 14.6 us  [the longest x4 14.6 us: around(): lax.ppermute(block, 'plane', [(i, (i + step) % plane_count) for i in rang...]
    ppermute x1 -> x8, starting transfers between devices: 3.93 us -> 9.91 us  [the longest x4 5.56 us: around(): lax.ppermute(block, 'plane', [(i, (i + step) % plane_count) for i in rang...]
    unnamed x20 -> x42, local copies, waits for them, and re-layouts: 10.9 us -> 8.86 us
  transfers between devices with their start and end apart: 8 -> 15, of which waited for: 6 -> 7; matrix products, arithmetic and copies ran while one was open for 2% -> 5% of each run, Pallas kernels for 1% -> 3%
where the time goes in v1:
time: 179 us
  waiting for transfers between devices  67.4 us (38%)
  starting transfers between devices  50.7 us (28%)
  Pallas kernels  43.2 us (24%)
  local copies, waits for them, and re-layouts  11.1 us (6%)
  other arithmetic  3.28 us (2%)
    pallas_call x1, Pallas kernels, steps(): pl.pallas_call(steps_kernel, out_shape=jax.ShapeDtypeStruct((64, 8, 384),...  31.4 us
    all_to_all x1, waiting for transfers between devices, on_device(): lax.all_to_all(pack_inverse(matrix, span_count), 'span', 0, 0, tiled=True)  22.2 us
    all_to_all x1, waiting for transfers between devices, on_device(): received = lax.all_to_all(out, 'span', 0, 0, tiled=True)  21.5 us
    ppermute x4, waiting for transfers between devices, around(): lax.ppermute(block, 'plane', [(i, (i + step) % plane_count) for i in rang...  14.6 us
    all_to_all x1, starting transfers between devices, on_device(): lax.all_to_all(pack_inverse(matrix, span_count), 'span', 0, 0, tiled=True)  13.3 us
    all_to_all x1, starting transfers between devices, on_device(): received = lax.all_to_all(out, 'span', 0, 0, tiled=True)  10.4 us
    unnamed x42, local copies, waits for them, and re-layouts  8.86 us
    all_to_all x1, starting transfers between devices, on_device(): lax.all_to_all(jnp.broadcast_to(square, (span_count, 1, 128)), 'span', 0,...  7.65 us
  transfers between devices with their start and end apart: 15, of which 7 were waited for; matrix products, arithmetic and copies ran while one was open for 5% of the time, Pallas kernels for 3%

profile of v1, /device:TPU:1, one launch (start us, length us, event | category | flops | bytes accessed | tf_op | source)
XLA Modules:
  0.0 178.6 jit_solution(5716596549902965384)
XLA Ops:
  0.6 0.0 copy-start
  0.6 0.9 copy-done
  1.6 0.6 copy.54
  2.2 2.3 %shard_map.149 = s32[64,32,128]{2,1,0:T(8,128)} custom-call(f32[81,81]{1,0:T(8,128)} %bitcast.23), custom_call_target="tpu_custom_call" | custom-call | tf_op jit(solution)/shard_map/pallas_call | solution.py:127
  4.6 13.3 %all-to-all-start = ((s32[64,32,128]{2,1,0:T(8,128)}), s32[64,32,128]{2,1,0:T(8,128)S(1)}, u32[]{:S(2)}, u32[]{:S(2)}) async-start(s32[64,32,128]{2,1,0:T(8,128)} %shard_map.149), calls=%async_computation | async-start | bytes 2097152 | tf_op jit(solution)/shard_map/all_to_all | solution.py:396
  17.9 0.8 copy.40.adj_ref
  18.7 1.4 copy.41.c0_ref.c1_ref.c2_ref
  20.1 3.6 %shard_map.150 = s32[64,8,384]{2,1,0:T(8,128)} custom-call(s32[3]{0:T(128)} %step_ref.1, f32[3,4,81,128]{3,2,1,0:T(8,128)} %copy.40.adj_ref, bf16[8,2,4,81,128]{4,3,2,1,0:T(8,128)(2,1)} %copy.41.c0_ref.c1_ref.c2_ref, bf16[8,2,4,81,128]{4,3,2,1,0:T(8,128)(2,1)} %copy.41.c0_ref.c1_ref.c2_ref, bf16[8,2,4,81,128]{4,3,2,1,0:T(8,128)(2,1)} %copy.41.c0_ref.c1_ref.c2_ref), custom_call_target="tpu_custom_call" | custom-call | tf_op jit(solution)/shard_map/pallas_call | solution.py:168
  23.6 22.2 %all-to-all-done.own_ref = s32[64,32,128]{2,1,0:T(8,128)S(1)} async-done(((s32[64,32,128]{2,1,0:T(8,128)}), s32[64,32,128]{2,1,0:T(8,128)S(1)}, u32[]{:S(2)}, u32[]{:S(2)}) %all-to-all-start) | async-done | bytes 1048608 | tf_op jit(solution)/shard_map/all_to_all | solution.py:396
  45.9 6.5 %all-to-all-start.1 = ((s32[64,8,384]{2,1,0:T(8,128)}), s32[64,8,384]{2,1,0:T(8,128)S(1)}, u32[]{:S(2)}, u32[]{:S(2)}) async-start(s32[64,8,384]{2,1,0:T(8,128)} %shard_map.150), calls=%async_computation.1 | async-start | bytes 1572864 | tf_op jit(solution)/shard_map/all_to_all | solution.py:407
  52.3 0.0 copy-start.15
  52.3 0.0 copy-start.16
  52.4 0.0 copy-start.17
  52.4 1.3 collective-permute-start
  53.7 1.5 collective-permute-start.2
  55.2 11.6 %collective-permute-done.left_ref = s32[32,32,128]{2,1,0:T(8,128)S(1)} collective-permute-done((s32[32,32,128]{2,1,0:T(8,128)S(1)}, s32[32,32,128]{2,1,0:T(8,128)S(1)}, u32[]{:S(2)}, u32[]{:S(2)}) %collective-permute-start) | collective-permute-done | bytes 524320 | tf_op jit(solution)/shard_map/ppermute | solution.py:388
  66.8 0.1 collective-permute-start.4
  66.9 0.0 collective-permute-done.2.right_ref
  66.9 2.7 %collective-permute-start.6 = (s32[16,32,128]{2,1,0:T(8,128)S(1)}, s32[16,32,128]{2,1,0:T(8,128)S(1)}, u32[]{:S(2)}, u32[]{:S(2)}) collective-permute-start(s32[16,32,128]{2,1,0:T(8,128)S(1)} %slice.13), channel_id=1, source_target_pairs={{0,3},{1,0},{2,1},{3,2},{4,7},{5,4},{6,5},{7,6},{8,11},{9,8},{10,9... | collective-permute-start | bytes 786440 | tf_op jit(solution)/shard_map/ppermute | solution.py:388
  69.7 1.9 %collective-permute-start.1 = (s32[32,32,128]{2,1,0:T(8,128)S(1)}, s32[32,32,128]{2,1,0:T(8,128)S(1)}, u32[]{:S(2)}, u32[]{:S(2)}) collective-permute-start(s32[32,32,128]{2,1,0:T(8,128)S(1)} %collective-permute-done.left_ref), channel_id=1, source_target_pairs={{0,4},{4,0},{8,12},{12,8},{16,20},{20,16},{24,28},{28,24},{32,36},... | collective-permute-start | bytes 1572872 | tf_op jit(solution)/shard_map/ppermute | solution.py:393
  71.5 0.0 collective-permute-start.3
  71.5 0.0 copy-done.17
  71.6 3.0 %collective-permute-done.4.oa_ref = s32[16,32,128]{2,1,0:T(8,128)S(1)} collective-permute-done((s32[16,32,128]{2,1,0:T(8,128)S(1)}, s32[16,32,128]{2,1,0:T(8,128)S(1)}, u32[]{:S(2)}, u32[]{:S(2)}) %collective-permute-start.4) | collective-permute-done | bytes 262176 | tf_op jit(solution)/shard_map/ppermute | solution.py:388
  74.6 2.2 %collective-permute-start.5 = (s32[16,32,128]{2,1,0:T(8,128)S(1)}, s32[16,32,128]{2,1,0:T(8,128)}, u32[]{:S(2)}, u32[]{:S(2)}) collective-permute-start(s32[16,32,128]{2,1,0:T(8,128)S(1)} %collective-permute-done.4.oa_ref), channel_id=1, source_target_pairs={{0,4},{4,0},{8,12},{12,8},{16,20},{20,16},{24,28},{28,24},{32,36},... | collective-permute-start | bytes 786440 | tf_op jit(solution)/shard_map/ppermute | solution.py:393
  76.8 0.0 collective-permute-done.6.ob_ref
  76.8 0.3 collective-permute-start.7
  77.1 1.4 fusion.back_ref
  78.5 0.8 copy.45
  79.3 0.7 pad_add_fusion.place_ref
  80.0 0.0 collective-permute-done.5.oa2_ref
  80.0 0.0 collective-permute-done.7.ob2_ref
  80.0 0.0 collective-permute-done.1.left2_ref
  80.0 0.0 collective-permute-done.3.right2_ref
  80.0 0.0 all-to-all-done.1.r_ref
  80.0 0.0 copy-start.3
  80.0 0.0 copy-done.6
  80.0 0.0 copy-done.7
  80.0 0.0 copy-done.10
  80.0 0.0 copy-done.11
  80.1 0.0 copy-done.4
  80.1 0.7 copy-done.8
  80.8 0.3 copy-done.3
  81.1 31.4 %shard_map.151 = f32[64,8,384]{2,1,0:T(8,128)} custom-call(s32[2]{0:T(128)} %pad_add_fusion.place_ref, f32[2,128]{1,0:T(2,128)} %metric_ref.1, s32[64,8,384]{2,1,0:T(8,128)} %copy-done.3, s32[64,32,128]{2,1,0:T(8,128)} %copy-done.2, s32[32,32,128]{2,1,0:T(8,128)} %copy-done.6, s32[32,32,128]{2,1,0:T(8,128)} %copy-done.8, s32[32,32,128]{2,1,0:T(8,128)} %copy-done.7, ...), custom_call_target="tpu_custom_call" | custom-call | tf_op jit(solution)/shard_map/pallas_call | solution.py:294
  112.5 0.0 copy-start.12
  112.5 10.4 %all-to-all-start.2 = ((f32[64,8,384]{2,1,0:T(8,128)}), f32[64,8,384]{2,1,0:T(8,128)S(1)}, u32[]{:S(2)}, u32[]{:S(2)}) async-start(f32[64,8,384]{2,1,0:T(8,128)} %shard_map.151), calls=%async_computation.2 | async-start | bytes 1572864 | tf_op jit(solution)/shard_map/all_to_all | solution.py:409
  123.0 0.6 copy.51
  123.6 0.6 copy.52
  124.2 21.5 %all-to-all-done.2.r_ref = f32[64,8,384]{2,1,0:T(8,128)S(1)} async-done(((f32[64,8,384]{2,1,0:T(8,128)}), f32[64,8,384]{2,1,0:T(8,128)S(1)}, u32[]{:S(2)}, u32[]{:S(2)}) %all-to-all-start.2) | async-done | bytes 786464 | tf_op jit(solution)/shard_map/all_to_all | solution.py:409
  145.7 0.9 copy-done.1
  146.6 3.7 %shard_map.153 = f32[4,1024]{1,0:T(4,128)} custom-call(f32[64,8,384]{2,1,0:T(8,128)} %copy-done.1, s32[1,2048]{1,0:T(1,128)} %bitcast.24, s32[1,2048]{1,0:T(1,128)} %bitcast.25), custom_call_target="tpu_custom_call" | custom-call | tf_op jit(solution)/shard_map/pallas_call | solution.py:334
  150.3 2.4 %collective-permute-start.10 = (f32[4,1024]{1,0:T(4,128)}, f32[4,1024]{1,0:T(4,128)S(1)}, u32[]{:S(2)}, u32[]{:S(2)}) collective-permute-start(f32[4,1024]{1,0:T(4,128)} %shard_map.153), channel_id=1, source_target_pairs={{0,3},{1,0},{2,1},{3,2},{4,7},{5,4},{6,5},{7,6},{8,11},{9,8},{10,9... | collective-permute-start | bytes 49160 | tf_op jit(solution)/shard_map/ppermute | solution.py:416
  152.7 0.0 collective-permute-start.9
  152.7 0.6 collective-permute-start.8
  153.3 0.5 collective-permute-done.10
  153.8 3.2 %collective-permute-done.9 = f32[4,1024]{1,0:T(4,128)S(1)} collective-permute-done((f32[4,1024]{1,0:T(4,128)}, f32[4,1024]{1,0:T(4,128)S(1)}, u32[]{:S(2)}, u32[]{:S(2)}) %collective-permute-start.9) | collective-permute-done | bytes 16416 | tf_op jit(solution)/shard_map/ppermute | solution.py:416
  157.0 0.0 collective-permute-done.8
  157.0 1.3 multiply_reduce_fusion
  158.3 1.3 broadcast_in_dim.15
  159.6 7.7 %all-to-all-start.3 = ((f32[64,1,128]{2,1,0:T(1,128)}), f32[64,1,128]{2,1,0:T(1,128)S(1)}, u32[]{:S(2)}, u32[]{:S(2)}) async-start(f32[64,1,128]{2,1,0:T(1,128)} %broadcast_in_dim.15), calls=%async_computation.3 | async-start | bytes 65536 | tf_op jit(solution)/shard_map/all_to_all | solution.py:421
  167.3 2.1 %shard_map.152 = f32[3,4,81,128]{3,2,1,0:T(8,128)} custom-call(f32[64,8,384]{2,1,0:T(8,128)} %copy-done.1), custom_call_target="tpu_custom_call" | custom-call | tf_op jit(solution)/shard_map/pallas_call | solution.py:357
  169.4 2.0 %copy.47 = f32[3,4,81,128]{3,1,2,0:T(4,128)} copy(f32[3,4,81,128]{3,2,1,0:T(8,128)} %shard_map.152) | data formatting | bytes 995328
  171.4 5.3 %all-to-all-done.3 = f32[64,1,128]{2,1,0:T(1,128)S(1)} async-done(((f32[64,1,128]{2,1,0:T(1,128)}), f32[64,1,128]{2,1,0:T(1,128)S(1)}, u32[]{:S(2)}, u32[]{:S(2)}) %all-to-all-start.3) | async-done | bytes 32800 | tf_op jit(solution)/shard_map/all_to_all | solution.py:421
  176.6 0.7 slice_reduce_fusion
  178.0 0.6 dynamic-slice_multiply_fusion
  (26 shorter events, 0.2 us)
Async XLA Ops:
  0.6 0.9 copy-start
  2.2 15.7 %copy-start.9 = (f32[3,4,81,128]{3,1,2,0:T(4,128)S(1)}, f32[3,4,81,128]{3,1,2,0:T(4,128)}, u32[]{:S(2)}) copy-start(f32[3,4,81,128]{3,1,2,0:T(4,128)} %param.14) | copy-start | bytes 1492996
  4.6 14.1 %copy-start.5 = (bf16[8,2,4,81,128]{4,2,3,1,0:T(4,128)(2,1)S(1)}, bf16[8,2,4,81,128]{4,2,3,1,0:T(4,128)(2,1)}, u32[]{:S(2)}) copy-start(bf16[8,2,4,81,128]{4,2,3,1,0:T(4,128)(2,1)} %param.15) | copy-start | bytes 3981316
  4.6 41.3 %all-to-all-start = ((s32[64,32,128]{2,1,0:T(8,128)}), s32[64,32,128]{2,1,0:T(8,128)S(1)}, u32[]{:S(2)}, u32[]{:S(2)}) async-start(s32[64,32,128]{2,1,0:T(8,128)} %shard_map.149), calls=%async_computation | async-start | bytes 2097152 | tf_op jit(solution)/shard_map/all_to_all | solution.py:396
  45.9 20.9 %copy-start.2 = (s32[64,32,128]{2,1,0:T(8,128)}, s32[64,32,128]{2,1,0:T(8,128)S(1)}, u32[]{:S(2)}) copy-start(s32[64,32,128]{2,1,0:T(8,128)S(1)} %all-to-all-done.own_ref) | copy-start | bytes 3145732
  45.9 34.1 %all-to-all-start.1 = ((s32[64,8,384]{2,1,0:T(8,128)}), s32[64,8,384]{2,1,0:T(8,128)S(1)}, u32[]{:S(2)}, u32[]{:S(2)}) async-start(s32[64,8,384]{2,1,0:T(8,128)} %shard_map.150), calls=%async_computation.1 | async-start | bytes 1572864 | tf_op jit(solution)/shard_map/all_to_all | solution.py:407
  52.3 19.2 %copy-start.15 = (s32[256]{0:T(256)S(1)}, s32[256]{0:T(256)}, u32[]{:S(2)}) copy-start(s32[256]{0:T(256)} %constant.79.clone) | copy-start | bytes 3076
  52.3 19.2 %copy-start.16 = (s32[256]{0:T(256)S(1)}, s32[256]{0:T(256)}, u32[]{:S(2)}) copy-start(s32[256]{0:T(256)} %constant.86) | copy-start | bytes 3076
  52.4 19.2 %copy-start.17 = (s32[256]{0:T(256)S(1)}, s32[256]{0:T(256)}, u32[]{:S(2)}) copy-start(s32[256]{0:T(256)} %constant.89) | copy-start | bytes 3076
  52.4 14.3 %collective-permute-start = (s32[32,32,128]{2,1,0:T(8,128)S(1)}, s32[32,32,128]{2,1,0:T(8,128)S(1)}, u32[]{:S(2)}, u32[]{:S(2)}) collective-permute-start(s32[32,32,128]{2,1,0:T(8,128)S(1)} %dynamic-slice_bitcast_fusion), channel_id=1, source_target_pairs={{0,1},{1,2},{2,3},{3,0},{4,5},{5,6},{6,7},{7,4},{8,9},{9,10},{10,1... | collective-permute-start | bytes 1572872 | tf_op jit(solution)/shard_map/ppermute | solution.py:388
  53.7 13.2 %collective-permute-start.2 = (s32[32,32,128]{2,1,0:T(8,128)S(1)}, s32[32,32,128]{2,1,0:T(8,128)S(1)}, u32[]{:S(2)}, u32[]{:S(2)}) collective-permute-start(s32[32,32,128]{2,1,0:T(8,128)S(1)} %dynamic-slice_bitcast_fusion), channel_id=1, source_target_pairs={{0,3},{1,0},{2,1},{3,2},{4,7},{5,4},{6,5},{7,6},{8,11},{9,8},{10,9... | collective-permute-start | bytes 1572872 | tf_op jit(solution)/shard_map/ppermute | solution.py:388
  66.8 13.3 %copy-start.6 = (s32[32,32,128]{2,1,0:T(8,128)}, s32[32,32,128]{2,1,0:T(8,128)S(1)}, u32[]{:S(2)}) copy-start(s32[32,32,128]{2,1,0:T(8,128)S(1)} %collective-permute-done.left_ref) | copy-start | bytes 1572868
  66.8 7.8 %collective-permute-start.4 = (s32[16,32,128]{2,1,0:T(8,128)S(1)}, s32[16,32,128]{2,1,0:T(8,128)S(1)}, u32[]{:S(2)}, u32[]{:S(2)}) collective-permute-start(s32[16,32,128]{2,1,0:T(8,128)S(1)} %slice.12), channel_id=1, source_target_pairs={{0,1},{1,2},{2,3},{3,0},{4,5},{5,6},{6,7},{7,4},{8,9},{9,10},{10,1... | collective-permute-start | bytes 786440 | tf_op jit(solution)/shard_map/ppermute | solution.py:388
  66.9 13.1 %copy-start.7 = (s32[32,32,128]{2,1,0:T(8,128)}, s32[32,32,128]{2,1,0:T(8,128)S(1)}, u32[]{:S(2)}) copy-start(s32[32,32,128]{2,1,0:T(8,128)S(1)} %collective-permute-done.2.right_ref) | copy-start | bytes 1572868
  66.9 9.9 %collective-permute-start.6 = (s32[16,32,128]{2,1,0:T(8,128)S(1)}, s32[16,32,128]{2,1,0:T(8,128)S(1)}, u32[]{:S(2)}, u32[]{:S(2)}) collective-permute-start(s32[16,32,128]{2,1,0:T(8,128)S(1)} %slice.13), channel_id=1, source_target_pairs={{0,3},{1,0},{2,1},{3,2},{4,7},{5,4},{6,5},{7,6},{8,11},{9,8},{10,9... | collective-permute-start | bytes 786440 | tf_op jit(solution)/shard_map/ppermute | solution.py:388
  69.7 10.3 %collective-permute-start.1 = (s32[32,32,128]{2,1,0:T(8,128)S(1)}, s32[32,32,128]{2,1,0:T(8,128)S(1)}, u32[]{:S(2)}, u32[]{:S(2)}) collective-permute-start(s32[32,32,128]{2,1,0:T(8,128)S(1)} %collective-permute-done.left_ref), channel_id=1, source_target_pairs={{0,4},{4,0},{8,12},{12,8},{16,20},{20,16},{24,28},{28,24},{32,36},... | collective-permute-start | bytes 1572872 | tf_op jit(solution)/shard_map/ppermute | solution.py:393
  71.5 8.5 %collective-permute-start.3 = (s32[32,32,128]{2,1,0:T(8,128)S(1)}, s32[32,32,128]{2,1,0:T(8,128)}, u32[]{:S(2)}, u32[]{:S(2)}) collective-permute-start(s32[32,32,128]{2,1,0:T(8,128)S(1)} %collective-permute-done.2.right_ref), channel_id=1, source_target_pairs={{0,4},{4,0},{8,12},{12,8},{16,20},{20,16},{24,28},{28,24},{32,36},... | collective-permute-start | bytes 1572872 | tf_op jit(solution)/shard_map/ppermute | solution.py:393
  74.6 5.5 %copy-start.10 = (s32[16,32,128]{2,1,0:T(8,128)}, s32[16,32,128]{2,1,0:T(8,128)S(1)}, u32[]{:S(2)}) copy-start(s32[16,32,128]{2,1,0:T(8,128)S(1)} %collective-permute-done.4.oa_ref) | copy-start | bytes 786436
  74.6 5.4 %collective-permute-start.5 = (s32[16,32,128]{2,1,0:T(8,128)S(1)}, s32[16,32,128]{2,1,0:T(8,128)}, u32[]{:S(2)}, u32[]{:S(2)}) collective-permute-start(s32[16,32,128]{2,1,0:T(8,128)S(1)} %collective-permute-done.4.oa_ref), channel_id=1, source_target_pairs={{0,4},{4,0},{8,12},{12,8},{16,20},{20,16},{24,28},{28,24},{32,36},... | collective-permute-start | bytes 786440 | tf_op jit(solution)/shard_map/ppermute | solution.py:393
  76.8 3.2 %copy-start.11 = (s32[16,32,128]{2,1,0:T(8,128)}, s32[16,32,128]{2,1,0:T(8,128)S(1)}, u32[]{:S(2)}) copy-start(s32[16,32,128]{2,1,0:T(8,128)S(1)} %collective-permute-done.6.ob_ref) | copy-start | bytes 786436
  76.8 3.2 %collective-permute-start.7 = (s32[16,32,128]{2,1,0:T(8,128)S(1)}, s32[16,32,128]{2,1,0:T(8,128)}, u32[]{:S(2)}, u32[]{:S(2)}) collective-permute-start(s32[16,32,128]{2,1,0:T(8,128)S(1)} %collective-permute-done.6.ob_ref), channel_id=1, source_target_pairs={{0,4},{4,0},{8,12},{12,8},{16,20},{20,16},{24,28},{28,24},{32,36},... | collective-permute-start | bytes 786440 | tf_op jit(solution)/shard_map/ppermute | solution.py:393
  78.5 1.6 copy-start.4
  80.0 0.8 copy-start.8
  80.0 1.1 copy-start.3
  112.5 10.4 %copy-start.13 = (s32[1024,2]{0,1:T(2,128)S(1)}, s32[1024,2]{0,1:T(2,128)}, u32[]{:S(2)}) copy-start(s32[1024,2]{0,1:T(2,128)} %param.20) | copy-start | bytes 24580
  112.5 11.1 %copy-start.14 = (s32[1024,2]{0,1:T(2,128)S(1)}, s32[1024,2]{0,1:T(2,128)}, u32[]{:S(2)}) copy-start(s32[1024,2]{0,1:T(2,128)} %param.19) | copy-start | bytes 24580
  112.5 44.5 %copy-start.12 = (f32[4,1024]{1,0:T(4,128)S(1)}, f32[4,1024]{1,0:T(4,128)}, u32[]{:S(2)}) copy-start(f32[4,1024]{1,0:T(4,128)} %param.21) | copy-start | bytes 49156
  112.5 33.2 %all-to-all-start.2 = ((f32[64,8,384]{2,1,0:T(8,128)}), f32[64,8,384]{2,1,0:T(8,128)S(1)}, u32[]{:S(2)}, u32[]{:S(2)}) async-start(f32[64,8,384]{2,1,0:T(8,128)} %shard_map.151), calls=%async_computation.2 | async-start | bytes 1572864 | tf_op jit(solution)/shard_map/all_to_all | solution.py:409
  145.7 0.9 copy-start.1
  150.3 3.5 %collective-permute-start.10 = (f32[4,1024]{1,0:T(4,128)}, f32[4,1024]{1,0:T(4,128)S(1)}, u32[]{:S(2)}, u32[]{:S(2)}) collective-permute-start(f32[4,1024]{1,0:T(4,128)} %shard_map.153), channel_id=1, source_target_pairs={{0,3},{1,0},{2,1},{3,2},{4,7},{5,4},{6,5},{7,6},{8,11},{9,8},{10,9... | collective-permute-start | bytes 49160 | tf_op jit(solution)/shard_map/ppermute | solution.py:416
  152.7 4.3 %collective-permute-start.9 = (f32[4,1024]{1,0:T(4,128)}, f32[4,1024]{1,0:T(4,128)S(1)}, u32[]{:S(2)}, u32[]{:S(2)}) collective-permute-start(f32[4,1024]{1,0:T(4,128)} %shard_map.153), channel_id=1, source_target_pairs={{0,2},{1,3},{2,0},{3,1},{4,6},{5,7},{6,4},{7,5},{8,10},{9,11},{10,... | collective-permute-start | bytes 49160 | tf_op jit(solution)/shard_map/ppermute | solution.py:416
  152.7 4.3 %collective-permute-start.8 = (f32[4,1024]{1,0:T(4,128)}, f32[4,1024]{1,0:T(4,128)S(1)}, u32[]{:S(2)}, u32[]{:S(2)}) collective-permute-start(f32[4,1024]{1,0:T(4,128)} %shard_map.153), channel_id=1, source_target_pairs={{0,1},{1,2},{2,3},{3,0},{4,5},{5,6},{6,7},{7,4},{8,9},{9,10},{10,1... | collective-permute-start | bytes 49160 | tf_op jit(solution)/shard_map/ppermute | solution.py:416
  159.6 17.0 %all-to-all-start.3 = ((f32[64,1,128]{2,1,0:T(1,128)}), f32[64,1,128]{2,1,0:T(1,128)S(1)}, u32[]{:S(2)}, u32[]{:S(2)}) async-start(f32[64,1,128]{2,1,0:T(1,128)} %broadcast_in_dim.15), calls=%async_computation.3 | async-start | bytes 65536 | tf_op jit(solution)/shard_map/all_to_all | solution.py:421

commit v2 on v1

--- a/solution.py
+++ b/solution.py
@@ -43,27 +43,38 @@
 
 def lane_order():
     chips = np.arange(32)
-    pieces = [(np.arange(64) // 2, np.arange(64) % 2, 0, 0)]
-    for part, shift in ((chips, 3), (chips, 1), (chips[:16], 2), (chips[16:], 2)):
+    pieces = []
+    for part, shift in ((chips, 0), (chips, 3), (chips, 1), (chips[:16], 2), (chips[16:], 2)):
         for core in range(2):
-            pieces.append((part, np.full(part.shape, core), 1, shift))
-    chip = np.concatenate([p[0] for p in pieces])
-    core = np.concatenate([p[1] for p in pieces])
-    relative = np.concatenate([np.full(p[0].shape, p[2]) for p in pieces])
-    shift = np.concatenate([np.full(p[0].shape, p[3]) for p in pieces])
-    return [v.astype(np.int32) for v in (chip, core, relative, shift)]
+            pieces.append((part, np.full(part.shape, core), np.full(part.shape, shift)))
+    return [np.concatenate([p[k] for p in pieces]).astype(np.int32) for k in range(3)]
+
+
+def in_two(array):
+    high = array.astype(jnp.bfloat16)
+    return high, (array - high.astype(F32)).astype(jnp.bfloat16)
+
+
+def split_table(table):
+    high = table.astype(jnp.bfloat16)
+    return high, (table - high.astype(np.float64)).astype(jnp.bfloat16)
 
 
 def transforms(core, plane):
     zl = np.arange(256)
     z_of = 4 * (zl % 64) + zl // 64
-    table = jnp.asarray(fourier_table(256).astype(np.float32)[:, z_of])
-    chip, lane_core, relative, shift = (jnp.asarray(v) for v in lane_order())
-    span_of = 2 * chip + lane_core + relative * core * (1 - 2 * lane_core)
+    high, low = split_table(fourier_table(256)[:, z_of])
+    chip, lane_core, shift = (jnp.asarray(v) for v in lane_order())
+    span_of = 2 * chip + lane_core + core * (1 - 2 * lane_core)
     order = 4 * span_of + (plane + shift) % 4
-    pick = jnp.where(order[:, None] == jnp.arange(256)[None, :], 1.0, 0.0).astype(F32)
-    back = jnp.dot(pick, table, precision=HIGHEST)
-    return back.T, back
+    pick = jnp.where(order[:, None] == jnp.arange(256)[None, :], 1.0, 0.0).astype(jnp.bfloat16)
+    both = jnp.asarray(np.concatenate([high, low], axis=1))
+    back = jnp.dot(pick, both, preferred_element_type=F32).astype(jnp.bfloat16)
+    high, low = back[:, :256], back[:, 256:]
+    return (
+        jnp.concatenate([high.T, high.T, low.T], axis=0),
+        jnp.concatenate([high, high, low], axis=0),
+    )
 
 
 def slope_table():
@@ -72,7 +83,7 @@
     both = np.zeros((2 * QP, QP), np.float32)
     both[:Q, :Q] = np.kron(d, eye)
     both[QP : QP + Q, :Q] = np.kron(eye, d)
-    return jnp.asarray(both)
+    return jnp.asarray(np.concatenate(split_table(both), axis=0))
 
 
 def vmem_spec():
@@ -89,6 +100,14 @@
 
 def pair_up(low, high):
     return (high.astype(jnp.int32) << 16) | (low.astype(jnp.int32) & 0xFFFF)
+
+
+def scale_code(largest):
+    return jnp.floor(jnp.log2(jnp.maximum(largest, 1e-30)) * 2.0**16) + 2.0
+
+
+def scale_of(code):
+    return jnp.exp2(code * 2.0**-16)
 
 
 def low_of(pair):
@@ -184,15 +203,22 @@
     )(checkpoint_step, adjoint, checkpoints, checkpoints, checkpoints)
 
 
+def transform(array, table_ref):
+    high, low = in_two(array)
+    return jnp.dot(
+        jnp.concatenate([high, low, high], axis=1), table_ref[...], preferred_element_type=F32
+    )
+
+
 def steps_kernel(
-    place_ref, metric_ref, r_ref, own_ref, left_ref, left2_ref, right_ref, right2_ref,
+    place_ref, metric_ref, r_ref, own_ref, own2_ref, left_ref, left2_ref, right_ref, right2_ref,
     oa_ref, oa2_ref, ob_ref, ob2_ref, fwd_ref, back_ref, both_ref,
     out_ref,
-    ht, rows, x, v, coef, solved, wall, turn,
+    ht, rows, x, v, coef, solved, wall, spread, turn,
 ):
     chip = place_ref[0]
     lanes = (
-        (own_ref, left_ref, left2_ref),
+        (own_ref, own2_ref, left_ref, left2_ref),
         (right_ref, right2_ref, oa_ref, oa2_ref, ob_ref, ob2_ref),
     )
 
@@ -228,9 +254,9 @@
         pair = jnp.concatenate(stack, axis=0).T
         unit = pair[SCALE_LANE : SCALE_LANE + 1, :].astype(F32) * (2.0**-27 / LEVELS)
         for e in range(2):
-            turn[...] = (low_of(pair) if e == 0 else high_of(pair)) * unit
+            spread[...] = (low_of(pair) if e == 0 else high_of(pair)) * unit
             for i in range(3):
-                part = turn[i * Q : (i + 1) * Q, :]
+                part = spread[i * Q : (i + 1) * Q, :]
                 if g == 0:
                     x[e * 3 + i, 0:Q, :] = part
                 else:
@@ -242,15 +268,16 @@
             m1 = metric_ref[1, chip + 64 * e]
             for c in range(3):
                 field = x[e * 3 + c]
-                slopes = jnp.dot(both_ref[...], field, precision=HIGHEST, preferred_element_type=F32)
+                high, low = in_two(field)
+                large = jnp.dot(both_ref[...], high, preferred_element_type=F32)
+                small = jnp.dot(both_ref[0 : 2 * QP, :], low, preferred_element_type=F32)
+                slopes = large[0 : 2 * QP] + (large[2 * QP : 4 * QP] + small)
                 x[e * 3 + c] = (
                     field
                     + v[0, e, step] * (m0 * slopes[0:QP])
                     + v[1, e, step] * (m1 * slopes[QP : 2 * QP])
                 )
-        modes = jnp.dot(
-            x[...].reshape(6 * QP, 256), fwd_ref[...], precision=HIGHEST, preferred_element_type=F32
-        )
+        modes = transform(x[...].reshape(6 * QP, 256), fwd_ref)
         coef[0] = modes[:, 0:128]
         coef[1] = modes[:, 128:256]
         for half in range(2):
@@ -263,37 +290,44 @@
                     )
 
                 zero = jnp.zeros((QP, 128), F32)
-                sums = lax.fori_loop(0, Q, column, (zero, zero, zero), unroll=3)
+                sums = lax.fori_loop(0, Q, column, (zero, zero, zero), unroll=27)
                 for c in range(3):
                     solved[e * 3 + c, :, half * 128 : (half + 1) * 128] = sums[c] * rows[half]
-        planes = jnp.dot(
-            solved[...].reshape(6 * QP, 256), back_ref[...], precision=HIGHEST, preferred_element_type=F32
-        )
+        planes = transform(solved[...].reshape(6 * QP, 256), back_ref)
         x[...] = planes.reshape(6, QP, 256)
         for e in range(2):
             product = x[e * 3 + 1] * v[1, e, step]
             if step == 0:
-                wall[e, 0:QP] = product
+                wall[e] = product
             else:
-                wall[e, 0:QP] = wall[e, 0:QP] + product
-
-    for e in range(2):
-        wall[e, QP:128, :] = jnp.zeros((128 - QP, 256), F32)
-        turned = wall[e].T
-        for z in range(4):
-            out_ref[:, z * 2 + e, 256:384] = turned[z * 64 : (z + 1) * 64, :]
-        turn[3 * Q : 256, :] = jnp.zeros((256 - 3 * Q, 256), F32)
-        for c in range(3):
-            turn[c * Q : (c + 1) * Q, :] = x[e * 3 + c, 0:Q, :]
-        turned = turn[...].T
-        for z in range(4):
-            out_ref[:, z * 2 + e, 0:256] = turned[z * 64 : (z + 1) * 64, :]
+                wall[e] = wall[e] + product
+
+    def levels(array):
+        largest = jnp.max(jnp.max(jnp.abs(array), axis=0), axis=0, keepdims=True)
+        code = scale_code(largest)
+        return code.astype(jnp.int32), LEVELS / scale_of(code)
+
+    code, unit = levels(wall[...])
+    turn[0:QP, :] = pair_up(jnp.round(wall[0] * unit), jnp.round(wall[1] * unit))
+    turn[QP:128, :] = jnp.broadcast_to(code, (128 - QP, 256))
+    turned = turn[0:128, :].T
+    for z in range(4):
+        out_ref[:, z, 256:384] = turned[z * 64 : (z + 1) * 64, :]
+    code, unit = levels(x[...])
+    for c in range(3):
+        turn[c * Q : (c + 1) * Q, :] = pair_up(
+            jnp.round(x[c, 0:Q, :] * unit), jnp.round(x[c + 3, 0:Q, :] * unit)
+        )
+    turn[3 * Q : 256, :] = jnp.broadcast_to(code, (256 - 3 * Q, 256))
+    turned = turn[...].T
+    for z in range(4):
+        out_ref[:, z, 0:256] = turned[z * 64 : (z + 1) * 64, :]
 
 
 def steps(place, metric, points, inverse, fwd, back):
     return pl.pallas_call(
         steps_kernel,
-        out_shape=jax.ShapeDtypeStruct((64, 8, 384), F32),
+        out_shape=jax.ShapeDtypeStruct((64, 4, 384), jnp.int32),
         in_specs=[smem_spec(), smem_spec()] + [vmem_spec()] * (len(inverse) + 4),
         out_specs=vmem_spec(),
         scratch_shapes=[
@@ -303,8 +337,9 @@
             pltpu.VMEM((2, 2, 3, QP, 256), F32),
             pltpu.VMEM((2, 6 * QP, 128), F32),
             pltpu.VMEM((6, QP, 256), F32),
-            pltpu.VMEM((2, 128, 256), F32),
+            pltpu.VMEM((2, QP, 256), F32),
             pltpu.VMEM((256, 256), F32),
+            pltpu.VMEM((256, 256), jnp.int32),
         ],
         compiler_params=params(),
     )(place, metric, points, *inverse, fwd, back, slope_table())
@@ -316,15 +351,12 @@
     pick = jnp.where(mode == local_ref[...], 1.0, 0.0).astype(jnp.bfloat16)
     here = mode == element_ref[...]
     for z in range(4):
-        field = jnp.concatenate([r_ref[:, z * 2, :], r_ref[:, z * 2 + 1, :]], axis=0)
-        high = field.astype(jnp.bfloat16)
-        rest = field - high.astype(F32)
-        middle = rest.astype(jnp.bfloat16)
-        low = (rest - middle.astype(F32)).astype(jnp.bfloat16)
-        values = (
-            jnp.dot(low, pick, preferred_element_type=F32)
-            + jnp.dot(middle, pick, preferred_element_type=F32)
-            + jnp.dot(high, pick, preferred_element_type=F32)
+        pair = r_ref[:, z, :]
+        unit = scale_of(pair[:, QP : QP + 1].astype(F32)) * (1.0 / LEVELS)
+        field = jnp.concatenate([low_of(pair) * unit, high_of(pair) * unit], axis=0)
+        high, low = in_two(field)
+        values = jnp.dot(low, pick, preferred_element_type=F32) + jnp.dot(
+            high, pick, preferred_element_type=F32
         )
         total = jnp.sum(jnp.where(here, values, 0.0), axis=0, keepdims=True)
         o_ref[z : z + 1, :] = total[:, 0 : points // 2] + total[:, points // 2 :]
@@ -336,7 +368,7 @@
         out_shape=jax.ShapeDtypeStruct((4, local.shape[1] // 2), F32),
         grid=(1,),
         in_specs=[
-            pl.BlockSpec((64, 8, 128), lambda i: (0, 0, 2)),
+            pl.BlockSpec((64, 4, 128), lambda i: (0, 0, 2)),
             pl.BlockSpec(local.shape, lambda i: (0, 0)),
             pl.BlockSpec(element.shape, lambda i: (0, 0)),
         ],
@@ -345,10 +377,31 @@
     )(received, local, element)
 
 
+def weigh_kernel(weight_ref, p0_ref, p1_ref, p2_ref, p3_ref, weighted_ref, square_ref):
+    weighted = weight_ref[...] * ((p0_ref[...] + p1_ref[...]) + (p2_ref[...] + p3_ref[...]))
+    weighted_ref[...] = weighted
+    square = jnp.sum(jnp.sum(weighted * weighted, axis=0, keepdims=True), axis=1, keepdims=True)
+    square_ref[...] = jnp.broadcast_to(square.reshape(1, 1, 1), square_ref.shape)
+
+
+def weigh(weight, parts, targets):
+    return pl.pallas_call(
+        weigh_kernel,
+        out_shape=(
+            jax.ShapeDtypeStruct(weight.shape, F32),
+            jax.ShapeDtypeStruct((targets, 1, 128), F32),
+        ),
+        in_specs=[vmem_spec()] * 5,
+        out_specs=(vmem_spec(), vmem_spec()),
+        compiler_params=params(),
+    )(weight, *parts)
+
+
 def unpack_kernel(r_ref, o_ref, t_ref):
     for z in range(4):
-        stack = jnp.concatenate([r_ref[:, z * 2, :], r_ref[:, z * 2 + 1, :]], axis=0)
-        t_ref[z] = stack.T
+        pair = r_ref[:, z, :].T
+        unit = scale_of(pair[SCALE_LANE : SCALE_LANE + 1, :].astype(F32)) * (1.0 / LEVELS)
+        t_ref[z] = jnp.concatenate([low_of(pair) * unit, high_of(pair) * unit], axis=1)
         for c in range(3):
             o_ref[c, z] = t_ref[z, c * Q : (c + 1) * Q, :]
 
@@ -358,7 +411,7 @@
         unpack_kernel,
         out_shape=jax.ShapeDtypeStruct((3, 4, Q, 128), F32),
         grid=(1,),
-        in_specs=[pl.BlockSpec((64, 8, 256), lambda i: (0, 0, 0))],
+        in_specs=[pl.BlockSpec((64, 4, 256), lambda i: (0, 0, 0))],
         out_specs=pl.BlockSpec((3, 4, Q, 128), lambda i: (0, 0, 0, 0)),
         scratch_shapes=[pltpu.VMEM((4, 256, 128), F32)],
         compiler_params=params(),
@@ -393,34 +446,29 @@
         return lax.ppermute(block, "span", [(i, i ^ 1) for i in range(span_count)])
 
     matrix = lax.dynamic_index_in_dim(helmholtz_inverse, plane, 0, keepdims=False)
-    every = lax.all_to_all(pack_inverse(matrix, span_count), "span", 0, 0, tiled=True)
+    same_core = [list(range(c, span_count, 2)) for c in range(2)]
+    own = lax.all_to_all(
+        pack_inverse(matrix, span_count // 2), "span", 0, 0, tiled=True, axis_index_groups=same_core
+    )
+    local = wall_local.T.reshape(1, 2 * wall_count)
+    element = wall_element.T.reshape(1, 2 * wall_count) - plane * adjoint.shape[3]
     sent = pack_points(adjoint, checkpoints, checkpoint_step)
-    every, sent = lax.optimization_barrier((every, sent))
-    mine = lax.dynamic_index_in_dim(
-        every.reshape(span_count // 2, 2, 32, 128), core, 1, keepdims=False
-    )
-    left = around(mine, 1)
-    right = around(mine, 3)
+    own, sent, local, element = lax.optimization_barrier((own, sent, local, element))
+    left = around(own, 1)
+    right = around(own, 3)
     oa = around(left[:16], 1)
     ob = around(right[16:], 3)
-    inverse = (every, left, across(left), right, across(right), oa, across(oa), ob, across(ob))
+    inverse = []
+    for piece in (own, left, right, oa, ob):
+        inverse += [piece, across(piece)]
     points = lax.all_to_all(sent, "span", 0, 0, tiled=True)
     out = steps(place, metric, points, inverse, fwd, back)
     received = lax.all_to_all(out, "span", 0, 0, tiled=True)
 
-    local = wall_local.T.reshape(1, 2 * wall_count)
-    element = wall_element.T.reshape(1, 2 * wall_count) - plane * adjoint.shape[3]
     partial_sum = wall_sums(received, local, element)
-    gradient = partial_sum
-    for k in range(1, plane_count):
-        gradient = gradient + lax.ppermute(
-            partial_sum, "plane", [(i, (i + k) % plane_count) for i in range(plane_count)]
-        )
-    weighted = wall_weight * gradient
-    square = jnp.sum(weighted * weighted)
-    squares = lax.all_to_all(
-        jnp.broadcast_to(square, (span_count, 1, 128)), "span", 0, 0, tiled=True
-    )
+    parts = [partial_sum] + [around(partial_sum, k) for k in range(1, plane_count)]
+    weighted, square = weigh(wall_weight, parts, span_count)
+    squares = lax.all_to_all(square, "span", 0, 0, tiled=True)
     total = jnp.sum(squares[:, 0, 0])
     share_width = wall_count // plane_count
     share = lax.dynamic_slice_in_dim(weighted, plane * share_width, share_width, 1)

time: 179 us -> 150 us (0.84)
  waiting for transfers between devices: 67.4 us -> 32.2 us
  blocking collectives: 0 us -> 25.3 us
  starting transfers between devices: 50.7 us -> 40.5 us
  Pallas kernels: 43.2 us -> 37 us
    all_to_all x3 -> x2, waiting for transfers between devices: 49 us -> 14.5 us  [the longest x1 9.25 us: on_device(): lax.all_to_all(pack_inverse(matrix, span_count // 2), 'span', 0, 0, tiled...]
    all_to_all x0 -> x1, blocking collectives: none -> 25.3 us  [on_device(): received = lax.all_to_all(out, 'span', 0, 0, tiled=True)]
    all_to_all x3 -> x2, starting transfers between devices: 31.4 us -> 18.8 us  [the longest x1 12 us: on_device(): lax.all_to_all(pack_inverse(matrix, span_count // 2), 'span', 0, 0, tiled...]
    pallas_call x1 -> x2, Pallas kernels: 31.4 us -> 25.9 us  [the longest x1 24.3 us: steps(): pl.pallas_call(steps_kernel, out_shape=jax.ShapeDtypeStruct((64, 4, 384),...]
    ppermute x3 -> x0, waiting for transfers between devices: 3.73 us -> none  [on_device(): lax.ppermute(partial_sum, 'plane', [(i, (i + k) % plane_count) for i in r...]
    ppermute x4 -> x7, waiting for transfers between devices: 14.6 us -> 17.7 us  [around(): lax.ppermute(block, 'plane', [(i, (i + step) % plane_count) for i in rang...]
    ppermute x3 -> x0, starting transfers between devices: 2.97 us -> none  [on_device(): lax.ppermute(partial_sum, 'plane', [(i, (i + k) % plane_count) for i in r...]
    ppermute x4 -> x5, starting transfers between devices: 4.35 us -> 6.88 us  [across(): return lax.ppermute(block, 'span', [(i, i ^ 1) for i in range(span_count)])]
  transfers between devices with their start and end apart: 15 -> 15, of which waited for: 7 -> 8; matrix products, arithmetic and copies ran while one was open for 5% -> 5% of each run, Pallas kernels for 3% -> 4%
where the time goes in v2:
time: 150 us
  starting transfers between devices  40.5 us (27%)
  Pallas kernels  37 us (25%)
  waiting for transfers between devices  32.2 us (21%)
  blocking collectives  25.3 us (17%)
  local copies, waits for them, and re-layouts  9.44 us (6%)
  other arithmetic  3.36 us (2%)
  between operations  1.56 us (1%)
    all_to_all x1, blocking collectives, on_device(): received = lax.all_to_all(out, 'span', 0, 0, tiled=True)  25.3 us
    pallas_call x1, Pallas kernels, steps(): pl.pallas_call(steps_kernel, out_shape=jax.ShapeDtypeStruct((64, 4, 384),...  24.3 us
    ppermute x7, waiting for transfers between devices, around(): lax.ppermute(block, 'plane', [(i, (i + step) % plane_count) for i in rang...  17.7 us
    all_to_all x1, starting transfers between devices, on_device(): lax.all_to_all(pack_inverse(matrix, span_count // 2), 'span', 0, 0, tiled...  12 us
    all_to_all x1, waiting for transfers between devices, on_device(): lax.all_to_all(pack_inverse(matrix, span_count // 2), 'span', 0, 0, tiled...  9.25 us
    unnamed x40, local copies, waits for them, and re-layouts  8.41 us
    ppermute x7, starting transfers between devices, around(): lax.ppermute(block, 'plane', [(i, (i + step) % plane_count) for i in rang...  7.6 us
    all_to_all x1, starting transfers between devices, on_device(): points = lax.all_to_all(sent, 'span', 0, 0, tiled=True)  7.24 us
  transfers between devices with their start and end apart: 15, of which 8 were waited for; matrix products, arithmetic and copies ran while one was open for 5% of the time, Pallas kernels for 4%

profile of v2, /device:TPU:1, one launch (start us, length us, event | category | flops | bytes accessed | tf_op | source)
XLA Modules:
  0.0 149.6 jit_solution(9942906452757883348)
XLA Ops:
  0.6 0.0 copy-start
  0.6 0.0 copy-start.11
  0.7 0.0 copy-start.12
  0.7 0.0 copy-start.6
  0.7 0.0 copy-start.3
  0.7 0.9 copy-done
  1.6 0.6 copy.32
  2.2 2.1 %shard_map.140 = s32[32,32,128]{2,1,0:T(8,128)} custom-call(f32[81,81]{1,0:T(8,128)} %bitcast.19), custom_call_target="tpu_custom_call" | custom-call | tf_op jit(solution)/shard_map/pallas_call | solution.py:146
  4.3 12.0 %all-to-all-start = ((s32[32,32,128]{2,1,0:T(8,128)}), s32[32,32,128]{2,1,0:T(8,128)S(1)}, u32[]{:S(2)}, u32[]{:S(2)}) async-start(s32[32,32,128]{2,1,0:T(8,128)} %shard_map.140), calls=%async_computation | async-start | bytes 1048576 | tf_op jit(solution)/shard_map/all_to_all | solution.py:450
  16.3 0.0 copy-done.11
  16.4 0.6 copy.30
  17.0 0.0 copy-done.12
  17.0 0.6 copy.29
  17.6 0.0 copy-done.6
  17.6 0.9 copy.22.adj_ref
  18.4 0.0 copy-done.3
  18.4 1.4 copy.23.c0_ref.c1_ref.c2_ref
  19.8 3.5 %shard_map.141 = s32[64,8,384]{2,1,0:T(8,128)} custom-call(s32[3]{0:T(128)} %step_ref.1, f32[3,4,81,128]{3,2,1,0:T(8,128)} %copy.22.adj_ref, bf16[8,2,4,81,128]{4,3,2,1,0:T(8,128)(2,1)} %copy.23.c0_ref.c1_ref.c2_ref, bf16[8,2,4,81,128]{4,3,2,1,0:T(8,128)(2,1)} %copy.23.c0_ref.c1_ref.c2_ref, bf16[8,2,4,81,128]{4,3,2,1,0:T(8,128)(2,1)} %copy.23.c0_ref.c1_ref.c2_ref), custom_call_target="tpu_custom_call" | custom-call | tf_op jit(solution)/shard_map/pallas_call | solution.py:187
  23.3 9.2 %all-to-all-done.own_ref = s32[32,32,128]{2,1,0:T(8,128)S(1)} async-done(((s32[32,32,128]{2,1,0:T(8,128)}), s32[32,32,128]{2,1,0:T(8,128)S(1)}, u32[]{:S(2)}, u32[]{:S(2)}) %all-to-all-start) | async-done | bytes 524320 | tf_op jit(solution)/shard_map/all_to_all | solution.py:450
  32.6 7.2 %all-to-all-start.1 = ((s32[64,8,384]{2,1,0:T(8,128)}), s32[64,8,384]{2,1,0:T(8,128)S(1)}, u32[]{:S(2)}, u32[]{:S(2)}) async-start(s32[64,8,384]{2,1,0:T(8,128)} %shard_map.141), calls=%async_computation.1 | async-start | bytes 1572864 | tf_op jit(solution)/shard_map/all_to_all | solution.py:464
  39.9 2.6 %collective-permute-start.3 = (s32[32,32,128]{2,1,0:T(8,128)S(1)}, s32[32,32,128]{2,1,0:T(8,128)S(1)}, u32[]{:S(2)}, u32[]{:S(2)}) collective-permute-start(s32[32,32,128]{2,1,0:T(8,128)S(1)} %all-to-all-done.own_ref), channel_id=1, source_target_pairs={{0,3},{1,0},{2,1},{3,2},{4,7},{5,4},{6,5},{7,6},{8,11},{9,8},{10,9... | collective-permute-start | bytes 1572872 | tf_op jit(solution)/shard_map/ppermute | solution.py:441
  42.4 0.0 collective-permute-start.1
  42.4 0.0 copy-done.13
  42.4 10.8 %collective-permute-done.3.right_ref = s32[32,32,128]{2,1,0:T(8,128)S(1)} collective-permute-done((s32[32,32,128]{2,1,0:T(8,128)S(1)}, s32[32,32,128]{2,1,0:T(8,128)S(1)}, u32[]{:S(2)}, u32[]{:S(2)}) %collective-permute-start.3) | collective-permute-done | bytes 524320 | tf_op jit(solution)/shard_map/ppermute | solution.py:441
  53.3 3.5 %collective-permute-start.7 = (s32[16,32,128]{2,1,0:T(8,128)S(1)}, s32[16,32,128]{2,1,0:T(8,128)S(1)}, u32[]{:S(2)}, u32[]{:S(2)}) collective-permute-start(s32[16,32,128]{2,1,0:T(8,128)S(1)} %slice.21), channel_id=1, source_target_pairs={{0,3},{1,0},{2,1},{3,2},{4,7},{5,4},{6,5},{7,6},{8,11},{9,8},{10,9... | collective-permute-start | bytes 786440 | tf_op jit(solution)/shard_map/ppermute | solution.py:441
  56.8 0.0 collective-permute-done.1.left_ref
  56.8 0.1 collective-permute-start.5
  56.9 0.3 convolution_convert_fusion
  57.2 1.7 %collective-permute-start = (s32[32,32,128]{2,1,0:T(8,128)S(1)}, s32[32,32,128]{2,1,0:T(8,128)}, u32[]{:S(2)}, u32[]{:S(2)}) collective-permute-start(s32[32,32,128]{2,1,0:T(8,128)S(1)} %all-to-all-done.own_ref), channel_id=1, source_target_pairs={{0,4},{4,0},{8,12},{12,8},{16,20},{20,16},{24,28},{28,24},{32,36},... | collective-permute-start | bytes 1572872 | tf_op jit(solution)/shard_map/ppermute | solution.py:446
  58.8 0.1 collective-permute-start.4
  58.9 0.4 collective-permute-start.2
  59.4 1.7 %collective-permute-done.7.ob_ref = s32[16,32,128]{2,1,0:T(8,128)S(1)} collective-permute-done((s32[16,32,128]{2,1,0:T(8,128)S(1)}, s32[16,32,128]{2,1,0:T(8,128)S(1)}, u32[]{:S(2)}, u32[]{:S(2)}) %collective-permute-start.7) | collective-permute-done | bytes 262176 | tf_op jit(solution)/shard_map/ppermute | solution.py:441
  61.1 2.2 %collective-permute-start.8 = (s32[16,32,128]{2,1,0:T(8,128)S(1)}, s32[16,32,128]{2,1,0:T(8,128)}, u32[]{:S(2)}, u32[]{:S(2)}) collective-permute-start(s32[16,32,128]{2,1,0:T(8,128)S(1)} %collective-permute-done.7.ob_ref), channel_id=1, source_target_pairs={{0,4},{4,0},{8,12},{12,8},{16,20},{20,16},{24,28},{28,24},{32,36},... | collective-permute-start | bytes 786440 | tf_op jit(solution)/shard_map/ppermute | solution.py:446
  63.3 1.1 collective-permute-done.5.oa_ref
  64.4 2.5 %collective-permute-start.6 = (s32[16,32,128]{2,1,0:T(8,128)}, s32[16,32,128]{2,1,0:T(8,128)}, u32[]{:S(2)}, u32[]{:S(2)}) collective-permute-start(s32[16,32,128]{2,1,0:T(8,128)} %collective-permute-done.5.oa_ref), channel_id=1, source_target_pairs={{0,4},{4,0},{8,12},{12,8},{16,20},{20,16},{24,28},{28,24},{32,36},... | collective-permute-start | bytes 786440 | tf_op jit(solution)/shard_map/ppermute | solution.py:446
  66.9 0.0 copy-done.4
  66.9 0.9 copy.26.fwd_ref
  67.9 0.6 pad_add_fusion.place_ref
  68.5 0.8 pad_maximum_fusion.1.back_ref
  69.2 0.0 collective-permute-done.own2_ref
  69.2 0.0 collective-permute-done.8.ob2_ref
  69.2 0.0 collective-permute-done.6.oa2_ref
  69.3 0.0 collective-permute-done.4.right2_ref
  69.3 0.0 collective-permute-done.2.left2_ref
  69.3 0.0 all-to-all-done.1.r_ref
  69.3 0.9 copy-done.1
  70.2 24.3 %shard_map.142 = s32[64,4,384]{2,1,0:T(4,128)} custom-call(s32[2]{0:T(128)} %pad_add_fusion.place_ref, f32[2,128]{1,0:T(2,128)} %metric_ref.1, s32[64,8,384]{2,1,0:T(8,128)} %copy-done.1, s32[32,32,128]{2,1,0:T(8,128)} %copy-done.2, s32[32,32,128]{2,1,0:T(8,128)} %collective-permute-done.own2_ref, s32[32,32,128]{2,1,0:T(8,128)} %copy-done.5, ...), custom_call_target="tpu_custom_call" | custom-call | tf_op jit(solution)/shard_map/pallas_call | solution.py:328
  94.5 25.3 %all_to_all.20.r_ref = s32[64,4,384]{2,1,0:T(4,128)} all-to-all(s32[64,4,384]{2,1,0:T(4,128)} %shard_map.142), channel_id=1, replica_groups=mesh['span'=64,'plane'=4] {'span'}, dimensions={0} | all-to-all | bytes 786432 | tf_op jit(solution)/shard_map/all_to_all | solution.py:466
  119.8 3.3 %shard_map.144.p0_ref = f32[4,1024]{1,0:T(4,128)} custom-call(s32[64,4,384]{2,1,0:T(4,128)} %all_to_all.20.r_ref, s32[1,2048]{1,0:T(1,128)} %bitcast.21, s32[1,2048]{1,0:T(1,128)} %bitcast.20), custom_call_target="tpu_custom_call" | custom-call | tf_op jit(solution)/shard_map/pallas_call | solution.py:366
  123.2 0.2 collective-permute-start.11
  123.4 0.4 collective-permute-start.10
  123.8 0.9 collective-permute-start.9
  124.6 1.3 collective-permute-done.11.p3_ref
  126.0 1.7 %collective-permute-done.10.p2_ref = f32[4,1024]{1,0:T(4,128)S(1)} collective-permute-done((f32[4,1024]{1,0:T(4,128)}, f32[4,1024]{1,0:T(4,128)S(1)}, u32[]{:S(2)}, u32[]{:S(2)}) %collective-permute-start.10) | collective-permute-done | bytes 16416 | tf_op jit(solution)/shard_map/ppermute | solution.py:441
  127.7 1.0 collective-permute-done.9.p1_ref
  128.7 0.0 copy-done.8
  128.7 0.6 copy-done.10
  129.3 1.5 %shard_map.145 = (f32[4,1024]{1,0:T(4,128)}, f32[64,1,128]{2,1,0:T(1,128)}) custom-call(f32[4,1024]{1,0:T(4,128)} %weight_ref.1, f32[4,1024]{1,0:T(4,128)} %shard_map.144.p0_ref, f32[4,1024]{1,0:T(4,128)} %copy-done.10, f32[4,1024]{1,0:T(4,128)} %copy-done.9, f32[4,1024]{1,0:T(4,128)} %copy-done.8), custom_call_target="tpu_custom_call" | custom-call | tf_op jit(solution)/shard_map/pallas_call | solution.py:388
  130.8 6.7 %all-to-all-start.3 = ((f32[64,1,128]{2,1,0:T(1,128)}), f32[64,1,128]{2,1,0:T(1,128)S(1)}, u32[]{:S(2)}, u32[]{:S(2)}) async-start(f32[64,1,128]{2,1,0:T(1,128)} %get-tuple-element.13), calls=%async_computation.3 | async-start | bytes 65536 | tf_op jit(solution)/shard_map/all_to_all | solution.py:471
  137.5 2.2 %shard_map.143 = f32[3,4,81,128]{3,2,1,0:T(8,128)} custom-call(s32[64,4,384]{2,1,0:T(4,128)} %all_to_all.20.r_ref), custom_call_target="tpu_custom_call" | custom-call | tf_op jit(solution)/shard_map/pallas_call | solution.py:410
  139.7 2.0 %copy.27 = f32[3,4,81,128]{3,1,2,0:T(4,128)} copy(f32[3,4,81,128]{3,2,1,0:T(8,128)} %shard_map.143) | data formatting | bytes 995328
  141.7 5.2 %all-to-all-done.3 = f32[64,1,128]{2,1,0:T(1,128)S(1)} async-done(((f32[64,1,128]{2,1,0:T(1,128)}), f32[64,1,128]{2,1,0:T(1,128)S(1)}, u32[]{:S(2)}, u32[]{:S(2)}) %all-to-all-start.3) | async-done | bytes 32800 | tf_op jit(solution)/shard_map/all_to_all | solution.py:471
  146.9 0.7 slice_reduce_fusion
  148.3 1.3 dynamic-slice_multiply_fusion
  (26 shorter events, 0.2 us)
Async XLA Ops:
  0.6 0.9 copy-start
  0.6 15.7 %copy-start.11 = (s32[1024,2]{0,1:T(2,128)S(1)}, s32[1024,2]{0,1:T(2,128)}, u32[]{:S(2)}) copy-start(s32[1024,2]{0,1:T(2,128)} %param.18) | copy-start | bytes 24580
  0.7 16.3 %copy-start.12 = (s32[1024,2]{0,1:T(2,128)S(1)}, s32[1024,2]{0,1:T(2,128)}, u32[]{:S(2)}) copy-start(s32[1024,2]{0,1:T(2,128)} %param.19) | copy-start | bytes 24580
  0.7 16.9 %copy-start.6 = (f32[3,4,81,128]{3,1,2,0:T(4,128)S(1)}, f32[3,4,81,128]{3,1,2,0:T(4,128)}, u32[]{:S(2)}) copy-start(f32[3,4,81,128]{3,1,2,0:T(4,128)} %param.13) | copy-start | bytes 1492996
  0.7 17.7 %copy-start.3 = (bf16[8,2,4,81,128]{4,2,3,1,0:T(4,128)(2,1)S(1)}, bf16[8,2,4,81,128]{4,2,3,1,0:T(4,128)(2,1)}, u32[]{:S(2)}) copy-start(bf16[8,2,4,81,128]{4,2,3,1,0:T(4,128)(2,1)} %param.14) | copy-start | bytes 3981316
  4.3 28.3 %all-to-all-start = ((s32[32,32,128]{2,1,0:T(8,128)}), s32[32,32,128]{2,1,0:T(8,128)S(1)}, u32[]{:S(2)}, u32[]{:S(2)}) async-start(s32[32,32,128]{2,1,0:T(8,128)} %shard_map.140), calls=%async_computation | async-start | bytes 1048576 | tf_op jit(solution)/shard_map/all_to_all | solution.py:450
  23.3 19.1 %copy-start.13 = (s32[256]{0:T(256)S(1)}, s32[256]{0:T(256)}, u32[]{:S(2)}) copy-start(s32[256]{0:T(256)} %constant.81) | copy-start | bytes 3076
  23.3 19.1 %copy-start.14 = (s32[256]{0:T(256)S(1)}, s32[256]{0:T(256)}, u32[]{:S(2)}) copy-start(s32[256]{0:T(256)} %constant.79) | copy-start | bytes 3076
  23.3 19.1 %copy-start.15 = (s32[256]{0:T(256)S(1)}, s32[256]{0:T(256)}, u32[]{:S(2)}) copy-start(s32[256]{0:T(256)} %constant.71.clone) | copy-start | bytes 3076
  23.3 33.5 %copy-start.16 = (bf16[256,512]{1,0:T(8,128)(2,1)S(1)}, bf16[256,512]{1,0:T(8,128)(2,1)}, u32[]{:S(2)}) copy-start(bf16[256,512]{1,0:T(8,128)(2,1)} %constant.72.clone) | copy-start | bytes 786436
  32.6 24.6 %copy-start.2 = (s32[32,32,128]{2,1,0:T(8,128)}, s32[32,32,128]{2,1,0:T(8,128)S(1)}, u32[]{:S(2)}) copy-start(s32[32,32,128]{2,1,0:T(8,128)S(1)} %all-to-all-done.own_ref) | copy-start | bytes 1572868
  32.6 36.7 %all-to-all-start.1 = ((s32[64,8,384]{2,1,0:T(8,128)}), s32[64,8,384]{2,1,0:T(8,128)S(1)}, u32[]{:S(2)}, u32[]{:S(2)}) async-start(s32[64,8,384]{2,1,0:T(8,128)} %shard_map.141), calls=%async_computation.1 | async-start | bytes 1572864 | tf_op jit(solution)/shard_map/all_to_all | solution.py:464
  39.9 13.4 %collective-permute-start.3 = (s32[32,32,128]{2,1,0:T(8,128)S(1)}, s32[32,32,128]{2,1,0:T(8,128)S(1)}, u32[]{:S(2)}, u32[]{:S(2)}) collective-permute-start(s32[32,32,128]{2,1,0:T(8,128)S(1)} %all-to-all-done.own_ref), channel_id=1, source_target_pairs={{0,3},{1,0},{2,1},{3,2},{4,7},{5,4},{6,5},{7,6},{8,11},{9,8},{10,9... | collective-permute-start | bytes 1572872 | tf_op jit(solution)/shard_map/ppermute | solution.py:441
  42.4 14.4 %collective-permute-start.1 = (s32[32,32,128]{2,1,0:T(8,128)S(1)}, s32[32,32,128]{2,1,0:T(8,128)S(1)}, u32[]{:S(2)}, u32[]{:S(2)}) collective-permute-start(s32[32,32,128]{2,1,0:T(8,128)S(1)} %all-to-all-done.own_ref), channel_id=1, source_target_pairs={{0,1},{1,2},{2,3},{3,0},{4,5},{5,6},{6,7},{7,4},{8,9},{9,10},{10,1... | collective-permute-start | bytes 1572872 | tf_op jit(solution)/shard_map/ppermute | solution.py:441
  53.3 13.7 %copy-start.4 = (s32[32,32,128]{2,1,0:T(8,128)}, s32[32,32,128]{2,1,0:T(8,128)S(1)}, u32[]{:S(2)}) copy-start(s32[32,32,128]{2,1,0:T(8,128)S(1)} %collective-permute-done.3.right_ref) | copy-start | bytes 1572868
  53.3 7.8 %collective-permute-start.7 = (s32[16,32,128]{2,1,0:T(8,128)S(1)}, s32[16,32,128]{2,1,0:T(8,128)S(1)}, u32[]{:S(2)}, u32[]{:S(2)}) collective-permute-start(s32[16,32,128]{2,1,0:T(8,128)S(1)} %slice.21), channel_id=1, source_target_pairs={{0,3},{1,0},{2,1},{3,2},{4,7},{5,4},{6,5},{7,6},{8,11},{9,8},{10,9... | collective-permute-start | bytes 786440 | tf_op jit(solution)/shard_map/ppermute | solution.py:441
  56.8 11.1 %copy-start.5 = (s32[32,32,128]{2,1,0:T(8,128)}, s32[32,32,128]{2,1,0:T(8,128)S(1)}, u32[]{:S(2)}) copy-start(s32[32,32,128]{2,1,0:T(8,128)S(1)} %collective-permute-done.1.left_ref) | copy-start | bytes 1572868
  56.8 7.6 %collective-permute-start.5 = (s32[16,32,128]{2,1,0:T(8,128)S(1)}, s32[16,32,128]{2,1,0:T(8,128)}, u32[]{:S(2)}, u32[]{:S(2)}) collective-permute-start(s32[16,32,128]{2,1,0:T(8,128)S(1)} %slice.20), channel_id=1, source_target_pairs={{0,1},{1,2},{2,3},{3,0},{4,5},{5,6},{6,7},{7,4},{8,9},{9,10},{10,1... | collective-permute-start | bytes 786440 | tf_op jit(solution)/shard_map/ppermute | solution.py:441
  57.2 12.1 %collective-permute-start = (s32[32,32,128]{2,1,0:T(8,128)S(1)}, s32[32,32,128]{2,1,0:T(8,128)}, u32[]{:S(2)}, u32[]{:S(2)}) collective-permute-start(s32[32,32,128]{2,1,0:T(8,128)S(1)} %all-to-all-done.own_ref), channel_id=1, source_target_pairs={{0,4},{4,0},{8,12},{12,8},{16,20},{20,16},{24,28},{28,24},{32,36},... | collective-permute-start | bytes 1572872 | tf_op jit(solution)/shard_map/ppermute | solution.py:446
  58.8 10.4 %collective-permute-start.4 = (s32[32,32,128]{2,1,0:T(8,128)S(1)}, s32[32,32,128]{2,1,0:T(8,128)}, u32[]{:S(2)}, u32[]{:S(2)}) collective-permute-start(s32[32,32,128]{2,1,0:T(8,128)S(1)} %collective-permute-done.3.right_ref), channel_id=1, source_target_pairs={{0,4},{4,0},{8,12},{12,8},{16,20},{20,16},{24,28},{28,24},{32,36},... | collective-permute-start | bytes 1572872 | tf_op jit(solution)/shard_map/ppermute | solution.py:446
  58.9 10.3 %collective-permute-start.2 = (s32[32,32,128]{2,1,0:T(8,128)S(1)}, s32[32,32,128]{2,1,0:T(8,128)}, u32[]{:S(2)}, u32[]{:S(2)}) collective-permute-start(s32[32,32,128]{2,1,0:T(8,128)S(1)} %collective-permute-done.1.left_ref), channel_id=1, source_target_pairs={{0,4},{4,0},{8,12},{12,8},{16,20},{20,16},{24,28},{28,24},{32,36},... | collective-permute-start | bytes 1572872 | tf_op jit(solution)/shard_map/ppermute | solution.py:446
  61.1 8.2 %copy-start.7 = (s32[16,32,128]{2,1,0:T(8,128)}, s32[16,32,128]{2,1,0:T(8,128)S(1)}, u32[]{:S(2)}) copy-start(s32[16,32,128]{2,1,0:T(8,128)S(1)} %collective-permute-done.7.ob_ref) | copy-start | bytes 786436
  61.1 8.2 %collective-permute-start.8 = (s32[16,32,128]{2,1,0:T(8,128)S(1)}, s32[16,32,128]{2,1,0:T(8,128)}, u32[]{:S(2)}, u32[]{:S(2)}) collective-permute-start(s32[16,32,128]{2,1,0:T(8,128)S(1)} %collective-permute-done.7.ob_ref), channel_id=1, source_target_pairs={{0,4},{4,0},{8,12},{12,8},{16,20},{20,16},{24,28},{28,24},{32,36},... | collective-permute-start | bytes 786440 | tf_op jit(solution)/shard_map/ppermute | solution.py:446
  64.4 4.8 %collective-permute-start.6 = (s32[16,32,128]{2,1,0:T(8,128)}, s32[16,32,128]{2,1,0:T(8,128)}, u32[]{:S(2)}, u32[]{:S(2)}) collective-permute-start(s32[16,32,128]{2,1,0:T(8,128)} %collective-permute-done.5.oa_ref), channel_id=1, source_target_pairs={{0,4},{4,0},{8,12},{12,8},{16,20},{20,16},{24,28},{28,24},{32,36},... | collective-permute-start | bytes 786440 | tf_op jit(solution)/shard_map/ppermute | solution.py:446
  69.3 0.9 copy-start.1
  123.2 2.8 %collective-permute-start.11 = (f32[4,1024]{1,0:T(4,128)}, f32[4,1024]{1,0:T(4,128)S(1)}, u32[]{:S(2)}, u32[]{:S(2)}) collective-permute-start(f32[4,1024]{1,0:T(4,128)} %shard_map.144.p0_ref), channel_id=1, source_target_pairs={{0,3},{1,0},{2,1},{3,2},{4,7},{5,4},{6,5},{7,6},{8,11},{9,8},{10,9... | collective-permute-start | bytes 49160 | tf_op jit(solution)/shard_map/ppermute | solution.py:441
  123.4 4.3 %collective-permute-start.10 = (f32[4,1024]{1,0:T(4,128)}, f32[4,1024]{1,0:T(4,128)S(1)}, u32[]{:S(2)}, u32[]{:S(2)}) collective-permute-start(f32[4,1024]{1,0:T(4,128)} %shard_map.144.p0_ref), channel_id=1, source_target_pairs={{0,2},{1,3},{2,0},{3,1},{4,6},{5,7},{6,4},{7,5},{8,10},{9,11},{10,... | collective-permute-start | bytes 49160 | tf_op jit(solution)/shard_map/ppermute | solution.py:441
  123.8 4.9 %collective-permute-start.9 = (f32[4,1024]{1,0:T(4,128)}, f32[4,1024]{1,0:T(4,128)S(1)}, u32[]{:S(2)}, u32[]{:S(2)}) collective-permute-start(f32[4,1024]{1,0:T(4,128)} %shard_map.144.p0_ref), channel_id=1, source_target_pairs={{0,1},{1,2},{2,3},{3,0},{4,5},{5,6},{6,7},{7,4},{8,9},{9,10},{10,1... | collective-permute-start | bytes 49160 | tf_op jit(solution)/shard_map/ppermute | solution.py:441
  126.0 2.7 %copy-start.8 = (f32[4,1024]{1,0:T(4,128)}, f32[4,1024]{1,0:T(4,128)S(1)}, u32[]{:S(2)}) copy-start(f32[4,1024]{1,0:T(4,128)S(1)} %collective-permute-done.11.p3_ref) | copy-start | bytes 49156
  127.7 1.0 copy-start.9
  128.7 0.6 copy-start.10
  130.8 16.1 %all-to-all-start.3 = ((f32[64,1,128]{2,1,0:T(1,128)}), f32[64,1,128]{2,1,0:T(1,128)S(1)}, u32[]{:S(2)}, u32[]{:S(2)}) async-start(f32[64,1,128]{2,1,0:T(1,128)} %get-tuple-element.13), calls=%async_computation.3 | async-start | bytes 65536 | tf_op jit(solution)/shard_map/all_to_all | solution.py:471

commit v3 on v2

--- a/solution.py
+++ b/solution.py
@@ -1,3 +1,5 @@
+import functools
+
 import jax
 import jax.numpy as jnp
 import numpy as np
@@ -15,6 +17,7 @@
 VMEM_BYTES = 56 * 1024 * 1024
 LEVELS = 32767.0
 SCALE_LANE = 250
+LINES = 58
 
 
 def chebyshev_matrix(degree):
@@ -131,12 +134,18 @@
     turned = w_ref[...].T
     w_ref[...] = turned
     f_ref[...] = jnp.zeros_like(f_ref)
-    for r in range(Q):
-        line, lane = divmod(r * QP, 128)
-        first = min(Q, 128 - lane)
-        f_ref[line, lane : lane + first] = w_ref[r, 0:first]
-        if first < Q:
-            f_ref[line + 1, 0 : Q - first] = w_ref[r, first:Q]
+    for k in range(16):
+        line, lane = divmod(k * QP, 128)
+        count = (Q - k + 15) // 16
+        block = w_ref[pl.ds(k, count, stride=16), :]
+        if lane:
+            block = jnp.roll(block, lane, axis=1)
+        place = lax.broadcasted_iota(jnp.int32, (count, 128), 1)
+        here = pl.ds(line, count, stride=11)
+        f_ref[here, :] = f_ref[here, :] + jnp.where(place >= lane, block, 0.0)
+        if lane + Q > 128:
+            after = pl.ds(line + 1, count, stride=11)
+            f_ref[after, :] = f_ref[after, :] + jnp.where(place < lane, block, 0.0)
     f_ref[56, 0:Q] = w_ref[Q, 0:Q]
     f_ref[57, 0:Q] = w_ref[Q + 1, 0:Q]
     o_ref[...] = jnp.broadcast_to(pair_up(f_ref[0:32, :], f_ref[32:64, :])[None], o_ref.shape)
@@ -210,32 +219,64 @@
     )
 
 
-def steps_kernel(
-    place_ref, metric_ref, r_ref, own_ref, own2_ref, left_ref, left2_ref, right_ref, right2_ref,
-    oa_ref, oa2_ref, ob_ref, ob2_ref, fwd_ref, back_ref, both_ref,
-    out_ref,
-    ht, rows, x, v, coef, solved, wall, spread, turn,
-):
+def turn_pieces(pieces, write):
+    def lines(k, both):
+        pair = jnp.concatenate([ref[:, k, :] for ref in pieces], axis=0).T
+        write(pl.multiple_of(k * 128, 128), low_of(pair))
+        if both:
+            write(pl.multiple_of(k * 128 + 4096, 128), high_of(pair))
+
+    def both_halves(k, carry):
+        lines(k, True)
+        return carry
+
+    def low_half(k, carry):
+        lines(k, False)
+        return carry
+
+    lax.fori_loop(0, LINES - 32, both_halves, 0)
+    lax.fori_loop(LINES - 32, 32, low_half, 0)
+
+
+def turn_kernel(own_ref, own2_ref, o_ref):
+    def write(row, block):
+        o_ref[pl.ds(row, 128), 0:64] = block
+
+    turn_pieces((own_ref, own2_ref), write)
+
+
+def turn_own(own, own2):
+    return pl.pallas_call(
+        turn_kernel,
+        out_shape=jax.ShapeDtypeStruct((LINES * 128, 128), F32),
+        in_specs=[vmem_spec()] * 2,
+        out_specs=vmem_spec(),
+        compiler_params=params(),
+    )(own, own2)
+
+
+def advance(place_ref, metric_ref, x, v, step, both_ref, fwd_ref, coef):
     chip = place_ref[0]
-    lanes = (
-        (own_ref, own2_ref, left_ref, left2_ref),
-        (right_ref, right2_ref, oa_ref, oa2_ref, ob_ref, ob2_ref),
-    )
-
-    def turn_inverse(k, carry):
-        row = pl.multiple_of(k * 128, 128)
-        for half in range(2):
-            pair = jnp.concatenate([ref[:, k, :] for ref in lanes[half]], axis=0).T
-            ht[half, pl.ds(row, 128), :] = low_of(pair)
-            ht[half, pl.ds(row + 4096, 128), :] = high_of(pair)
-        return carry
-
-    lax.fori_loop(0, 32, turn_inverse, 0)
-    for half in range(2):
-        rows[half] = (
-            ht[half, 7168 : 7168 + QP, :] * 2.0**15 + ht[half, 7296 : 7296 + QP, :]
-        ) * (2.0**-30 / LEVELS)
-
+    for e in range(2):
+        m0 = metric_ref[0, chip + 64 * e]
+        m1 = metric_ref[1, chip + 64 * e]
+        for c in range(3):
+            field = x[e * 3 + c]
+            high, low = in_two(field)
+            large = jnp.dot(both_ref[...], high, preferred_element_type=F32)
+            small = jnp.dot(both_ref[0 : 2 * QP, :], low, preferred_element_type=F32)
+            slopes = large[0 : 2 * QP] + (large[2 * QP : 4 * QP] + small)
+            x[e * 3 + c] = (
+                field
+                + v[0, e, step] * (m0 * slopes[0:QP])
+                + v[1, e, step] * (m1 * slopes[QP : 2 * QP])
+            )
+    modes = transform(x[...].reshape(6 * QP, 256), fwd_ref)
+    coef[0] = modes[:, 0:128]
+    coef[1] = modes[:, 128:256]
+
+
+def first_kernel(place_ref, metric_ref, r_ref, fwd_ref, both_ref, coef, v, x, spread):
     x[...] = jnp.zeros_like(x)
     v[...] = jnp.zeros_like(v)
     for g in range(3):
@@ -261,32 +302,59 @@
                     x[e * 3 + i, 0:Q, :] = part
                 else:
                     v[(g - 1), e, i, 0:Q, :] = part
+    advance(place_ref, metric_ref, x, v, 0, both_ref, fwd_ref, coef)
+
+
+def first_modes(place, metric, points, fwd, both):
+    return pl.pallas_call(
+        first_kernel,
+        out_shape=(
+            jax.ShapeDtypeStruct((2, 6 * QP, 128), F32),
+            jax.ShapeDtypeStruct((2, 2, 3, QP, 256), F32),
+        ),
+        in_specs=[smem_spec(), smem_spec()] + [vmem_spec()] * 3,
+        out_specs=(vmem_spec(), vmem_spec()),
+        scratch_shapes=[pltpu.VMEM((6, QP, 256), F32), pltpu.VMEM((256, 256), F32)],
+        compiler_params=params(),
+    )(place, metric, points, fwd, both)
+
+
+def steps_kernel(
+    place_ref, metric_ref, turned_ref, left_ref, left2_ref, right_ref, right2_ref, oa_ref, oa2_ref, ob_ref, ob2_ref,
+    first_ref, v, fwd_ref, back_ref, both_ref,
+    out_ref,
+    ht, rows, x, coef, solved, wall, turn, sem,
+):
+    load = pltpu.make_async_copy(turned_ref, ht.at[0], sem)
+    load.start()
+
+    def write(row, block):
+        ht[1, pl.ds(row, 128), :] = block
+
+    turn_pieces((right_ref, right2_ref, oa_ref, oa2_ref, ob_ref, ob2_ref), write)
+    load.wait()
+
+    def write_left(row, block):
+        ht[0, pl.ds(row, 128), 64:128] = block
+
+    turn_pieces((left_ref, left2_ref), write_left)
+    for half in range(2):
+        rows[half] = (
+            ht[half, 7168 : 7168 + QP, :] * 2.0**15 + ht[half, 7296 : 7296 + QP, :]
+        ) * (2.0**-30 / LEVELS)
 
     for step in range(NSTEP):
-        for e in range(2):
-            m0 = metric_ref[0, chip + 64 * e]
-            m1 = metric_ref[1, chip + 64 * e]
-            for c in range(3):
-                field = x[e * 3 + c]
-                high, low = in_two(field)
-                large = jnp.dot(both_ref[...], high, preferred_element_type=F32)
-                small = jnp.dot(both_ref[0 : 2 * QP, :], low, preferred_element_type=F32)
-                slopes = large[0 : 2 * QP] + (large[2 * QP : 4 * QP] + small)
-                x[e * 3 + c] = (
-                    field
-                    + v[0, e, step] * (m0 * slopes[0:QP])
-                    + v[1, e, step] * (m1 * slopes[QP : 2 * QP])
-                )
-        modes = transform(x[...].reshape(6 * QP, 256), fwd_ref)
-        coef[0] = modes[:, 0:128]
-        coef[1] = modes[:, 128:256]
+        if step > 0:
+            advance(place_ref, metric_ref, x, v, step, both_ref, fwd_ref, coef)
+        modes = coef if step > 0 else first_ref
         for half in range(2):
             for e in range(2):
 
-                def column(r, sums, half=half, e=e):
+                def column(r, sums, half=half, e=e, modes=modes):
                     h = ht[half, pl.ds(pl.multiple_of(r * QP, 8), QP), :]
                     return tuple(
-                        sums[c] + h * coef[half, pl.ds((e * 3 + c) * QP + r, 1), :] for c in range(3)
+                        sums[c] + h * modes[half, pl.ds((e * 3 + c) * QP + r, 1), :]
+                        for c in range(3)
                     )
 
                 zero = jnp.zeros((QP, 128), F32)
@@ -324,25 +392,25 @@
         out_ref[:, z, 0:256] = turned[z * 64 : (z + 1) * 64, :]
 
 
-def steps(place, metric, points, inverse, fwd, back):
+def steps(place, metric, turned, pieces, first, velocity, fwd, back, both):
     return pl.pallas_call(
         steps_kernel,
         out_shape=jax.ShapeDtypeStruct((64, 4, 384), jnp.int32),
-        in_specs=[smem_spec(), smem_spec()] + [vmem_spec()] * (len(inverse) + 4),
+        in_specs=[smem_spec(), smem_spec(), pl.BlockSpec(memory_space=pl.ANY)]
+        + [vmem_spec()] * (len(pieces) + 5),
         out_specs=vmem_spec(),
         scratch_shapes=[
-            pltpu.VMEM((2, 64 * 128, 128), F32),
+            pltpu.VMEM((2, LINES * 128, 128), F32),
             pltpu.VMEM((2, QP, 128), F32),
             pltpu.VMEM((6, QP, 256), F32),
-            pltpu.VMEM((2, 2, 3, QP, 256), F32),
             pltpu.VMEM((2, 6 * QP, 128), F32),
             pltpu.VMEM((6, QP, 256), F32),
             pltpu.VMEM((2, QP, 256), F32),
-            pltpu.VMEM((256, 256), F32),
             pltpu.VMEM((256, 256), jnp.int32),
+            pltpu.SemaphoreType.DMA,
         ],
         compiler_params=params(),
-    )(place, metric, points, *inverse, fwd, back, slope_table())
+    )(place, metric, turned, *pieces, first, velocity, fwd, back, both)
 
 
 def wall_kernel(r_ref, local_ref, element_ref, o_ref):
@@ -395,6 +463,23 @@
         out_specs=(vmem_spec(), vmem_spec()),
         compiler_params=params(),
     )(weight, *parts)
+
+
+def share_kernel(plane_ref, weighted_ref, squares_ref, o_ref, *, entries):
+    width = o_ref.shape[1]
+    total = jnp.sum(squares_ref[:, 0, :], axis=0, keepdims=True)[:, 0:1]
+    start = pl.multiple_of(plane_ref[0] * width, 128)
+    o_ref[...] = weighted_ref[:, pl.ds(start, width)] * lax.rsqrt(total * (1.0 / entries) + 1e-06)
+
+
+def share(plane, weighted, squares, width, entries):
+    return pl.pallas_call(
+        functools.partial(share_kernel, entries=entries),
+        out_shape=jax.ShapeDtypeStruct((weighted.shape[0], width), F32),
+        in_specs=[smem_spec(), vmem_spec(), vmem_spec()],
+        out_specs=vmem_spec(),
+        compiler_params=params(),
+    )(plane, weighted, squares)
 
 
 def unpack_kernel(r_ref, o_ref, t_ref):
@@ -454,26 +539,37 @@
     element = wall_element.T.reshape(1, 2 * wall_count) - plane * adjoint.shape[3]
     sent = pack_points(adjoint, checkpoints, checkpoint_step)
     own, sent, local, element = lax.optimization_barrier((own, sent, local, element))
+    own2 = across(own)
     left = around(own, 1)
     right = around(own, 3)
+    points = lax.all_to_all(sent, "span", 0, 0, tiled=True)
+    turned = turn_own(own, own2)
+    left, right, turned = lax.optimization_barrier((left, right, turned))
     oa = around(left[:16], 1)
     ob = around(right[16:], 3)
-    inverse = []
-    for piece in (own, left, right, oa, ob):
-        inverse += [piece, across(piece)]
-    points = lax.all_to_all(sent, "span", 0, 0, tiled=True)
-    out = steps(place, metric, points, inverse, fwd, back)
+    both = slope_table()
+    first, velocity = first_modes(place, metric, points, fwd, both)
+    pieces = []
+    for piece in (left, right):
+        pieces += [piece, across(piece)]
+    oa, ob, first = lax.optimization_barrier((oa, ob, first))
+    for piece in (oa, ob):
+        pieces += [piece, across(piece)]
+    out = steps(place, metric, turned, pieces, first, velocity, fwd, back, both)
     received = lax.all_to_all(out, "span", 0, 0, tiled=True)
 
     partial_sum = wall_sums(received, local, element)
     parts = [partial_sum] + [around(partial_sum, k) for k in range(1, plane_count)]
     weighted, square = weigh(wall_weight, parts, span_count)
     squares = lax.all_to_all(square, "span", 0, 0, tiled=True)
-    total = jnp.sum(squares[:, 0, 0])
-    share_width = wall_count // plane_count
-    share = lax.dynamic_slice_in_dim(weighted, plane * share_width, share_width, 1)
-    inverse_rms = lax.rsqrt(total / (adjoint.shape[1] * span_count * wall_count) + 1e-06)
-    return (unpack(received), share * inverse_rms)
+    gradient = share(
+        plane.reshape(1).astype(jnp.int32),
+        weighted,
+        squares,
+        wall_count // plane_count,
+        adjoint.shape[1] * span_count * wall_count,
+    )
+    return (unpack(received), gradient)
 
 
 def solution(mesh):

time: 150 us -> 157 us (1.047)
  Pallas kernels: 37 us -> 52.2 us
  waiting for transfers between devices: 32.2 us -> 26.8 us
  starting transfers between devices: 40.5 us -> 36 us
  local copies, waits for them, and re-layouts: 9.44 us -> 13.1 us
  other arithmetic: 3.36 us -> 1.46 us
    pallas_call x0 -> x3, Pallas kernels: none -> 11.9 us  [the longest x1 6.99 us: turn_own(): pl.pallas_call(turn_kernel, out_shape=jax.ShapeDtypeStruct((LINES * 128,...]
    ppermute x7, waiting for transfers between devices: 17.7 us -> 11.4 us  [around(): lax.ppermute(block, 'plane', [(i, (i + step) % plane_count) for i in rang...]
    pallas_call x1, Pallas kernels: 24.3 us -> 27.8 us  [steps(): pl.pallas_call(steps_kernel, out_shape=jax.ShapeDtypeStruct((64, 4, 384),...]
    ppermute x5, starting transfers between devices: 6.88 us -> 3.41 us  [across(): return lax.ppermute(block, 'span', [(i, i ^ 1) for i in range(span_count)])]
    unnamed x40 -> x50, local copies, waits for them, and re-layouts: 8.41 us -> 10.6 us
    ppermute x7, starting transfers between devices: 7.6 us -> 6 us  [around(): lax.ppermute(block, 'plane', [(i, (i + step) % plane_count) for i in rang...]
  transfers between devices with their start and end apart: 15 -> 15, of which waited for: 8 -> 10; matrix products, arithmetic and copies ran while one was open for 5% -> 6% of each run, Pallas kernels for 4% -> 10%
where the time goes in v3:
time: 157 us; the launch traced here: 156 us
  Pallas kernels  52.2 us (33%)
  starting transfers between devices  36 us (23%)
  waiting for transfers between devices  26.8 us (17%)
  blocking collectives  25.4 us (16%)
  local copies, waits for them, and re-layouts  13.1 us (8%)
    pallas_call x1, Pallas kernels, steps(): pl.pallas_call(steps_kernel, out_shape=jax.ShapeDtypeStruct((64, 4, 384),...  27.8 us
    all_to_all x1, blocking collectives, on_device(): received = lax.all_to_all(out, 'span', 0, 0, tiled=True)  25.4 us
    all_to_all x1, starting transfers between devices, on_device(): lax.all_to_all(pack_inverse(matrix, span_count // 2), 'span', 0, 0, tiled...  12 us
    ppermute x7, waiting for transfers between devices, around(): lax.ppermute(block, 'plane', [(i, (i + step) % plane_count) for i in rang...  11.4 us
    unnamed x50, local copies, waits for them, and re-layouts  10.6 us
    all_to_all x1, waiting for transfers between devices, on_device(): lax.all_to_all(pack_inverse(matrix, span_count // 2), 'span', 0, 0, tiled...  9.22 us
    all_to_all x1, starting transfers between devices, on_device(): squares = lax.all_to_all(square, 'span', 0, 0, tiled=True)  7.3 us
    all_to_all x1, starting transfers between devices, on_device(): points = lax.all_to_all(sent, 'span', 0, 0, tiled=True)  7.24 us
  transfers between devices with their start and end apart: 15, of which 10 were waited for; matrix products, arithmetic and copies ran while one was open for 6% of the time, Pallas kernels for 10%

profile of v3, /device:TPU:1, one launch (start us, length us, event | category | flops | bytes accessed | tf_op | source)
XLA Modules:
  0.0 156.1 jit_solution(5965328201102806913)
XLA Ops:
  0.6 0.0 copy-start
  0.7 0.9 copy-done
  1.6 0.6 copy.34
  2.2 2.0 %shard_map.140 = s32[32,32,128]{2,1,0:T(8,128)} custom-call(f32[81,81]{1,0:T(8,128)} %bitcast.20), custom_call_target="tpu_custom_call" | custom-call | tf_op jit(solution)/shard_map/pallas_call | solution.py:155
  4.2 12.0 %all-to-all-start = ((s32[32,32,128]{2,1,0:T(8,128)}), s32[32,32,128]{2,1,0:T(8,128)S(1)}, u32[]{:S(2)}, u32[]{:S(2)}) async-start(s32[32,32,128]{2,1,0:T(8,128)} %shard_map.140), calls=%async_computation | async-start | bytes 1048576 | tf_op jit(solution)/shard_map/all_to_all | solution.py:535
  16.2 0.6 copy.32
  16.8 0.0 copy-done.17
  16.9 0.6 copy.31
  17.5 0.0 copy-done.8
  17.5 0.8 copy.23.adj_ref
  18.3 1.4 copy.24.c0_ref.c1_ref.c2_ref
  19.7 3.6 %shard_map.141 = s32[64,8,384]{2,1,0:T(8,128)} custom-call(s32[3]{0:T(128)} %step_ref.1, f32[3,4,81,128]{3,2,1,0:T(8,128)} %copy.23.adj_ref, bf16[8,2,4,81,128]{4,3,2,1,0:T(8,128)(2,1)} %copy.24.c0_ref.c1_ref.c2_ref, bf16[8,2,4,81,128]{4,3,2,1,0:T(8,128)(2,1)} %copy.24.c0_ref.c1_ref.c2_ref, bf16[8,2,4,81,128]{4,3,2,1,0:T(8,128)(2,1)} %copy.24.c0_ref.c1_ref.c2_ref), custom_call_target="tpu_custom_call" | custom-call | tf_op jit(solution)/shard_map/pallas_call | solution.py:196
  23.3 9.2 %all-to-all-done.own_ref = s32[32,32,128]{2,1,0:T(8,128)S(1)} async-done(((s32[32,32,128]{2,1,0:T(8,128)}), s32[32,32,128]{2,1,0:T(8,128)S(1)}, u32[]{:S(2)}, u32[]{:S(2)}) %all-to-all-start) | async-done | bytes 524320 | tf_op jit(solution)/shard_map/all_to_all | solution.py:535
  32.5 7.2 %all-to-all-start.1 = ((s32[64,8,384]{2,1,0:T(8,128)}), s32[64,8,384]{2,1,0:T(8,128)S(1)}, u32[]{:S(2)}, u32[]{:S(2)}) async-start(s32[64,8,384]{2,1,0:T(8,128)} %shard_map.141), calls=%async_computation.1 | async-start | bytes 1572864 | tf_op jit(solution)/shard_map/all_to_all | solution.py:545
  39.7 0.5 collective-permute-start.2
  40.3 2.5 %collective-permute-start.1 = (s32[32,32,128]{2,1,0:T(8,128)S(1)}, s32[32,32,128]{2,1,0:T(8,128)S(1)}, u32[]{:S(2)}, u32[]{:S(2)}) collective-permute-start(s32[32,32,128]{2,1,0:T(8,128)S(1)} %all-to-all-done.own_ref), channel_id=1, source_target_pairs={{0,3},{1,0},{2,1},{3,2},{4,7},{5,4},{6,5},{7,6},{8,11},{9,8},{10,9... | collective-permute-start | bytes 1572872 | tf_op jit(solution)/shard_map/ppermute | solution.py:526
  42.8 0.0 collective-permute-start
  42.8 0.3 convolution_convert_fusion
  43.1 0.0 collective-permute-done.2.own2_ref
  43.1 0.0 copy-done.2
  43.1 0.0 copy-start.7
  43.1 0.8 copy-done.7
  43.9 7.0 %shard_map.142.turned_ref = f32[7424,128]{1,0:T(8,128)} custom-call(s32[32,32,128]{2,1,0:T(8,128)} %copy-done.2, s32[32,32,128]{2,1,0:T(8,128)} %copy-done.7), custom_call_target="tpu_custom_call" | custom-call | tf_op jit(solution)/shard_map/pallas_call | solution.py:249
  50.9 3.1 %collective-permute-done.1.right_ref = s32[32,32,128]{2,1,0:T(8,128)S(1)} collective-permute-done((s32[32,32,128]{2,1,0:T(8,128)S(1)}, s32[32,32,128]{2,1,0:T(8,128)S(1)}, u32[]{:S(2)}, u32[]{:S(2)}) %collective-permute-start.1) | collective-permute-done | bytes 524320 | tf_op jit(solution)/shard_map/ppermute | solution.py:526
  54.1 3.1 %collective-permute-done.left_ref = s32[32,32,128]{2,1,0:T(8,128)S(1)} collective-permute-done((s32[32,32,128]{2,1,0:T(8,128)S(1)}, s32[32,32,128]{2,1,0:T(8,128)S(1)}, u32[]{:S(2)}, u32[]{:S(2)}) %collective-permute-start) | collective-permute-done | bytes 524320 | tf_op jit(solution)/shard_map/ppermute | solution.py:526
  57.2 0.8 slice.12
  57.9 1.2 collective-permute-start.3
  59.1 0.7 slice.13
  59.8 0.0 collective-permute-start.4
  59.8 0.0 collective-permute-start.6
  59.9 1.5 collective-permute-start.5
  61.4 0.9 copy.27.fwd_ref
  62.3 0.6 pad_add_fusion.place_ref
  62.9 0.0 all-to-all-done.1.r_ref
  62.9 0.9 copy-done.1
  63.8 3.4 %shard_map.143 = (f32[2,528,128]{2,1,0:T(8,128)}, f32[2,2,3,88,256]{4,3,2,1,0:T(8,128)}) custom-call(s32[2]{0:T(128)} %pad_add_fusion.place_ref, f32[2,128]{1,0:T(2,128)} %metric_ref.3, s32[64,8,384]{2,1,0:T(8,128)} %copy-done.1, bf16[768,256]{1,0:T(8,128)(2,1)} %copy.27.fwd_ref, bf16[352,88]{1,0:T(8,128)(2,1)} %constant.63.clone.both_ref), custom_call_target="tpu_custom_call" | custom-call | tf_op jit(solution)/shard_map/pallas_call | solution.py:309
  67.2 0.3 collective-permute-done.6.ob_ref
  67.5 0.9 collective-permute-done.5.oa_ref
  68.4 1.7 %collective-permute-start.7 = (s32[16,32,128]{2,1,0:T(8,128)}, s32[16,32,128]{2,1,0:T(8,128)S(1)}, u32[]{:S(2)}, u32[]{:S(2)}) collective-permute-start(s32[16,32,128]{2,1,0:T(8,128)} %collective-permute-done.5.oa_ref), channel_id=1, source_target_pairs={{0,4},{4,0},{8,12},{12,8},{16,20},{20,16},{24,28},{28,24},{32,36},... | collective-permute-start | bytes 786440 | tf_op jit(solution)/shard_map/ppermute | solution.py:531
  70.1 0.0 collective-permute-start.8
  70.1 0.8 pad_maximum_fusion.1.back_ref
  70.9 0.0 collective-permute-done.3.left2_ref
  70.9 0.0 collective-permute-done.4.right2_ref
  70.9 0.9 collective-permute-done.7.oa2_ref
  71.8 0.0 collective-permute-done.8.ob2_ref
  71.8 0.7 copy-done.10
  72.5 0.1 copy-done.11
  72.6 27.8 %shard_map.144 = s32[64,4,384]{2,1,0:T(4,128)} custom-call(s32[2]{0:T(128)} %pad_add_fusion.place_ref, f32[2,128]{1,0:T(2,128)} %metric_ref.3, f32[7424,128]{1,0:T(8,128)} %shard_map.142.turned_ref, s32[32,32,128]{2,1,0:T(8,128)} %copy-done.5, s32[32,32,128]{2,1,0:T(8,128)} %copy-done.6, s32[32,32,128]{2,1,0:T(8,128)} %copy-done.4, ...), custom_call_target="tpu_custom_call" | custom-call | tf_op jit(solution)/shard_map/pallas_call | solution.py:396
  100.4 25.4 %all_to_all.20.r_ref = s32[64,4,384]{2,1,0:T(4,128)} all-to-all(s32[64,4,384]{2,1,0:T(4,128)} %shard_map.144), channel_id=1, replica_groups=mesh['span'=64,'plane'=4] {'span'}, dimensions={0} | all-to-all | bytes 786432 | tf_op jit(solution)/shard_map/all_to_all | solution.py:559
  125.8 3.3 %shard_map.146.p0_ref = f32[4,1024]{1,0:T(4,128)} custom-call(s32[64,4,384]{2,1,0:T(4,128)} %all_to_all.20.r_ref, s32[1,2048]{1,0:T(1,128)} %bitcast.22, s32[1,2048]{1,0:T(1,128)} %bitcast.21), custom_call_target="tpu_custom_call" | custom-call | tf_op jit(solution)/shard_map/pallas_call | solution.py:434
  129.1 0.0 collective-permute-start.11
  129.1 2.0 %collective-permute-start.10 = (f32[4,1024]{1,0:T(4,128)}, f32[4,1024]{1,0:T(4,128)S(1)}, u32[]{:S(2)}, u32[]{:S(2)}) collective-permute-start(f32[4,1024]{1,0:T(4,128)} %shard_map.146.p0_ref), channel_id=1, source_target_pairs={{0,2},{1,3},{2,0},{3,1},{4,6},{5,7},{6,4},{7,5},{8,10},{9,11},{10,... | collective-permute-start | bytes 49160 | tf_op jit(solution)/shard_map/ppermute | solution.py:526
  131.2 0.0 collective-permute-start.9
  131.2 0.8 collective-permute-done.11.p3_ref
  131.9 1.5 collective-permute-done.10.p2_ref
  133.4 1.7 %collective-permute-done.9.p1_ref = f32[4,1024]{1,0:T(4,128)S(1)} collective-permute-done((f32[4,1024]{1,0:T(4,128)}, f32[4,1024]{1,0:T(4,128)S(1)}, u32[]{:S(2)}, u32[]{:S(2)}) %collective-permute-start.9) | collective-permute-done | bytes 16416 | tf_op jit(solution)/shard_map/ppermute | solution.py:526
  135.2 0.6 copy-done.15
  135.8 1.5 shard_map.147
  137.3 7.3 %all-to-all-start.3 = ((f32[64,1,128]{2,1,0:T(1,128)}), f32[64,1,128]{2,1,0:T(1,128)S(1)}, u32[]{:S(2)}, u32[]{:S(2)}) async-start(f32[64,1,128]{2,1,0:T(1,128)} %get-tuple-element.29), calls=%async_computation.3 | async-start | bytes 65536 | tf_op jit(solution)/shard_map/all_to_all | solution.py:564
  144.6 2.2 %shard_map.145 = f32[3,4,81,128]{3,2,1,0:T(8,128)} custom-call(s32[64,4,384]{2,1,0:T(4,128)} %all_to_all.20.r_ref), custom_call_target="tpu_custom_call" | custom-call | tf_op jit(solution)/shard_map/pallas_call | solution.py:495
  146.8 2.0 %copy.29 = f32[3,4,81,128]{3,1,2,0:T(4,128)} copy(f32[3,4,81,128]{3,2,1,0:T(8,128)} %shard_map.145) | data formatting | bytes 995328
  148.7 5.3 %all-to-all-done.3.squares_ref = f32[64,1,128]{2,1,0:T(1,128)S(1)} async-done(((f32[64,1,128]{2,1,0:T(1,128)}), f32[64,1,128]{2,1,0:T(1,128)S(1)}, u32[]{:S(2)}, u32[]{:S(2)}) %all-to-all-start.3) | async-done | bytes 32800 | tf_op jit(solution)/shard_map/all_to_all | solution.py:564
  154.0 0.6 copy-done.12
  154.6 1.5 shard_map.148
  (37 shorter events, 0.2 us)
Async XLA Ops:
  0.6 0.9 copy-start
  0.6 15.6 %copy-start.16 = (s32[1024,2]{0,1:T(2,128)S(1)}, s32[1024,2]{0,1:T(2,128)}, u32[]{:S(2)}) copy-start(s32[1024,2]{0,1:T(2,128)} %param.18) | copy-start | bytes 24580
  0.7 16.2 %copy-start.17 = (s32[1024,2]{0,1:T(2,128)S(1)}, s32[1024,2]{0,1:T(2,128)}, u32[]{:S(2)}) copy-start(s32[1024,2]{0,1:T(2,128)} %param.19) | copy-start | bytes 24580
  0.7 16.8 %copy-start.8 = (f32[3,4,81,128]{3,1,2,0:T(4,128)S(1)}, f32[3,4,81,128]{3,1,2,0:T(4,128)}, u32[]{:S(2)}) copy-start(f32[3,4,81,128]{3,1,2,0:T(4,128)} %param.13) | copy-start | bytes 1492996
  0.7 17.6 %copy-start.3 = (bf16[8,2,4,81,128]{4,2,3,1,0:T(4,128)(2,1)S(1)}, bf16[8,2,4,81,128]{4,2,3,1,0:T(4,128)(2,1)}, u32[]{:S(2)}) copy-start(bf16[8,2,4,81,128]{4,2,3,1,0:T(4,128)(2,1)} %param.14) | copy-start | bytes 3981316
  4.2 28.3 %all-to-all-start = ((s32[32,32,128]{2,1,0:T(8,128)}), s32[32,32,128]{2,1,0:T(8,128)S(1)}, u32[]{:S(2)}, u32[]{:S(2)}) async-start(s32[32,32,128]{2,1,0:T(8,128)} %shard_map.140), calls=%async_computation | async-start | bytes 1048576 | tf_op jit(solution)/shard_map/all_to_all | solution.py:535
  23.3 19.5 %copy-start.18 = (s32[256]{0:T(256)S(1)}, s32[256]{0:T(256)}, u32[]{:S(2)}) copy-start(s32[256]{0:T(256)} %constant.71) | copy-start | bytes 3076
  23.3 19.5 %copy-start.19 = (s32[256]{0:T(256)S(1)}, s32[256]{0:T(256)}, u32[]{:S(2)}) copy-start(s32[256]{0:T(256)} %constant.69) | copy-start | bytes 3076
  23.3 19.5 %copy-start.20 = (s32[256]{0:T(256)S(1)}, s32[256]{0:T(256)}, u32[]{:S(2)}) copy-start(s32[256]{0:T(256)} %constant.61.clone) | copy-start | bytes 3076
  23.3 19.6 %copy-start.21 = (bf16[256,512]{1,0:T(8,128)(2,1)S(1)}, bf16[256,512]{1,0:T(8,128)(2,1)}, u32[]{:S(2)}) copy-start(bf16[256,512]{1,0:T(8,128)(2,1)} %constant.62.clone) | copy-start | bytes 786436
  32.5 10.6 %copy-start.2 = (s32[32,32,128]{2,1,0:T(8,128)}, s32[32,32,128]{2,1,0:T(8,128)S(1)}, u32[]{:S(2)}) copy-start(s32[32,32,128]{2,1,0:T(8,128)S(1)} %all-to-all-done.own_ref) | copy-start | bytes 1572868
  32.5 30.4 %all-to-all-start.1 = ((s32[64,8,384]{2,1,0:T(8,128)}), s32[64,8,384]{2,1,0:T(8,128)S(1)}, u32[]{:S(2)}, u32[]{:S(2)}) async-start(s32[64,8,384]{2,1,0:T(8,128)} %shard_map.141), calls=%async_computation.1 | async-start | bytes 1572864 | tf_op jit(solution)/shard_map/all_to_all | solution.py:545
  39.7 3.4 %collective-permute-start.2 = (s32[32,32,128]{2,1,0:T(8,128)S(1)}, s32[32,32,128]{2,1,0:T(8,128)S(1)}, u32[]{:S(2)}, u32[]{:S(2)}) collective-permute-start(s32[32,32,128]{2,1,0:T(8,128)S(1)} %all-to-all-done.own_ref), channel_id=1, source_target_pairs={{0,4},{4,0},{8,12},{12,8},{16,20},{20,16},{24,28},{28,24},{32,36},... | collective-permute-start | bytes 1572872 | tf_op jit(solution)/shard_map/ppermute | solution.py:531
  40.3 13.8 %collective-permute-start.1 = (s32[32,32,128]{2,1,0:T(8,128)S(1)}, s32[32,32,128]{2,1,0:T(8,128)S(1)}, u32[]{:S(2)}, u32[]{:S(2)}) collective-permute-start(s32[32,32,128]{2,1,0:T(8,128)S(1)} %all-to-all-done.own_ref), channel_id=1, source_target_pairs={{0,3},{1,0},{2,1},{3,2},{4,7},{5,4},{6,5},{7,6},{8,11},{9,8},{10,9... | collective-permute-start | bytes 1572872 | tf_op jit(solution)/shard_map/ppermute | solution.py:526
  42.8 14.4 %collective-permute-start = (s32[32,32,128]{2,1,0:T(8,128)S(1)}, s32[32,32,128]{2,1,0:T(8,128)S(1)}, u32[]{:S(2)}, u32[]{:S(2)}) collective-permute-start(s32[32,32,128]{2,1,0:T(8,128)S(1)} %all-to-all-done.own_ref), channel_id=1, source_target_pairs={{0,1},{1,2},{2,3},{3,0},{4,5},{5,6},{6,7},{7,4},{8,9},{9,10},{10,1... | collective-permute-start | bytes 1572872 | tf_op jit(solution)/shard_map/ppermute | solution.py:526
  43.1 0.8 copy-start.7
  54.1 8.3 %copy-start.4 = (s32[32,32,128]{2,1,0:T(8,128)}, s32[32,32,128]{2,1,0:T(8,128)S(1)}, u32[]{:S(2)}) copy-start(s32[32,32,128]{2,1,0:T(8,128)S(1)} %collective-permute-done.1.right_ref) | copy-start | bytes 1572868
  57.1 5.2 %copy-start.5 = (s32[32,32,128]{2,1,0:T(8,128)}, s32[32,32,128]{2,1,0:T(8,128)S(1)}, u32[]{:S(2)}) copy-start(s32[32,32,128]{2,1,0:T(8,128)S(1)} %collective-permute-done.left_ref) | copy-start | bytes 1572868
  57.9 13.0 %collective-permute-start.3 = (s32[32,32,128]{2,1,0:T(8,128)S(1)}, s32[32,32,128]{2,1,0:T(8,128)S(1)}, u32[]{:S(2)}, u32[]{:S(2)}) collective-permute-start(s32[32,32,128]{2,1,0:T(8,128)S(1)} %collective-permute-done.left_ref), channel_id=1, source_target_pairs={{0,4},{4,0},{8,12},{12,8},{16,20},{20,16},{24,28},{28,24},{32,36},... | collective-permute-start | bytes 1572872 | tf_op jit(solution)/shard_map/ppermute | solution.py:531
  59.8 11.1 %collective-permute-start.4 = (s32[32,32,128]{2,1,0:T(8,128)S(1)}, s32[32,32,128]{2,1,0:T(8,128)}, u32[]{:S(2)}, u32[]{:S(2)}) collective-permute-start(s32[32,32,128]{2,1,0:T(8,128)S(1)} %collective-permute-done.1.right_ref), channel_id=1, source_target_pairs={{0,4},{4,0},{8,12},{12,8},{16,20},{20,16},{24,28},{28,24},{32,36},... | collective-permute-start | bytes 1572872 | tf_op jit(solution)/shard_map/ppermute | solution.py:531
  59.8 7.7 %collective-permute-start.6 = (s32[16,32,128]{2,1,0:T(8,128)}, s32[16,32,128]{2,1,0:T(8,128)S(1)}, u32[]{:S(2)}, u32[]{:S(2)}) collective-permute-start(s32[16,32,128]{2,1,0:T(8,128)} %slice.13), channel_id=1, source_target_pairs={{0,3},{1,0},{2,1},{3,2},{4,7},{5,4},{6,5},{7,6},{8,11},{9,8},{10,9... | collective-permute-start | bytes 786440 | tf_op jit(solution)/shard_map/ppermute | solution.py:526
  59.9 8.6 %collective-permute-start.5 = (s32[16,32,128]{2,1,0:T(8,128)}, s32[16,32,128]{2,1,0:T(8,128)}, u32[]{:S(2)}, u32[]{:S(2)}) collective-permute-start(s32[16,32,128]{2,1,0:T(8,128)} %slice.12), channel_id=1, source_target_pairs={{0,1},{1,2},{2,3},{3,0},{4,5},{5,6},{6,7},{7,4},{8,9},{9,10},{10,1... | collective-permute-start | bytes 786440 | tf_op jit(solution)/shard_map/ppermute | solution.py:526
  62.9 0.9 copy-start.1
  67.5 4.3 %copy-start.9 = (s32[16,32,128]{2,1,0:T(8,128)}, s32[16,32,128]{2,1,0:T(8,128)S(1)}, u32[]{:S(2)}) copy-start(s32[16,32,128]{2,1,0:T(8,128)S(1)} %collective-permute-done.6.ob_ref) | copy-start | bytes 786436
  68.4 3.4 %collective-permute-start.7 = (s32[16,32,128]{2,1,0:T(8,128)}, s32[16,32,128]{2,1,0:T(8,128)S(1)}, u32[]{:S(2)}, u32[]{:S(2)}) collective-permute-start(s32[16,32,128]{2,1,0:T(8,128)} %collective-permute-done.5.oa_ref), channel_id=1, source_target_pairs={{0,4},{4,0},{8,12},{12,8},{16,20},{20,16},{24,28},{28,24},{32,36},... | collective-permute-start | bytes 786440 | tf_op jit(solution)/shard_map/ppermute | solution.py:531
  70.1 1.7 %collective-permute-start.8 = (s32[16,32,128]{2,1,0:T(8,128)S(1)}, s32[16,32,128]{2,1,0:T(8,128)S(1)}, u32[]{:S(2)}, u32[]{:S(2)}) collective-permute-start(s32[16,32,128]{2,1,0:T(8,128)S(1)} %collective-permute-done.6.ob_ref), channel_id=1, source_target_pairs={{0,4},{4,0},{8,12},{12,8},{16,20},{20,16},{24,28},{28,24},{32,36},... | collective-permute-start | bytes 786440 | tf_op jit(solution)/shard_map/ppermute | solution.py:531
  70.9 0.9 copy-start.6
  71.8 0.7 copy-start.10
  71.8 0.8 copy-start.11
  129.1 2.8 %collective-permute-start.11 = (f32[4,1024]{1,0:T(4,128)}, f32[4,1024]{1,0:T(4,128)S(1)}, u32[]{:S(2)}, u32[]{:S(2)}) collective-permute-start(f32[4,1024]{1,0:T(4,128)} %shard_map.146.p0_ref), channel_id=1, source_target_pairs={{0,3},{1,0},{2,1},{3,2},{4,7},{5,4},{6,5},{7,6},{8,11},{9,8},{10,9... | collective-permute-start | bytes 49160 | tf_op jit(solution)/shard_map/ppermute | solution.py:526
  129.1 4.3 %collective-permute-start.10 = (f32[4,1024]{1,0:T(4,128)}, f32[4,1024]{1,0:T(4,128)S(1)}, u32[]{:S(2)}, u32[]{:S(2)}) collective-permute-start(f32[4,1024]{1,0:T(4,128)} %shard_map.146.p0_ref), channel_id=1, source_target_pairs={{0,2},{1,3},{2,0},{3,1},{4,6},{5,7},{6,4},{7,5},{8,10},{9,11},{10,... | collective-permute-start | bytes 49160 | tf_op jit(solution)/shard_map/ppermute | solution.py:526
  131.2 4.0 %collective-permute-start.9 = (f32[4,1024]{1,0:T(4,128)}, f32[4,1024]{1,0:T(4,128)S(1)}, u32[]{:S(2)}, u32[]{:S(2)}) collective-permute-start(f32[4,1024]{1,0:T(4,128)} %shard_map.146.p0_ref), channel_id=1, source_target_pairs={{0,1},{1,2},{2,3},{3,0},{4,5},{5,6},{6,7},{7,4},{8,9},{9,10},{10,1... | collective-permute-start | bytes 49160 | tf_op jit(solution)/shard_map/ppermute | solution.py:526
  131.9 3.3 %copy-start.13 = (f32[4,1024]{1,0:T(4,128)}, f32[4,1024]{1,0:T(4,128)S(1)}, u32[]{:S(2)}) copy-start(f32[4,1024]{1,0:T(4,128)S(1)} %collective-permute-done.11.p3_ref) | copy-start | bytes 49156
  133.4 1.8 %copy-start.14 = (f32[4,1024]{1,0:T(4,128)}, f32[4,1024]{1,0:T(4,128)S(1)}, u32[]{:S(2)}) copy-start(f32[4,1024]{1,0:T(4,128)S(1)} %collective-permute-done.10.p2_ref) | copy-start | bytes 49156
  135.2 0.6 copy-start.15
  137.3 16.7 %all-to-all-start.3 = ((f32[64,1,128]{2,1,0:T(1,128)}), f32[64,1,128]{2,1,0:T(1,128)S(1)}, u32[]{:S(2)}, u32[]{:S(2)}) async-start(f32[64,1,128]{2,1,0:T(1,128)} %get-tuple-element.29), calls=%async_computation.3 | async-start | bytes 65536 | tf_op jit(solution)/shard_map/all_to_all | solution.py:564
  154.0 0.6 copy-start.12

commit v4 on v3

--- a/solution.py
+++ b/solution.py
@@ -17,7 +17,7 @@
 VMEM_BYTES = 56 * 1024 * 1024
 LEVELS = 32767.0
 SCALE_LANE = 250
-LINES = 58
+LINES = 56
 
 
 def chebyshev_matrix(degree):
@@ -47,9 +47,9 @@
 def lane_order():
     chips = np.arange(32)
     pieces = []
-    for part, shift in ((chips, 0), (chips, 3), (chips, 1), (chips[:16], 2), (chips[16:], 2)):
+    for shift in (0, 3, 1, 2):
         for core in range(2):
-            pieces.append((part, np.full(part.shape, core), np.full(part.shape, shift)))
+            pieces.append((chips, np.full(chips.shape, core), np.full(chips.shape, shift)))
     return [np.concatenate([p[k] for p in pieces]).astype(np.int32) for k in range(3)]
 
 
@@ -129,10 +129,10 @@
     lower = code - upper * 2.0**15
     w_ref[...] = jnp.zeros_like(w_ref)
     w_ref[0:Q, 0:Q] = jnp.round(h * (LEVELS / (code * 2.0**-30)))
+    turned = w_ref[...].T
+    w_ref[...] = turned
     w_ref[0:Q, Q : Q + 1] = upper
     w_ref[0:Q, Q + 1 : Q + 2] = lower
-    turned = w_ref[...].T
-    w_ref[...] = turned
     f_ref[...] = jnp.zeros_like(f_ref)
     for k in range(16):
         line, lane = divmod(k * QP, 128)
@@ -143,12 +143,11 @@
         place = lax.broadcasted_iota(jnp.int32, (count, 128), 1)
         here = pl.ds(line, count, stride=11)
         f_ref[here, :] = f_ref[here, :] + jnp.where(place >= lane, block, 0.0)
-        if lane + Q > 128:
+        if lane + QP > 128:
             after = pl.ds(line + 1, count, stride=11)
             f_ref[after, :] = f_ref[after, :] + jnp.where(place < lane, block, 0.0)
-    f_ref[56, 0:Q] = w_ref[Q, 0:Q]
-    f_ref[57, 0:Q] = w_ref[Q + 1, 0:Q]
-    o_ref[...] = jnp.broadcast_to(pair_up(f_ref[0:32, :], f_ref[32:64, :])[None], o_ref.shape)
+    pair = pair_up(f_ref[0:32, :], f_ref[LINES // 2 : LINES // 2 + 32, :])
+    o_ref[...] = jnp.broadcast_to(pair[None], o_ref.shape)
 
 
 def pack_inverse(matrix, targets):
@@ -160,6 +159,22 @@
         scratch_shapes=[pltpu.VMEM((128, 128), F32), pltpu.VMEM((64, 128), F32)],
         compiler_params=params(),
     )(matrix)
+
+
+def turn_kernel(own_ref, o_ref):
+    for g in range(LINES // 8):
+        lines = [own_ref[:, 4 * g + b, :] for b in range(4)]
+        o_ref[g * 128 : (g + 1) * 128, :] = jnp.concatenate(lines, axis=0).T
+
+
+def turn_own(own):
+    return pl.pallas_call(
+        turn_kernel,
+        out_shape=jax.ShapeDtypeStruct((LINES // 8 * 128, 128), jnp.int32),
+        in_specs=[vmem_spec()],
+        out_specs=vmem_spec(),
+        compiler_params=params(),
+    )(own)
 
 
 def pack_points_kernel(step_ref, adj_ref, c0_ref, c1_ref, c2_ref, o_ref, t_ref):
@@ -219,40 +234,35 @@
     )
 
 
-def turn_pieces(pieces, write):
-    def lines(k, both):
-        pair = jnp.concatenate([ref[:, k, :] for ref in pieces], axis=0).T
-        write(pl.multiple_of(k * 128, 128), low_of(pair))
-        if both:
-            write(pl.multiple_of(k * 128 + 4096, 128), high_of(pair))
-
-    def both_halves(k, carry):
-        lines(k, True)
+def regroup(blocks):
+    lane = lax.broadcasted_iota(jnp.int32, blocks[0].shape, 1)
+
+    def exchange(a, b, keep, width):
+        return jnp.where(keep, a, pltpu.roll(b, width, 1)), jnp.where(
+            keep, pltpu.roll(a, 128 - width, 1), b
+        )
+
+    low = lane < 64
+    p0, p2 = exchange(blocks[0], blocks[2], low, 64)
+    p1, p3 = exchange(blocks[1], blocks[3], low, 64)
+    even = (lane & 32) == 0
+    p0, p1 = exchange(p0, p1, even, 32)
+    p2, p3 = exchange(p2, p3, even, 32)
+    return p0, p1, p2, p3
+
+
+def spread_pieces(pieces, first, last, ht, half):
+    def rows(k, carry):
+        blocks = regroup([ref[pl.ds(pl.multiple_of((k - f) * 32, 32), 32), :] for ref, f in pieces])
+        start = (k >> 2) * 512 + (k & 3) * 32
+        for b in range(4):
+            row = pl.multiple_of(start + b * 128, 32)
+            ht[half, pl.ds(row, 32), :] = low_of(blocks[b])
+            row = pl.multiple_of(start + b * 128 + LINES * 64, 32)
+            ht[half, pl.ds(row, 32), :] = high_of(blocks[b])
         return carry
 
-    def low_half(k, carry):
-        lines(k, False)
-        return carry
-
-    lax.fori_loop(0, LINES - 32, both_halves, 0)
-    lax.fori_loop(LINES - 32, 32, low_half, 0)
-
-
-def turn_kernel(own_ref, own2_ref, o_ref):
-    def write(row, block):
-        o_ref[pl.ds(row, 128), 0:64] = block
-
-    turn_pieces((own_ref, own2_ref), write)
-
-
-def turn_own(own, own2):
-    return pl.pallas_call(
-        turn_kernel,
-        out_shape=jax.ShapeDtypeStruct((LINES * 128, 128), F32),
-        in_specs=[vmem_spec()] * 2,
-        out_specs=vmem_spec(),
-        compiler_params=params(),
-    )(own, own2)
+    lax.fori_loop(first, last, rows, 0, unroll=2)
 
 
 def advance(place_ref, metric_ref, x, v, step, both_ref, fwd_ref, coef):
@@ -320,27 +330,21 @@
 
 
 def steps_kernel(
-    place_ref, metric_ref, turned_ref, left_ref, left2_ref, right_ref, right2_ref, oa_ref, oa2_ref, ob_ref, ob2_ref,
+    place_ref, metric_ref, own_ref, own2_ref, left_ref, left2_ref, right_ref, right2_ref, oa_ref, oa2_ref, ob_ref, ob2_ref,
     first_ref, v, fwd_ref, back_ref, both_ref,
     out_ref,
-    ht, rows, x, coef, solved, wall, turn, sem,
+    ht, rows, x, coef, solved, wall, turn,
 ):
-    load = pltpu.make_async_copy(turned_ref, ht.at[0], sem)
-    load.start()
-
-    def write(row, block):
-        ht[1, pl.ds(row, 128), :] = block
-
-    turn_pieces((right_ref, right2_ref, oa_ref, oa2_ref, ob_ref, ob2_ref), write)
-    load.wait()
-
-    def write_left(row, block):
-        ht[0, pl.ds(row, 128), 64:128] = block
-
-    turn_pieces((left_ref, left2_ref), write_left)
+    spread_pieces([(r, 0) for r in (own_ref, own2_ref, left_ref, left2_ref)], 0, 28, ht, 0)
+    for first, last, oref, oref2 in ((0, 14, oa_ref, oa2_ref), (14, 28, ob_ref, ob2_ref)):
+        spread_pieces(
+            [(right_ref, 0), (right2_ref, 0), (oref, first), (oref2, first)], first, last, ht, 1
+        )
     for half in range(2):
-        rows[half] = (
-            ht[half, 7168 : 7168 + QP, :] * 2.0**15 + ht[half, 7296 : 7296 + QP, :]
+        rows[half] = jnp.zeros((QP, 128), F32)
+        rows[half, 0:Q, :] = (
+            ht[half, pl.ds(Q, Q, stride=QP), :] * 2.0**15
+            + ht[half, pl.ds(Q + 1, Q, stride=QP), :]
         ) * (2.0**-30 / LEVELS)
 
     for step in range(NSTEP):
@@ -392,12 +396,11 @@
         out_ref[:, z, 0:256] = turned[z * 64 : (z + 1) * 64, :]
 
 
-def steps(place, metric, turned, pieces, first, velocity, fwd, back, both):
+def steps(place, metric, pieces, first, velocity, fwd, back, both):
     return pl.pallas_call(
         steps_kernel,
         out_shape=jax.ShapeDtypeStruct((64, 4, 384), jnp.int32),
-        in_specs=[smem_spec(), smem_spec(), pl.BlockSpec(memory_space=pl.ANY)]
-        + [vmem_spec()] * (len(pieces) + 5),
+        in_specs=[smem_spec(), smem_spec()] + [vmem_spec()] * (len(pieces) + 5),
         out_specs=vmem_spec(),
         scratch_shapes=[
             pltpu.VMEM((2, LINES * 128, 128), F32),
@@ -407,10 +410,9 @@
             pltpu.VMEM((6, QP, 256), F32),
             pltpu.VMEM((2, QP, 256), F32),
             pltpu.VMEM((256, 256), jnp.int32),
-            pltpu.SemaphoreType.DMA,
         ],
         compiler_params=params(),
-    )(place, metric, turned, *pieces, first, velocity, fwd, back, both)
+    )(place, metric, *pieces, first, velocity, fwd, back, both)
 
 
 def wall_kernel(r_ref, local_ref, element_ref, o_ref):
@@ -539,23 +541,21 @@
     element = wall_element.T.reshape(1, 2 * wall_count) - plane * adjoint.shape[3]
     sent = pack_points(adjoint, checkpoints, checkpoint_step)
     own, sent, local, element = lax.optimization_barrier((own, sent, local, element))
-    own2 = across(own)
+    own = turn_own(own)
     left = around(own, 1)
     right = around(own, 3)
     points = lax.all_to_all(sent, "span", 0, 0, tiled=True)
-    turned = turn_own(own, own2)
-    left, right, turned = lax.optimization_barrier((left, right, turned))
-    oa = around(left[:16], 1)
-    ob = around(right[16:], 3)
+    oa = around(left[:448], 1)
+    ob = around(right[448:], 3)
     both = slope_table()
     first, velocity = first_modes(place, metric, points, fwd, both)
     pieces = []
-    for piece in (left, right):
+    for piece in (own, left, right):
         pieces += [piece, across(piece)]
     oa, ob, first = lax.optimization_barrier((oa, ob, first))
     for piece in (oa, ob):
         pieces += [piece, across(piece)]
-    out = steps(place, metric, turned, pieces, first, velocity, fwd, back, both)
+    out = steps(place, metric, pieces, first, velocity, fwd, back, both)
     received = lax.all_to_all(out, "span", 0, 0, tiled=True)
 
     partial_sum = wall_sums(received, local, element)

time: 157 us -> 149 us (0.949)
  Pallas kernels: 52.2 us -> 41.4 us
  starting transfers between devices: 36 us -> 38.2 us
    pallas_call x1, Pallas kernels: 27.8 us -> 21.8 us  [steps(): pl.pallas_call(steps_kernel, out_shape=jax.ShapeDtypeStruct((64, 4, 384),...]
    pallas_call x1, Pallas kernels: 6.99 us -> 2.12 us  [turn_own(): pl.pallas_call(turn_kernel, out_shape=jax.ShapeDtypeStruct((LINES // 8 *...]
    ppermute x7, starting transfers between devices: 6 us -> 7.86 us  [around(): lax.ppermute(block, 'plane', [(i, (i + step) % plane_count) for i in rang...]
    unnamed x50 -> x48, local copies, waits for them, and re-layouts: 10.6 us -> 10.4 us
  transfers between devices with their start and end apart: 15 -> 15, of which waited for: 10 -> 8; matrix products, arithmetic and copies ran while one was open for 6% -> 6% of each run, Pallas kernels for 10% -> 8%
where the time goes in v4:
time: 149 us
  Pallas kernels  41.4 us (28%)
  starting transfers between devices  38.2 us (26%)
  waiting for transfers between devices  28 us (19%)
  blocking collectives  25.5 us (17%)
  local copies, waits for them, and re-layouts  12.9 us (9%)
  other arithmetic  1.49 us (1%)
    all_to_all x1, blocking collectives, on_device(): received = lax.all_to_all(out, 'span', 0, 0, tiled=True)  25.5 us
    pallas_call x1, Pallas kernels, steps(): pl.pallas_call(steps_kernel, out_shape=jax.ShapeDtypeStruct((64, 4, 384),...  21.8 us
    ppermute x7, waiting for transfers between devices, around(): lax.ppermute(block, 'plane', [(i, (i + step) % plane_count) for i in rang...  12.3 us
    all_to_all x1, starting transfers between devices, on_device(): lax.all_to_all(pack_inverse(matrix, span_count // 2), 'span', 0, 0, tiled...  12 us
    unnamed x48, local copies, waits for them, and re-layouts  10.4 us
    all_to_all x1, waiting for transfers between devices, on_device(): lax.all_to_all(pack_inverse(matrix, span_count // 2), 'span', 0, 0, tiled...  9.23 us
    ppermute x7, starting transfers between devices, around(): lax.ppermute(block, 'plane', [(i, (i + step) % plane_count) for i in rang...  7.86 us
    all_to_all x1, starting transfers between devices, on_device(): points = lax.all_to_all(sent, 'span', 0, 0, tiled=True)  7.24 us
  transfers between devices with their start and end apart: 15, of which 8 were waited for; matrix products, arithmetic and copies ran while one was open for 6% of the time, Pallas kernels for 8%

profile of v4, /device:TPU:1, one launch (start us, length us, event | category | flops | bytes accessed | tf_op | source)
XLA Modules:
  0.0 148.7 jit_solution(5153022728811907081)
XLA Ops:
  0.6 0.0 copy-start
  0.7 0.9 copy-done
  1.6 0.6 copy.34
  2.2 2.1 %shard_map.140 = s32[32,32,128]{2,1,0:T(8,128)} custom-call(f32[81,81]{1,0:T(8,128)} %bitcast.20), custom_call_target="tpu_custom_call" | custom-call | tf_op jit(solution)/shard_map/pallas_call | solution.py:154
  4.3 12.0 %all-to-all-start = ((s32[32,32,128]{2,1,0:T(8,128)}), s32[32,32,128]{2,1,0:T(8,128)S(1)}, u32[]{:S(2)}, u32[]{:S(2)}) async-start(s32[32,32,128]{2,1,0:T(8,128)} %shard_map.140), calls=%async_computation | async-start | bytes 1048576 | tf_op jit(solution)/shard_map/all_to_all | solution.py:537
  16.3 0.6 copy.32
  16.9 0.6 copy.31
  17.6 0.8 copy.23.adj_ref
  18.4 0.0 copy-done.4
  18.4 1.4 copy.24.c0_ref.c1_ref.c2_ref
  19.8 3.6 %shard_map.141 = s32[64,8,384]{2,1,0:T(8,128)} custom-call(s32[3]{0:T(128)} %step_ref.1, f32[3,4,81,128]{3,2,1,0:T(8,128)} %copy.23.adj_ref, bf16[8,2,4,81,128]{4,3,2,1,0:T(8,128)(2,1)} %copy.24.c0_ref.c1_ref.c2_ref, bf16[8,2,4,81,128]{4,3,2,1,0:T(8,128)(2,1)} %copy.24.c0_ref.c1_ref.c2_ref, bf16[8,2,4,81,128]{4,3,2,1,0:T(8,128)(2,1)} %copy.24.c0_ref.c1_ref.c2_ref), custom_call_target="tpu_custom_call" | custom-call | tf_op jit(solution)/shard_map/pallas_call | solution.py:211
  23.4 9.2 %all-to-all-done.own_ref = s32[32,32,128]{2,1,0:T(8,128)S(1)} async-done(((s32[32,32,128]{2,1,0:T(8,128)}), s32[32,32,128]{2,1,0:T(8,128)S(1)}, u32[]{:S(2)}, u32[]{:S(2)}) %all-to-all-start) | async-done | bytes 524320 | tf_op jit(solution)/shard_map/all_to_all | solution.py:537
  32.6 7.2 %all-to-all-start.1 = ((s32[64,8,384]{2,1,0:T(8,128)}), s32[64,8,384]{2,1,0:T(8,128)S(1)}, u32[]{:S(2)}, u32[]{:S(2)}) async-start(s32[64,8,384]{2,1,0:T(8,128)} %shard_map.141), calls=%async_computation.1 | async-start | bytes 1572864 | tf_op jit(solution)/shard_map/all_to_all | solution.py:547
  39.9 0.0 copy-done.2
  39.9 2.1 %shard_map.142.own_ref = s32[896,128]{1,0:T(8,128)} custom-call(s32[32,32,128]{2,1,0:T(8,128)} %copy-done.2), custom_call_target="tpu_custom_call" | custom-call | tf_op jit(solution)/shard_map/pallas_call | solution.py:171
  42.0 2.5 %collective-permute-start.3 = (s32[896,128]{1,0:T(8,128)}, s32[896,128]{1,0:T(8,128)S(1)}, u32[]{:S(2)}, u32[]{:S(2)}) collective-permute-start(s32[896,128]{1,0:T(8,128)} %shard_map.142.own_ref), channel_id=1, source_target_pairs={{0,3},{1,0},{2,1},{3,2},{4,7},{5,4},{6,5},{7,6},{8,11},{9,8},{10,9... | collective-permute-start | bytes 1376264 | tf_op jit(solution)/shard_map/ppermute | solution.py:528
  44.5 0.0 collective-permute-start.1
  44.5 0.3 convolution_convert_fusion
  44.8 0.8 collective-permute-start
  45.7 8.6 %collective-permute-done.3.right_ref = s32[896,128]{1,0:T(8,128)S(1)} collective-permute-done((s32[896,128]{1,0:T(8,128)}, s32[896,128]{1,0:T(8,128)S(1)}, u32[]{:S(2)}, u32[]{:S(2)}) %collective-permute-start.3) | collective-permute-done | bytes 458784 | tf_op jit(solution)/shard_map/ppermute | solution.py:528
  54.3 0.8 slice.17
  55.0 3.3 %collective-permute-start.6 = (s32[448,128]{1,0:T(8,128)}, s32[448,128]{1,0:T(8,128)}, u32[]{:S(2)}, u32[]{:S(2)}) collective-permute-start(s32[448,128]{1,0:T(8,128)} %slice.17), channel_id=1, source_target_pairs={{0,3},{1,0},{2,1},{3,2},{4,7},{5,4},{6,5},{7,6},{8,11},{9,8},{10,9... | collective-permute-start | bytes 688136 | tf_op jit(solution)/shard_map/ppermute | solution.py:528
  58.3 0.0 collective-permute-done.1.left_ref
  58.3 0.8 slice.16
  59.1 0.0 collective-permute-start.5
  59.1 1.6 %collective-permute-start.4 = (s32[896,128]{1,0:T(8,128)S(1)}, s32[896,128]{1,0:T(8,128)}, u32[]{:S(2)}, u32[]{:S(2)}) collective-permute-start(s32[896,128]{1,0:T(8,128)S(1)} %collective-permute-done.3.right_ref), channel_id=1, source_target_pairs={{0,4},{4,0},{8,12},{12,8},{16,20},{20,16},{24,28},{28,24},{32,36},... | collective-permute-start | bytes 1376264 | tf_op jit(solution)/shard_map/ppermute | solution.py:533
  60.7 0.0 collective-permute-start.2
  60.7 0.9 copy.27.fwd_ref
  61.7 0.7 pad_add_fusion.place_ref
  62.3 0.3 all-to-all-done.1.r_ref
  62.6 0.9 copy-done.1
  63.5 3.4 %shard_map.143 = (f32[2,528,128]{2,1,0:T(8,128)}, f32[2,2,3,88,256]{4,3,2,1,0:T(8,128)}) custom-call(s32[2]{0:T(128)} %pad_add_fusion.place_ref, f32[2,128]{1,0:T(2,128)} %metric_ref.3, s32[64,8,384]{2,1,0:T(8,128)} %copy-done.1, bf16[768,256]{1,0:T(8,128)(2,1)} %copy.27.fwd_ref, bf16[352,88]{1,0:T(8,128)(2,1)} %constant.63.clone.both_ref), custom_call_target="tpu_custom_call" | custom-call | tf_op jit(solution)/shard_map/pallas_call | solution.py:319
  66.9 0.0 collective-permute-done.6.ob_ref
  67.0 0.0 collective-permute-done.5.oa_ref
  67.0 1.7 %collective-permute-start.7 = (s32[448,128]{1,0:T(8,128)}, s32[448,128]{1,0:T(8,128)S(1)}, u32[]{:S(2)}, u32[]{:S(2)}) collective-permute-start(s32[448,128]{1,0:T(8,128)} %collective-permute-done.5.oa_ref), channel_id=1, source_target_pairs={{0,4},{4,0},{8,12},{12,8},{16,20},{20,16},{24,28},{28,24},{32,36},... | collective-permute-start | bytes 688136 | tf_op jit(solution)/shard_map/ppermute | solution.py:533
  68.7 0.0 collective-permute-start.8
  68.7 0.8 pad_maximum_fusion.1.back_ref
  69.4 0.0 collective-permute-done.own2_ref
  69.5 0.0 collective-permute-done.4.right2_ref
  69.5 0.0 collective-permute-done.2.left2_ref
  69.5 0.5 collective-permute-done.7.oa2_ref
  70.0 0.4 collective-permute-done.8.ob2_ref
  70.4 0.0 copy-done.8
  70.4 0.3 copy-done.9
  70.7 0.4 copy-done.10
  71.1 21.8 %shard_map.144 = s32[64,4,384]{2,1,0:T(4,128)} custom-call(s32[2]{0:T(128)} %pad_add_fusion.place_ref, f32[2,128]{1,0:T(2,128)} %metric_ref.3, s32[896,128]{1,0:T(8,128)} %shard_map.142.own_ref, s32[896,128]{1,0:T(8,128)} %copy-done.8, s32[896,128]{1,0:T(8,128)} %copy-done.6, s32[896,128]{1,0:T(8,128)} %collective-permute-done.2.left2_ref, ...), custom_call_target="tpu_custom_call" | custom-call | tf_op jit(solution)/shard_map/pallas_call | solution.py:400
  92.8 25.5 %all_to_all.20.r_ref = s32[64,4,384]{2,1,0:T(4,128)} all-to-all(s32[64,4,384]{2,1,0:T(4,128)} %shard_map.144), channel_id=1, replica_groups=mesh['span'=64,'plane'=4] {'span'}, dimensions={0} | all-to-all | bytes 786432 | tf_op jit(solution)/shard_map/all_to_all | solution.py:559
  118.4 3.3 %shard_map.146.p0_ref = f32[4,1024]{1,0:T(4,128)} custom-call(s32[64,4,384]{2,1,0:T(4,128)} %all_to_all.20.r_ref, s32[1,2048]{1,0:T(1,128)} %bitcast.22, s32[1,2048]{1,0:T(1,128)} %bitcast.21), custom_call_target="tpu_custom_call" | custom-call | tf_op jit(solution)/shard_map/pallas_call | solution.py:436
  121.7 1.5 collective-permute-start.11
  123.2 0.0 collective-permute-start.10
  123.2 0.6 collective-permute-start.9
  123.8 0.7 collective-permute-done.11.p3_ref
  124.5 3.0 %collective-permute-done.10.p2_ref = f32[4,1024]{1,0:T(4,128)S(1)} collective-permute-done((f32[4,1024]{1,0:T(4,128)}, f32[4,1024]{1,0:T(4,128)S(1)}, u32[]{:S(2)}, u32[]{:S(2)}) %collective-permute-start.10) | collective-permute-done | bytes 16416 | tf_op jit(solution)/shard_map/ppermute | solution.py:528
  127.5 0.0 collective-permute-done.9.p1_ref
  127.5 0.0 copy-done.12
  127.5 0.6 copy-done.13
  128.1 0.6 copy-done.14
  128.7 1.5 %shard_map.147 = (f32[4,1024]{1,0:T(4,128)}, f32[64,1,128]{2,1,0:T(1,128)}) custom-call(f32[4,1024]{1,0:T(4,128)} %weight_ref.1, f32[4,1024]{1,0:T(4,128)} %shard_map.146.p0_ref, f32[4,1024]{1,0:T(4,128)} %copy-done.14, f32[4,1024]{1,0:T(4,128)} %copy-done.13, f32[4,1024]{1,0:T(4,128)} %copy-done.12), custom_call_target="tpu_custom_call" | custom-call | tf_op jit(solution)/shard_map/pallas_call | solution.py:458
  130.2 7.0 %all-to-all-start.3 = ((f32[64,1,128]{2,1,0:T(1,128)}), f32[64,1,128]{2,1,0:T(1,128)S(1)}, u32[]{:S(2)}, u32[]{:S(2)}) async-start(f32[64,1,128]{2,1,0:T(1,128)} %get-tuple-element.23), calls=%async_computation.3 | async-start | bytes 65536 | tf_op jit(solution)/shard_map/all_to_all | solution.py:564
  137.2 2.2 %shard_map.145 = f32[3,4,81,128]{3,2,1,0:T(8,128)} custom-call(s32[64,4,384]{2,1,0:T(4,128)} %all_to_all.20.r_ref), custom_call_target="tpu_custom_call" | custom-call | tf_op jit(solution)/shard_map/pallas_call | solution.py:497
  139.4 2.0 %copy.29 = f32[3,4,81,128]{3,1,2,0:T(4,128)} copy(f32[3,4,81,128]{3,2,1,0:T(8,128)} %shard_map.145) | data formatting | bytes 995328
  141.4 5.2 %all-to-all-done.3.squares_ref = f32[64,1,128]{2,1,0:T(1,128)S(1)} async-done(((f32[64,1,128]{2,1,0:T(1,128)}), f32[64,1,128]{2,1,0:T(1,128)S(1)}, u32[]{:S(2)}, u32[]{:S(2)}) %all-to-all-start.3) | async-done | bytes 32800 | tf_op jit(solution)/shard_map/all_to_all | solution.py:564
  146.6 0.6 copy-done.11
  147.2 1.5 shard_map.148
  (35 shorter events, 0.2 us)
Async XLA Ops:
  0.6 0.9 copy-start
  0.6 15.7 %copy-start.15 = (s32[1024,2]{0,1:T(2,128)S(1)}, s32[1024,2]{0,1:T(2,128)}, u32[]{:S(2)}) copy-start(s32[1024,2]{0,1:T(2,128)} %param.18) | copy-start | bytes 24580
  0.7 16.3 %copy-start.16 = (s32[1024,2]{0,1:T(2,128)S(1)}, s32[1024,2]{0,1:T(2,128)}, u32[]{:S(2)}) copy-start(s32[1024,2]{0,1:T(2,128)} %param.19) | copy-start | bytes 24580
  0.7 16.9 %copy-start.7 = (f32[3,4,81,128]{3,1,2,0:T(4,128)S(1)}, f32[3,4,81,128]{3,1,2,0:T(4,128)}, u32[]{:S(2)}) copy-start(f32[3,4,81,128]{3,1,2,0:T(4,128)} %param.13) | copy-start | bytes 1492996
  2.2 16.2 %copy-start.4 = (bf16[8,2,4,81,128]{4,2,3,1,0:T(4,128)(2,1)S(1)}, bf16[8,2,4,81,128]{4,2,3,1,0:T(4,128)(2,1)}, u32[]{:S(2)}) copy-start(bf16[8,2,4,81,128]{4,2,3,1,0:T(4,128)(2,1)} %param.14) | copy-start | bytes 3981316
  4.3 28.3 %all-to-all-start = ((s32[32,32,128]{2,1,0:T(8,128)}), s32[32,32,128]{2,1,0:T(8,128)S(1)}, u32[]{:S(2)}, u32[]{:S(2)}) async-start(s32[32,32,128]{2,1,0:T(8,128)} %shard_map.140), calls=%async_computation | async-start | bytes 1048576 | tf_op jit(solution)/shard_map/all_to_all | solution.py:537
  23.3 16.5 %copy-start.17 = (s32[256]{0:T(256)S(1)}, s32[256]{0:T(256)}, u32[]{:S(2)}) copy-start(s32[256]{0:T(256)} %constant.71) | copy-start | bytes 3076
  23.3 16.5 %copy-start.18 = (s32[256]{0:T(256)S(1)}, s32[256]{0:T(256)}, u32[]{:S(2)}) copy-start(s32[256]{0:T(256)} %constant.69) | copy-start | bytes 3076
  23.4 16.5 %copy-start.19 = (s32[256]{0:T(256)S(1)}, s32[256]{0:T(256)}, u32[]{:S(2)}) copy-start(s32[256]{0:T(256)} %constant.61.clone) | copy-start | bytes 3076
  23.4 21.2 %copy-start.20 = (bf16[256,512]{1,0:T(8,128)(2,1)S(1)}, bf16[256,512]{1,0:T(8,128)(2,1)}, u32[]{:S(2)}) copy-start(bf16[256,512]{1,0:T(8,128)(2,1)} %constant.62.clone) | copy-start | bytes 786436
  32.6 7.3 %copy-start.2 = (s32[32,32,128]{2,1,0:T(8,128)}, s32[32,32,128]{2,1,0:T(8,128)S(1)}, u32[]{:S(2)}) copy-start(s32[32,32,128]{2,1,0:T(8,128)S(1)} %all-to-all-done.own_ref) | copy-start | bytes 1572868
  32.6 30.0 %all-to-all-start.1 = ((s32[64,8,384]{2,1,0:T(8,128)}), s32[64,8,384]{2,1,0:T(8,128)S(1)}, u32[]{:S(2)}, u32[]{:S(2)}) async-start(s32[64,8,384]{2,1,0:T(8,128)} %shard_map.141), calls=%async_computation.1 | async-start | bytes 1572864 | tf_op jit(solution)/shard_map/all_to_all | solution.py:547
  42.0 2.8 %copy-start.3 = (s32[896,128]{1,0:T(8,128)S(1)}, s32[896,128]{1,0:T(8,128)}, u32[]{:S(2)}) copy-start(s32[896,128]{1,0:T(8,128)} %shard_map.142.own_ref) | copy-start | bytes 1376260
  42.0 12.2 %collective-permute-start.3 = (s32[896,128]{1,0:T(8,128)}, s32[896,128]{1,0:T(8,128)S(1)}, u32[]{:S(2)}, u32[]{:S(2)}) collective-permute-start(s32[896,128]{1,0:T(8,128)} %shard_map.142.own_ref), channel_id=1, source_target_pairs={{0,3},{1,0},{2,1},{3,2},{4,7},{5,4},{6,5},{7,6},{8,11},{9,8},{10,9... | collective-permute-start | bytes 1376264 | tf_op jit(solution)/shard_map/ppermute | solution.py:528
  44.5 13.8 %collective-permute-start.1 = (s32[896,128]{1,0:T(8,128)}, s32[896,128]{1,0:T(8,128)S(1)}, u32[]{:S(2)}, u32[]{:S(2)}) collective-permute-start(s32[896,128]{1,0:T(8,128)} %shard_map.142.own_ref), channel_id=1, source_target_pairs={{0,1},{1,2},{2,3},{3,0},{4,5},{5,6},{6,7},{7,4},{8,9},{9,10},{10,1... | collective-permute-start | bytes 1376264 | tf_op jit(solution)/shard_map/ppermute | solution.py:528
  44.8 24.6 %collective-permute-start = (s32[896,128]{1,0:T(8,128)S(1)}, s32[896,128]{1,0:T(8,128)S(1)}, u32[]{:S(2)}, u32[]{:S(2)}) collective-permute-start(s32[896,128]{1,0:T(8,128)S(1)} %copy-done.3), channel_id=1, source_target_pairs={{0,4},{4,0},{8,12},{12,8},{16,20},{20,16},{24,28},{28,24},{32,36},... | collective-permute-start | bytes 1376264 | tf_op jit(solution)/shard_map/ppermute | solution.py:533
  54.3 12.7 %copy-start.5 = (s32[896,128]{1,0:T(8,128)}, s32[896,128]{1,0:T(8,128)S(1)}, u32[]{:S(2)}) copy-start(s32[896,128]{1,0:T(8,128)S(1)} %collective-permute-done.3.right_ref) | copy-start | bytes 1376260
  55.0 11.9 %collective-permute-start.6 = (s32[448,128]{1,0:T(8,128)}, s32[448,128]{1,0:T(8,128)}, u32[]{:S(2)}, u32[]{:S(2)}) collective-permute-start(s32[448,128]{1,0:T(8,128)} %slice.17), channel_id=1, source_target_pairs={{0,3},{1,0},{2,1},{3,2},{4,7},{5,4},{6,5},{7,6},{8,11},{9,8},{10,9... | collective-permute-start | bytes 688136 | tf_op jit(solution)/shard_map/ppermute | solution.py:528
  58.3 8.6 %copy-start.6 = (s32[896,128]{1,0:T(8,128)}, s32[896,128]{1,0:T(8,128)S(1)}, u32[]{:S(2)}) copy-start(s32[896,128]{1,0:T(8,128)S(1)} %collective-permute-done.1.left_ref) | copy-start | bytes 1376260
  59.1 7.9 %collective-permute-start.5 = (s32[448,128]{1,0:T(8,128)}, s32[448,128]{1,0:T(8,128)}, u32[]{:S(2)}, u32[]{:S(2)}) collective-permute-start(s32[448,128]{1,0:T(8,128)} %slice.16), channel_id=1, source_target_pairs={{0,1},{1,2},{2,3},{3,0},{4,5},{5,6},{6,7},{7,4},{8,9},{9,10},{10,1... | collective-permute-start | bytes 688136 | tf_op jit(solution)/shard_map/ppermute | solution.py:528
  59.1 10.3 %collective-permute-start.4 = (s32[896,128]{1,0:T(8,128)S(1)}, s32[896,128]{1,0:T(8,128)}, u32[]{:S(2)}, u32[]{:S(2)}) collective-permute-start(s32[896,128]{1,0:T(8,128)S(1)} %collective-permute-done.3.right_ref), channel_id=1, source_target_pairs={{0,4},{4,0},{8,12},{12,8},{16,20},{20,16},{24,28},{28,24},{32,36},... | collective-permute-start | bytes 1376264 | tf_op jit(solution)/shard_map/ppermute | solution.py:533
  60.7 8.8 %collective-permute-start.2 = (s32[896,128]{1,0:T(8,128)S(1)}, s32[896,128]{1,0:T(8,128)}, u32[]{:S(2)}, u32[]{:S(2)}) collective-permute-start(s32[896,128]{1,0:T(8,128)S(1)} %collective-permute-done.1.left_ref), channel_id=1, source_target_pairs={{0,4},{4,0},{8,12},{12,8},{16,20},{20,16},{24,28},{28,24},{32,36},... | collective-permute-start | bytes 1376264 | tf_op jit(solution)/shard_map/ppermute | solution.py:533
  62.6 0.9 copy-start.1
  67.0 3.0 %collective-permute-start.7 = (s32[448,128]{1,0:T(8,128)}, s32[448,128]{1,0:T(8,128)S(1)}, u32[]{:S(2)}, u32[]{:S(2)}) collective-permute-start(s32[448,128]{1,0:T(8,128)} %collective-permute-done.5.oa_ref), channel_id=1, source_target_pairs={{0,4},{4,0},{8,12},{12,8},{16,20},{20,16},{24,28},{28,24},{32,36},... | collective-permute-start | bytes 688136 | tf_op jit(solution)/shard_map/ppermute | solution.py:533
  68.7 1.7 %collective-permute-start.8 = (s32[448,128]{1,0:T(8,128)}, s32[448,128]{1,0:T(8,128)S(1)}, u32[]{:S(2)}, u32[]{:S(2)}) collective-permute-start(s32[448,128]{1,0:T(8,128)} %collective-permute-done.6.ob_ref), channel_id=1, source_target_pairs={{0,4},{4,0},{8,12},{12,8},{16,20},{20,16},{24,28},{28,24},{32,36},... | collective-permute-start | bytes 688136 | tf_op jit(solution)/shard_map/ppermute | solution.py:533
  69.4 0.9 copy-start.8
  70.0 0.7 copy-start.9
  70.4 0.7 copy-start.10
  121.7 2.8 %collective-permute-start.11 = (f32[4,1024]{1,0:T(4,128)}, f32[4,1024]{1,0:T(4,128)S(1)}, u32[]{:S(2)}, u32[]{:S(2)}) collective-permute-start(f32[4,1024]{1,0:T(4,128)} %shard_map.146.p0_ref), channel_id=1, source_target_pairs={{0,3},{1,0},{2,1},{3,2},{4,7},{5,4},{6,5},{7,6},{8,11},{9,8},{10,9... | collective-permute-start | bytes 49160 | tf_op jit(solution)/shard_map/ppermute | solution.py:528
  123.2 4.3 %collective-permute-start.10 = (f32[4,1024]{1,0:T(4,128)}, f32[4,1024]{1,0:T(4,128)S(1)}, u32[]{:S(2)}, u32[]{:S(2)}) collective-permute-start(f32[4,1024]{1,0:T(4,128)} %shard_map.146.p0_ref), channel_id=1, source_target_pairs={{0,2},{1,3},{2,0},{3,1},{4,6},{5,7},{6,4},{7,5},{8,10},{9,11},{10,... | collective-permute-start | bytes 49160 | tf_op jit(solution)/shard_map/ppermute | solution.py:528
  123.2 4.3 %collective-permute-start.9 = (f32[4,1024]{1,0:T(4,128)}, f32[4,1024]{1,0:T(4,128)S(1)}, u32[]{:S(2)}, u32[]{:S(2)}) collective-permute-start(f32[4,1024]{1,0:T(4,128)} %shard_map.146.p0_ref), channel_id=1, source_target_pairs={{0,1},{1,2},{2,3},{3,0},{4,5},{5,6},{6,7},{7,4},{8,9},{9,10},{10,1... | collective-permute-start | bytes 49160 | tf_op jit(solution)/shard_map/ppermute | solution.py:528
  124.5 3.0 %copy-start.12 = (f32[4,1024]{1,0:T(4,128)}, f32[4,1024]{1,0:T(4,128)S(1)}, u32[]{:S(2)}) copy-start(f32[4,1024]{1,0:T(4,128)S(1)} %collective-permute-done.11.p3_ref) | copy-start | bytes 49156
  127.5 0.6 copy-start.13
  128.1 0.6 copy-start.14
  130.2 16.4 %all-to-all-start.3 = ((f32[64,1,128]{2,1,0:T(1,128)}), f32[64,1,128]{2,1,0:T(1,128)S(1)}, u32[]{:S(2)}, u32[]{:S(2)}) async-start(f32[64,1,128]{2,1,0:T(1,128)} %get-tuple-element.23), calls=%async_computation.3 | async-start | bytes 65536 | tf_op jit(solution)/shard_map/all_to_all | solution.py:564
  146.6 0.6 copy-start.11

commit v5 on v4

--- a/solution.py
+++ b/solution.py
@@ -251,18 +251,21 @@
     return p0, p1, p2, p3
 
 
-def spread_pieces(pieces, first, last, ht, half):
-    def rows(k, carry):
-        blocks = regroup([ref[pl.ds(pl.multiple_of((k - f) * 32, 32), 32), :] for ref, f in pieces])
-        start = (k >> 2) * 512 + (k & 3) * 32
-        for b in range(4):
-            row = pl.multiple_of(start + b * 128, 32)
-            ht[half, pl.ds(row, 32), :] = low_of(blocks[b])
-            row = pl.multiple_of(start + b * 128 + LINES * 64, 32)
-            ht[half, pl.ds(row, 32), :] = high_of(blocks[b])
-        return carry
-
-    lax.fori_loop(first, last, rows, 0, unroll=2)
+def spread_rows(pieces, k, ht):
+    blocks = regroup([ref[pl.ds(pl.multiple_of((k - f) * 32, 32), 32), :] for ref, f in pieces])
+    start = (k >> 2) * 512 + (k & 3) * 32
+    for b in range(4):
+        row = pl.multiple_of(start + b * 128, 32)
+        ht[pl.ds(row, 32), :] = low_of(blocks[b])
+        row = pl.multiple_of(start + b * 128 + LINES * 64, 32)
+        ht[pl.ds(row, 32), :] = high_of(blocks[b])
+
+
+def row_scales(ht, rows):
+    rows[...] = jnp.zeros_like(rows)
+    rows[0:Q, :] = (
+        ht[pl.ds(Q, Q, stride=QP), :] * 2.0**15 + ht[pl.ds(Q + 1, Q, stride=QP), :]
+    ) * (2.0**-30 / LEVELS)
 
 
 def advance(place_ref, metric_ref, x, v, step, both_ref, fwd_ref, coef):
@@ -333,19 +336,21 @@
     place_ref, metric_ref, own_ref, own2_ref, left_ref, left2_ref, right_ref, right2_ref, oa_ref, oa2_ref, ob_ref, ob2_ref,
     first_ref, v, fwd_ref, back_ref, both_ref,
     out_ref,
-    ht, rows, x, coef, solved, wall, turn,
+    ht0, ht1, rows0, rows1, x, coef, solved, wall, turn,
 ):
-    spread_pieces([(r, 0) for r in (own_ref, own2_ref, left_ref, left2_ref)], 0, 28, ht, 0)
-    for first, last, oref, oref2 in ((0, 14, oa_ref, oa2_ref), (14, 28, ob_ref, ob2_ref)):
-        spread_pieces(
-            [(right_ref, 0), (right2_ref, 0), (oref, first), (oref2, first)], first, last, ht, 1
-        )
-    for half in range(2):
-        rows[half] = jnp.zeros((QP, 128), F32)
-        rows[half, 0:Q, :] = (
-            ht[half, pl.ds(Q, Q, stride=QP), :] * 2.0**15
-            + ht[half, pl.ds(Q + 1, Q, stride=QP), :]
-        ) * (2.0**-30 / LEVELS)
+    halves = (ht0, ht1)
+    scales = (rows0, rows1)
+
+    def spread_first(k, carry):
+        spread_rows([(r, 0) for r in (own_ref, own2_ref, left_ref, left2_ref)], k, ht0)
+        return carry
+
+    def spread_second(e, k):
+        far = (oa_ref, oa2_ref) if e == 0 else (ob_ref, ob2_ref)
+        spread_rows([(right_ref, 0), (right2_ref, 0), (far[0], 14 * e), (far[1], 14 * e)], k, ht1)
+
+    lax.fori_loop(0, 28, spread_first, 0, unroll=2)
+    row_scales(ht0, rows0)
 
     for step in range(NSTEP):
         if step > 0:
@@ -354,17 +359,26 @@
         for half in range(2):
             for e in range(2):
 
-                def column(r, sums, half=half, e=e, modes=modes):
-                    h = ht[half, pl.ds(pl.multiple_of(r * QP, 8), QP), :]
-                    return tuple(
-                        sums[c] + h * modes[half, pl.ds((e * 3 + c) * QP + r, 1), :]
-                        for c in range(3)
+                def columns(i, sums, half=half, e=e, modes=modes, step=step):
+                    for t in range(27):
+                        if step == 0 and half == 0 and t % 5 == 0 and t < 25:
+                            spread_second(e, jnp.minimum(5 * i + t // 5, 13) + 14 * e)
+                        r = i * 27 + t
+                        h = halves[half][pl.ds(pl.multiple_of(r * QP, 8), QP), :]
+                        sums = tuple(
+                            sums[c] + h * modes[half, pl.ds((e * 3 + c) * QP + r, 1), :]
+                            for c in range(3)
+                        )
+                    return sums
+
+                zero = jnp.zeros((QP, 128), F32)
+                sums = lax.fori_loop(0, Q // 27, columns, (zero, zero, zero))
+                for c in range(3):
+                    solved[e * 3 + c, :, half * 128 : (half + 1) * 128] = (
+                        sums[c] * scales[half][...]
                     )
-
-                zero = jnp.zeros((QP, 128), F32)
-                sums = lax.fori_loop(0, Q, column, (zero, zero, zero), unroll=27)
-                for c in range(3):
-                    solved[e * 3 + c, :, half * 128 : (half + 1) * 128] = sums[c] * rows[half]
+            if step == 0 and half == 0:
+                row_scales(ht1, rows1)
         planes = transform(solved[...].reshape(6 * QP, 256), back_ref)
         x[...] = planes.reshape(6, QP, 256)
         for e in range(2):
@@ -403,8 +417,10 @@
         in_specs=[smem_spec(), smem_spec()] + [vmem_spec()] * (len(pieces) + 5),
         out_specs=vmem_spec(),
         scratch_shapes=[
-            pltpu.VMEM((2, LINES * 128, 128), F32),
-            pltpu.VMEM((2, QP, 128), F32),
+            pltpu.VMEM((LINES * 128, 128), F32),
+            pltpu.VMEM((LINES * 128, 128), F32),
+            pltpu.VMEM((QP, 128), F32),
+            pltpu.VMEM((QP, 128), F32),
             pltpu.VMEM((6, QP, 256), F32),
             pltpu.VMEM((2, 6 * QP, 128), F32),
             pltpu.VMEM((6, QP, 256), F32),
@@ -419,14 +435,15 @@
     points = local_ref.shape[1]
     mode = lax.broadcasted_iota(jnp.int32, (128, points), 0)
     pick = jnp.where(mode == local_ref[...], 1.0, 0.0).astype(jnp.bfloat16)
+    pick = jnp.concatenate([pick, pick], axis=0)
     here = mode == element_ref[...]
     for z in range(4):
         pair = r_ref[:, z, :]
         unit = scale_of(pair[:, QP : QP + 1].astype(F32)) * (1.0 / LEVELS)
         field = jnp.concatenate([low_of(pair) * unit, high_of(pair) * unit], axis=0)
         high, low = in_two(field)
-        values = jnp.dot(low, pick, preferred_element_type=F32) + jnp.dot(
-            high, pick, preferred_element_type=F32
+        values = jnp.dot(
+            jnp.concatenate([low, high], axis=1), pick, preferred_element_type=F32
         )
         total = jnp.sum(jnp.where(here, values, 0.0), axis=0, keepdims=True)
         o_ref[z : z + 1, :] = total[:, 0 : points // 2] + total[:, points // 2 :]
@@ -540,7 +557,9 @@
     local = wall_local.T.reshape(1, 2 * wall_count)
     element = wall_element.T.reshape(1, 2 * wall_count) - plane * adjoint.shape[3]
     sent = pack_points(adjoint, checkpoints, checkpoint_step)
-    own, sent, local, element = lax.optimization_barrier((own, sent, local, element))
+    own, sent, local, element, place, fwd, back = lax.optimization_barrier(
+        (own, sent, local, element, place, fwd, back)
+    )
     own = turn_own(own)
     left = around(own, 1)
     right = around(own, 3)
@@ -552,7 +571,6 @@
     pieces = []
     for piece in (own, left, right):
         pieces += [piece, across(piece)]
-    oa, ob, first = lax.optimization_barrier((oa, ob, first))
     for piece in (oa, ob):
         pieces += [piece, across(piece)]
     out = steps(place, metric, pieces, first, velocity, fwd, back, both)

time: 149 us -> 149 us (level)
  starting transfers between devices: 38.2 us -> 40.2 us
  local copies, waits for them, and re-layouts: 12.9 us -> 11 us
    ppermute x7, waiting for transfers between devices: 12.3 us -> 15.2 us  [around(): lax.ppermute(block, 'plane', [(i, (i + step) % plane_count) for i in rang...]
    all_to_all x1, waiting for transfers between devices: 9.23 us -> 7.41 us  [on_device(): lax.all_to_all(pack_inverse(matrix, span_count // 2), 'span', 0, 0, tiled...]
    unnamed x48 -> x46, local copies, waits for them, and re-layouts: 10.4 us -> 9.93 us
  transfers between devices with their start and end apart: 15 -> 15, of which waited for: 8 -> 7; matrix products, arithmetic and copies ran while one was open for 6% -> 5% of each run, Pallas kernels for 8% -> 8%
where the time goes in v5:
time: 149 us; the launch traced here: 148 us
  Pallas kernels  41.1 us (28%)
  starting transfers between devices  40.2 us (27%)
  waiting for transfers between devices  27.9 us (19%)
  blocking collectives  25.4 us (17%)
  local copies, waits for them, and re-layouts  11 us (7%)
    all_to_all x1, blocking collectives, on_device(): received = lax.all_to_all(out, 'span', 0, 0, tiled=True)  25.4 us
    pallas_call x1, Pallas kernels, steps(): pl.pallas_call(steps_kernel, out_shape=jax.ShapeDtypeStruct((64, 4, 384),...  21.9 us
    ppermute x7, waiting for transfers between devices, around(): lax.ppermute(block, 'plane', [(i, (i + step) % plane_count) for i in rang...  15.2 us
    all_to_all x1, starting transfers between devices, on_device(): lax.all_to_all(pack_inverse(matrix, span_count // 2), 'span', 0, 0, tiled...  12 us
    unnamed x46, local copies, waits for them, and re-layouts  9.93 us
    ppermute x7, starting transfers between devices, around(): lax.ppermute(block, 'plane', [(i, (i + step) % plane_count) for i in rang...  8.53 us
    all_to_all x1, waiting for transfers between devices, on_device(): lax.all_to_all(pack_inverse(matrix, span_count // 2), 'span', 0, 0, tiled...  7.41 us
    all_to_all x1, starting transfers between devices, on_device(): points = lax.all_to_all(sent, 'span', 0, 0, tiled=True)  7.24 us
  transfers between devices with their start and end apart: 15, of which 7 were waited for; matrix products, arithmetic and copies ran while one was open for 5% of the time, Pallas kernels for 8%

profile of v5, /device:TPU:1, one launch (start us, length us, event | category | flops | bytes accessed | tf_op | source)
XLA Modules:
  0.0 148.1 jit_solution(17809234230940142955)
XLA Ops:
  0.6 0.0 copy-start
  0.6 0.0 copy-start.14
  0.7 0.0 copy-start.3
  0.7 0.9 copy-done
  1.6 0.6 copy.34
  2.2 2.0 %shard_map.140 = s32[32,32,128]{2,1,0:T(8,128)} custom-call(f32[81,81]{1,0:T(8,128)} %bitcast.20), custom_call_target="tpu_custom_call" | custom-call | tf_op jit(solution)/shard_map/pallas_call | solution.py:154
  4.2 12.0 %all-to-all-start = ((s32[32,32,128]{2,1,0:T(8,128)}), s32[32,32,128]{2,1,0:T(8,128)S(1)}, u32[]{:S(2)}, u32[]{:S(2)}) async-start(s32[32,32,128]{2,1,0:T(8,128)} %shard_map.140), calls=%async_computation | async-start | bytes 1048576 | tf_op jit(solution)/shard_map/all_to_all | solution.py:554
  16.3 0.6 copy.32
  16.9 1.4 copy.24.c0_ref.c1_ref.c2_ref
  18.2 0.8 copy.23.adj_ref
  19.1 0.6 copy.31
  19.7 3.7 %shard_map.141 = s32[64,8,384]{2,1,0:T(8,128)} custom-call(s32[3]{0:T(128)} %step_ref.1, f32[3,4,81,128]{3,2,1,0:T(8,128)} %copy.23.adj_ref, bf16[8,2,4,81,128]{4,3,2,1,0:T(8,128)(2,1)} %copy.24.c0_ref.c1_ref.c2_ref, bf16[8,2,4,81,128]{4,3,2,1,0:T(8,128)(2,1)} %copy.24.c0_ref.c1_ref.c2_ref, bf16[8,2,4,81,128]{4,3,2,1,0:T(8,128)(2,1)} %copy.24.c0_ref.c1_ref.c2_ref), custom_call_target="tpu_custom_call" | custom-call | tf_op jit(solution)/shard_map/pallas_call | solution.py:211
  23.4 0.6 pad_add_fusion.place_ref
  23.9 0.0 copy-done.17
  24.0 0.0 copy-done.19
  24.0 0.3 convolution_convert_fusion
  24.3 0.8 pad_maximum_fusion.1.back_ref
  25.1 7.4 %all-to-all-done.own_ref = s32[32,32,128]{2,1,0:T(8,128)S(1)} async-done(((s32[32,32,128]{2,1,0:T(8,128)}), s32[32,32,128]{2,1,0:T(8,128)S(1)}, u32[]{:S(2)}, u32[]{:S(2)}) %all-to-all-start) | async-done | bytes 524320 | tf_op jit(solution)/shard_map/all_to_all | solution.py:554
  32.5 7.2 %all-to-all-start.1 = ((s32[64,8,384]{2,1,0:T(8,128)}), s32[64,8,384]{2,1,0:T(8,128)S(1)}, u32[]{:S(2)}, u32[]{:S(2)}) async-start(s32[64,8,384]{2,1,0:T(8,128)} %shard_map.141), calls=%async_computation.1 | async-start | bytes 1572864 | tf_op jit(solution)/shard_map/all_to_all | solution.py:566
  39.8 2.1 %shard_map.142.own_ref = s32[896,128]{1,0:T(8,128)} custom-call(s32[32,32,128]{2,1,0:T(8,128)} %copy-done.2), custom_call_target="tpu_custom_call" | custom-call | tf_op jit(solution)/shard_map/pallas_call | solution.py:171
  41.9 1.2 collective-permute-start.1
  43.1 1.5 collective-permute-start.3
  44.6 1.0 collective-permute-start
  45.6 9.4 %collective-permute-done.1.left_ref = s32[896,128]{1,0:T(8,128)S(1)} collective-permute-done((s32[896,128]{1,0:T(8,128)}, s32[896,128]{1,0:T(8,128)S(1)}, u32[]{:S(2)}, u32[]{:S(2)}) %collective-permute-start.1) | collective-permute-done | bytes 458784 | tf_op jit(solution)/shard_map/ppermute | solution.py:545
  55.0 0.1 collective-permute-start.5
  55.1 0.0 collective-permute-done.3.right_ref
  55.1 2.7 %collective-permute-start.7 = (s32[448,128]{1,0:T(8,128)S(1)}, s32[448,128]{1,0:T(8,128)}, u32[]{:S(2)}, u32[]{:S(2)}) collective-permute-start(s32[448,128]{1,0:T(8,128)S(1)} %slice.19), channel_id=1, source_target_pairs={{0,3},{1,0},{2,1},{3,2},{4,7},{5,4},{6,5},{7,6},{8,11},{9,8},{10,9... | collective-permute-start | bytes 688136 | tf_op jit(solution)/shard_map/ppermute | solution.py:545
  57.8 1.9 %collective-permute-start.2 = (s32[896,128]{1,0:T(8,128)S(1)}, s32[896,128]{1,0:T(8,128)S(1)}, u32[]{:S(2)}, u32[]{:S(2)}) collective-permute-start(s32[896,128]{1,0:T(8,128)S(1)} %collective-permute-done.1.left_ref), channel_id=1, source_target_pairs={{0,4},{4,0},{8,12},{12,8},{16,20},{20,16},{24,28},{28,24},{32,36},... | collective-permute-start | bytes 1376264 | tf_op jit(solution)/shard_map/ppermute | solution.py:550
  59.7 0.0 collective-permute-start.4
  59.7 2.4 %collective-permute-done.5.oa_ref = s32[448,128]{1,0:T(8,128)S(1)} collective-permute-done((s32[448,128]{1,0:T(8,128)S(1)}, s32[448,128]{1,0:T(8,128)S(1)}, u32[]{:S(2)}, u32[]{:S(2)}) %collective-permute-start.5) | collective-permute-done | bytes 229408 | tf_op jit(solution)/shard_map/ppermute | solution.py:545
  62.1 2.2 %collective-permute-start.6 = (s32[448,128]{1,0:T(8,128)S(1)}, s32[448,128]{1,0:T(8,128)}, u32[]{:S(2)}, u32[]{:S(2)}) collective-permute-start(s32[448,128]{1,0:T(8,128)S(1)} %collective-permute-done.5.oa_ref), channel_id=1, source_target_pairs={{0,4},{4,0},{8,12},{12,8},{16,20},{20,16},{24,28},{28,24},{32,36},... | collective-permute-start | bytes 688136 | tf_op jit(solution)/shard_map/ppermute | solution.py:550
  64.3 0.0 collective-permute-done.7.ob_ref
  64.3 0.3 collective-permute-start.8
  64.5 0.9 copy.27.fwd_ref
  65.5 0.0 all-to-all-done.1.r_ref
  65.5 0.9 copy-done.1
  66.4 3.4 %shard_map.143 = (f32[2,528,128]{2,1,0:T(8,128)}, f32[2,2,3,88,256]{4,3,2,1,0:T(8,128)}) custom-call(s32[2]{0:T(128)} %pad_add_fusion.place_ref, f32[2,128]{1,0:T(2,128)} %metric_ref.3, s32[64,8,384]{2,1,0:T(8,128)} %copy-done.1, bf16[768,256]{1,0:T(8,128)(2,1)} %copy.27.fwd_ref, bf16[352,88]{1,0:T(8,128)(2,1)} %constant.63.clone.both_ref), custom_call_target="tpu_custom_call" | custom-call | tf_op jit(solution)/shard_map/pallas_call | solution.py:322
  69.8 0.0 collective-permute-done.own2_ref
  69.8 0.0 collective-permute-done.6.oa2_ref
  69.9 0.0 collective-permute-done.8.ob2_ref
  69.9 0.0 collective-permute-done.2.left2_ref
  69.9 0.0 collective-permute-done.4.right2_ref
  69.9 0.0 copy-done.5
  69.9 0.0 copy-done.9
  69.9 0.7 copy-done.7
  70.6 0.2 copy-done.8
  70.8 21.9 %shard_map.144 = s32[64,4,384]{2,1,0:T(4,128)} custom-call(s32[2]{0:T(128)} %pad_add_fusion.place_ref, f32[2,128]{1,0:T(2,128)} %metric_ref.3, s32[896,128]{1,0:T(8,128)} %shard_map.142.own_ref, s32[896,128]{1,0:T(8,128)} %copy-done.7, s32[896,128]{1,0:T(8,128)} %copy-done.4, s32[896,128]{1,0:T(8,128)} %copy-done.8, s32[896,128]{1,0:T(8,128)} %copy-done.5, ...), custom_call_target="tpu_custom_call" | custom-call | tf_op jit(solution)/shard_map/pallas_call | solution.py:414
  92.6 25.4 %all_to_all.20.r_ref = s32[64,4,384]{2,1,0:T(4,128)} all-to-all(s32[64,4,384]{2,1,0:T(4,128)} %shard_map.144), channel_id=1, replica_groups=mesh['span'=64,'plane'=4] {'span'}, dimensions={0} | all-to-all | bytes 786432 | tf_op jit(solution)/shard_map/all_to_all | solution.py:577
  118.1 3.0 %shard_map.146.p0_ref = f32[4,1024]{1,0:T(4,128)} custom-call(s32[64,4,384]{2,1,0:T(4,128)} %all_to_all.20.r_ref, s32[1,2048]{1,0:T(1,128)} %bitcast.22, s32[1,2048]{1,0:T(1,128)} %bitcast.21), custom_call_target="tpu_custom_call" | custom-call | tf_op jit(solution)/shard_map/pallas_call | solution.py:453
  121.0 1.0 collective-permute-start.10
  122.1 1.4 collective-permute-start.11
  123.5 0.6 collective-permute-start.9
  124.1 1.3 collective-permute-done.10.p2_ref
  125.4 0.5 collective-permute-done.11.p3_ref
  125.9 1.6 %collective-permute-done.9.p1_ref = f32[4,1024]{1,0:T(4,128)S(1)} collective-permute-done((f32[4,1024]{1,0:T(4,128)}, f32[4,1024]{1,0:T(4,128)S(1)}, u32[]{:S(2)}, u32[]{:S(2)}) %collective-permute-start.9) | collective-permute-done | bytes 16416 | tf_op jit(solution)/shard_map/ppermute | solution.py:545
  127.5 0.0 copy-done.12
  127.5 0.6 copy-done.13
  128.1 1.5 %shard_map.147 = (f32[4,1024]{1,0:T(4,128)}, f32[64,1,128]{2,1,0:T(1,128)}) custom-call(f32[4,1024]{1,0:T(4,128)} %weight_ref.1, f32[4,1024]{1,0:T(4,128)} %shard_map.146.p0_ref, f32[4,1024]{1,0:T(4,128)} %copy-done.13, f32[4,1024]{1,0:T(4,128)} %copy-done.11, f32[4,1024]{1,0:T(4,128)} %copy-done.12), custom_call_target="tpu_custom_call" | custom-call | tf_op jit(solution)/shard_map/pallas_call | solution.py:475
  129.6 7.0 %all-to-all-start.3 = ((f32[64,1,128]{2,1,0:T(1,128)}), f32[64,1,128]{2,1,0:T(1,128)S(1)}, u32[]{:S(2)}, u32[]{:S(2)}) async-start(f32[64,1,128]{2,1,0:T(1,128)} %get-tuple-element.23), calls=%async_computation.3 | async-start | bytes 65536 | tf_op jit(solution)/shard_map/all_to_all | solution.py:582
  136.7 2.2 %shard_map.145 = f32[3,4,81,128]{3,2,1,0:T(8,128)} custom-call(s32[64,4,384]{2,1,0:T(4,128)} %all_to_all.20.r_ref), custom_call_target="tpu_custom_call" | custom-call | tf_op jit(solution)/shard_map/pallas_call | solution.py:514
  138.8 2.0 %copy.29 = f32[3,4,81,128]{3,1,2,0:T(4,128)} copy(f32[3,4,81,128]{3,2,1,0:T(8,128)} %shard_map.145) | data formatting | bytes 995328
  140.8 5.3 %all-to-all-done.3.squares_ref = f32[64,1,128]{2,1,0:T(1,128)S(1)} async-done(((f32[64,1,128]{2,1,0:T(1,128)}), f32[64,1,128]{2,1,0:T(1,128)S(1)}, u32[]{:S(2)}, u32[]{:S(2)}) %all-to-all-start.3) | async-done | bytes 32800 | tf_op jit(solution)/shard_map/all_to_all | solution.py:582
  146.1 0.6 copy-done.10
  146.7 1.5 shard_map.148
  (33 shorter events, 0.2 us)
Async XLA Ops:
  0.6 0.9 copy-start
  0.6 15.6 %copy-start.14 = (s32[1024,2]{0,1:T(2,128)S(1)}, s32[1024,2]{0,1:T(2,128)}, u32[]{:S(2)}) copy-start(s32[1024,2]{0,1:T(2,128)} %param.18) | copy-start | bytes 24580
  0.7 16.2 %copy-start.3 = (bf16[8,2,4,81,128]{4,2,3,1,0:T(4,128)(2,1)S(1)}, bf16[8,2,4,81,128]{4,2,3,1,0:T(4,128)(2,1)}, u32[]{:S(2)}) copy-start(bf16[8,2,4,81,128]{4,2,3,1,0:T(4,128)(2,1)} %param.14) | copy-start | bytes 3981316
  4.2 28.3 %all-to-all-start = ((s32[32,32,128]{2,1,0:T(8,128)}), s32[32,32,128]{2,1,0:T(8,128)S(1)}, u32[]{:S(2)}, u32[]{:S(2)}) async-start(s32[32,32,128]{2,1,0:T(8,128)} %shard_map.140), calls=%async_computation | async-start | bytes 1048576 | tf_op jit(solution)/shard_map/all_to_all | solution.py:554
  16.9 1.4 copy-start.6
  16.9 2.2 %copy-start.15 = (s32[1024,2]{0,1:T(2,128)S(1)}, s32[1024,2]{0,1:T(2,128)}, u32[]{:S(2)}) copy-start(s32[1024,2]{0,1:T(2,128)} %param.19) | copy-start | bytes 24580
  19.7 4.2 %copy-start.16 = (s32[256]{0:T(256)S(1)}, s32[256]{0:T(256)}, u32[]{:S(2)}) copy-start(s32[256]{0:T(256)} %constant.61.clone) | copy-start | bytes 3076
  19.7 4.2 %copy-start.17 = (s32[256]{0:T(256)S(1)}, s32[256]{0:T(256)}, u32[]{:S(2)}) copy-start(s32[256]{0:T(256)} %constant.69) | copy-start | bytes 3076
  19.7 4.2 %copy-start.18 = (s32[256]{0:T(256)S(1)}, s32[256]{0:T(256)}, u32[]{:S(2)}) copy-start(s32[256]{0:T(256)} %constant.71) | copy-start | bytes 3076
  19.7 4.3 %copy-start.19 = (bf16[256,512]{1,0:T(8,128)(2,1)S(1)}, bf16[256,512]{1,0:T(8,128)(2,1)}, u32[]{:S(2)}) copy-start(bf16[256,512]{1,0:T(8,128)(2,1)} %constant.62.clone) | copy-start | bytes 786436
  32.5 7.3 %copy-start.2 = (s32[32,32,128]{2,1,0:T(8,128)}, s32[32,32,128]{2,1,0:T(8,128)S(1)}, u32[]{:S(2)}) copy-start(s32[32,32,128]{2,1,0:T(8,128)S(1)} %all-to-all-done.own_ref) | copy-start | bytes 1572868
  32.5 33.0 %all-to-all-start.1 = ((s32[64,8,384]{2,1,0:T(8,128)}), s32[64,8,384]{2,1,0:T(8,128)S(1)}, u32[]{:S(2)}, u32[]{:S(2)}) async-start(s32[64,8,384]{2,1,0:T(8,128)} %shard_map.141), calls=%async_computation.1 | async-start | bytes 1572864 | tf_op jit(solution)/shard_map/all_to_all | solution.py:566
  41.9 13.1 %collective-permute-start.1 = (s32[896,128]{1,0:T(8,128)}, s32[896,128]{1,0:T(8,128)S(1)}, u32[]{:S(2)}, u32[]{:S(2)}) collective-permute-start(s32[896,128]{1,0:T(8,128)} %shard_map.142.own_ref), channel_id=1, source_target_pairs={{0,1},{1,2},{2,3},{3,0},{4,5},{5,6},{6,7},{7,4},{8,9},{9,10},{10,1... | collective-permute-start | bytes 1376264 | tf_op jit(solution)/shard_map/ppermute | solution.py:545
  43.1 12.0 %collective-permute-start.3 = (s32[896,128]{1,0:T(8,128)}, s32[896,128]{1,0:T(8,128)S(1)}, u32[]{:S(2)}, u32[]{:S(2)}) collective-permute-start(s32[896,128]{1,0:T(8,128)} %shard_map.142.own_ref), channel_id=1, source_target_pairs={{0,3},{1,0},{2,1},{3,2},{4,7},{5,4},{6,5},{7,6},{8,11},{9,8},{10,9... | collective-permute-start | bytes 1376264 | tf_op jit(solution)/shard_map/ppermute | solution.py:545
  44.6 25.3 %collective-permute-start = (s32[896,128]{1,0:T(8,128)}, s32[896,128]{1,0:T(8,128)S(1)}, u32[]{:S(2)}, u32[]{:S(2)}) collective-permute-start(s32[896,128]{1,0:T(8,128)} %shard_map.142.own_ref), channel_id=1, source_target_pairs={{0,4},{4,0},{8,12},{12,8},{16,20},{20,16},{24,28},{28,24},{32,36},... | collective-permute-start | bytes 1376264 | tf_op jit(solution)/shard_map/ppermute | solution.py:550
  54.9 14.9 %copy-start.4 = (s32[896,128]{1,0:T(8,128)}, s32[896,128]{1,0:T(8,128)S(1)}, u32[]{:S(2)}) copy-start(s32[896,128]{1,0:T(8,128)S(1)} %collective-permute-done.1.left_ref) | copy-start | bytes 1376260
  55.0 7.1 %collective-permute-start.5 = (s32[448,128]{1,0:T(8,128)S(1)}, s32[448,128]{1,0:T(8,128)S(1)}, u32[]{:S(2)}, u32[]{:S(2)}) collective-permute-start(s32[448,128]{1,0:T(8,128)S(1)} %slice.18), channel_id=1, source_target_pairs={{0,1},{1,2},{2,3},{3,0},{4,5},{5,6},{6,7},{7,4},{8,9},{9,10},{10,1... | collective-permute-start | bytes 688136 | tf_op jit(solution)/shard_map/ppermute | solution.py:545
  55.1 14.8 %copy-start.5 = (s32[896,128]{1,0:T(8,128)}, s32[896,128]{1,0:T(8,128)S(1)}, u32[]{:S(2)}) copy-start(s32[896,128]{1,0:T(8,128)S(1)} %collective-permute-done.3.right_ref) | copy-start | bytes 1376260
  55.1 9.2 %collective-permute-start.7 = (s32[448,128]{1,0:T(8,128)S(1)}, s32[448,128]{1,0:T(8,128)}, u32[]{:S(2)}, u32[]{:S(2)}) collective-permute-start(s32[448,128]{1,0:T(8,128)S(1)} %slice.19), channel_id=1, source_target_pairs={{0,3},{1,0},{2,1},{3,2},{4,7},{5,4},{6,5},{7,6},{8,11},{9,8},{10,9... | collective-permute-start | bytes 688136 | tf_op jit(solution)/shard_map/ppermute | solution.py:545
  57.8 12.0 %collective-permute-start.2 = (s32[896,128]{1,0:T(8,128)S(1)}, s32[896,128]{1,0:T(8,128)S(1)}, u32[]{:S(2)}, u32[]{:S(2)}) collective-permute-start(s32[896,128]{1,0:T(8,128)S(1)} %collective-permute-done.1.left_ref), channel_id=1, source_target_pairs={{0,4},{4,0},{8,12},{12,8},{16,20},{20,16},{24,28},{28,24},{32,36},... | collective-permute-start | bytes 1376264 | tf_op jit(solution)/shard_map/ppermute | solution.py:550
  59.7 10.2 %collective-permute-start.4 = (s32[896,128]{1,0:T(8,128)S(1)}, s32[896,128]{1,0:T(8,128)}, u32[]{:S(2)}, u32[]{:S(2)}) collective-permute-start(s32[896,128]{1,0:T(8,128)S(1)} %collective-permute-done.3.right_ref), channel_id=1, source_target_pairs={{0,4},{4,0},{8,12},{12,8},{16,20},{20,16},{24,28},{28,24},{32,36},... | collective-permute-start | bytes 1376264 | tf_op jit(solution)/shard_map/ppermute | solution.py:550
  62.1 7.9 %copy-start.9 = (s32[448,128]{1,0:T(8,128)}, s32[448,128]{1,0:T(8,128)S(1)}, u32[]{:S(2)}) copy-start(s32[448,128]{1,0:T(8,128)S(1)} %collective-permute-done.5.oa_ref) | copy-start | bytes 688132
  62.1 7.8 %collective-permute-start.6 = (s32[448,128]{1,0:T(8,128)S(1)}, s32[448,128]{1,0:T(8,128)}, u32[]{:S(2)}, u32[]{:S(2)}) collective-permute-start(s32[448,128]{1,0:T(8,128)S(1)} %collective-permute-done.5.oa_ref), channel_id=1, source_target_pairs={{0,4},{4,0},{8,12},{12,8},{16,20},{20,16},{24,28},{28,24},{32,36},... | collective-permute-start | bytes 688136 | tf_op jit(solution)/shard_map/ppermute | solution.py:550
  64.3 5.6 %collective-permute-start.8 = (s32[448,128]{1,0:T(8,128)}, s32[448,128]{1,0:T(8,128)}, u32[]{:S(2)}, u32[]{:S(2)}) collective-permute-start(s32[448,128]{1,0:T(8,128)} %collective-permute-done.7.ob_ref), channel_id=1, source_target_pairs={{0,4},{4,0},{8,12},{12,8},{16,20},{20,16},{24,28},{28,24},{32,36},... | collective-permute-start | bytes 688136 | tf_op jit(solution)/shard_map/ppermute | solution.py:550
  65.5 0.9 copy-start.1
  69.8 0.8 copy-start.7
  69.9 0.9 copy-start.8
  121.0 4.3 %collective-permute-start.10 = (f32[4,1024]{1,0:T(4,128)}, f32[4,1024]{1,0:T(4,128)S(1)}, u32[]{:S(2)}, u32[]{:S(2)}) collective-permute-start(f32[4,1024]{1,0:T(4,128)} %shard_map.146.p0_ref), channel_id=1, source_target_pairs={{0,2},{1,3},{2,0},{3,1},{4,6},{5,7},{6,4},{7,5},{8,10},{9,11},{10,... | collective-permute-start | bytes 49160 | tf_op jit(solution)/shard_map/ppermute | solution.py:545
  122.1 3.8 %collective-permute-start.11 = (f32[4,1024]{1,0:T(4,128)}, f32[4,1024]{1,0:T(4,128)S(1)}, u32[]{:S(2)}, u32[]{:S(2)}) collective-permute-start(f32[4,1024]{1,0:T(4,128)} %shard_map.146.p0_ref), channel_id=1, source_target_pairs={{0,3},{1,0},{2,1},{3,2},{4,7},{5,4},{6,5},{7,6},{8,11},{9,8},{10,9... | collective-permute-start | bytes 49160 | tf_op jit(solution)/shard_map/ppermute | solution.py:545
  123.5 4.0 %collective-permute-start.9 = (f32[4,1024]{1,0:T(4,128)}, f32[4,1024]{1,0:T(4,128)S(1)}, u32[]{:S(2)}, u32[]{:S(2)}) collective-permute-start(f32[4,1024]{1,0:T(4,128)} %shard_map.146.p0_ref), channel_id=1, source_target_pairs={{0,1},{1,2},{2,3},{3,0},{4,5},{5,6},{6,7},{7,4},{8,9},{9,10},{10,1... | collective-permute-start | bytes 49160 | tf_op jit(solution)/shard_map/ppermute | solution.py:545
  125.3 2.2 %copy-start.11 = (f32[4,1024]{1,0:T(4,128)}, f32[4,1024]{1,0:T(4,128)S(1)}, u32[]{:S(2)}) copy-start(f32[4,1024]{1,0:T(4,128)S(1)} %collective-permute-done.10.p2_ref) | copy-start | bytes 49156
  125.9 1.6 %copy-start.12 = (f32[4,1024]{1,0:T(4,128)}, f32[4,1024]{1,0:T(4,128)S(1)}, u32[]{:S(2)}) copy-start(f32[4,1024]{1,0:T(4,128)S(1)} %collective-permute-done.11.p3_ref) | copy-start | bytes 49156
  127.5 0.6 copy-start.13
  129.6 16.4 %all-to-all-start.3 = ((f32[64,1,128]{2,1,0:T(1,128)}), f32[64,1,128]{2,1,0:T(1,128)S(1)}, u32[]{:S(2)}, u32[]{:S(2)}) async-start(f32[64,1,128]{2,1,0:T(1,128)} %get-tuple-element.23), calls=%async_computation.3 | async-start | bytes 65536 | tf_op jit(solution)/shard_map/all_to_all | solution.py:582
  146.1 0.6 copy-start.10

commit v6 on v5

--- a/solution.py
+++ b/solution.py
@@ -268,6 +268,24 @@
     ) * (2.0**-30 / LEVELS)
 
 
+def regroup_kernel(own_ref, own2_ref, left_ref, left2_ref, o_ref):
+    def spread(k, carry):
+        spread_rows([(r, 0) for r in (own_ref, own2_ref, left_ref, left2_ref)], k, o_ref)
+        return carry
+
+    lax.fori_loop(0, 28, spread, 0, unroll=7)
+
+
+def regroup_half(pieces):
+    return pl.pallas_call(
+        regroup_kernel,
+        out_shape=jax.ShapeDtypeStruct((LINES * 128, 128), F32),
+        in_specs=[vmem_spec()] * 4,
+        out_specs=vmem_spec(),
+        compiler_params=params(),
+    )(*pieces)
+
+
 def advance(place_ref, metric_ref, x, v, step, both_ref, fwd_ref, coef):
     chip = place_ref[0]
     for e in range(2):
@@ -333,24 +351,26 @@
 
 
 def steps_kernel(
-    place_ref, metric_ref, own_ref, own2_ref, left_ref, left2_ref, right_ref, right2_ref, oa_ref, oa2_ref, ob_ref, ob2_ref,
+    place_ref, metric_ref, regrouped_ref, right_ref, right2_ref, oa_ref, oa2_ref, ob_ref, ob2_ref,
     first_ref, v, fwd_ref, back_ref, both_ref,
     out_ref,
-    ht0, ht1, rows0, rows1, x, coef, solved, wall, turn,
+    ht0, ht1, rows0, rows1, x, coef, solved, wall, turn, sem,
 ):
+    load = pltpu.make_async_copy(regrouped_ref, ht0, sem)
+    load.start()
     halves = (ht0, ht1)
     scales = (rows0, rows1)
-
-    def spread_first(k, carry):
-        spread_rows([(r, 0) for r in (own_ref, own2_ref, left_ref, left2_ref)], k, ht0)
-        return carry
-
-    def spread_second(e, k):
-        far = (oa_ref, oa2_ref) if e == 0 else (ob_ref, ob2_ref)
-        spread_rows([(right_ref, 0), (right2_ref, 0), (far[0], 14 * e), (far[1], 14 * e)], k, ht1)
-
-    lax.fori_loop(0, 28, spread_first, 0, unroll=2)
+    for first, far in ((0, (oa_ref, oa2_ref)), (14, (ob_ref, ob2_ref))):
+
+        def spread(k, carry, first=first, far=far):
+            near = [(right_ref, 0), (right2_ref, 0)]
+            spread_rows(near + [(ref, first) for ref in far], k, ht1)
+            return carry
+
+        lax.fori_loop(first, first + 14, spread, 0, unroll=7)
+    load.wait()
     row_scales(ht0, rows0)
+    row_scales(ht1, rows1)
 
     for step in range(NSTEP):
         if step > 0:
@@ -359,10 +379,8 @@
         for half in range(2):
             for e in range(2):
 
-                def columns(i, sums, half=half, e=e, modes=modes, step=step):
+                def columns(i, sums, half=half, e=e, modes=modes):
                     for t in range(27):
-                        if step == 0 and half == 0 and t % 5 == 0 and t < 25:
-                            spread_second(e, jnp.minimum(5 * i + t // 5, 13) + 14 * e)
                         r = i * 27 + t
                         h = halves[half][pl.ds(pl.multiple_of(r * QP, 8), QP), :]
                         sums = tuple(
@@ -377,8 +395,6 @@
                     solved[e * 3 + c, :, half * 128 : (half + 1) * 128] = (
                         sums[c] * scales[half][...]
                     )
-            if step == 0 and half == 0:
-                row_scales(ht1, rows1)
         planes = transform(solved[...].reshape(6 * QP, 256), back_ref)
         x[...] = planes.reshape(6, QP, 256)
         for e in range(2):
@@ -410,11 +426,12 @@
         out_ref[:, z, 0:256] = turned[z * 64 : (z + 1) * 64, :]
 
 
-def steps(place, metric, pieces, first, velocity, fwd, back, both):
+def steps(place, metric, regrouped, pieces, first, velocity, fwd, back, both):
     return pl.pallas_call(
         steps_kernel,
         out_shape=jax.ShapeDtypeStruct((64, 4, 384), jnp.int32),
-        in_specs=[smem_spec(), smem_spec()] + [vmem_spec()] * (len(pieces) + 5),
+        in_specs=[smem_spec(), smem_spec(), pl.BlockSpec(memory_space=pl.ANY)]
+        + [vmem_spec()] * (len(pieces) + 5),
         out_specs=vmem_spec(),
         scratch_shapes=[
             pltpu.VMEM((LINES * 128, 128), F32),
@@ -426,9 +443,10 @@
             pltpu.VMEM((6, QP, 256), F32),
             pltpu.VMEM((2, QP, 256), F32),
             pltpu.VMEM((256, 256), jnp.int32),
+            pltpu.SemaphoreType.DMA,
         ],
         compiler_params=params(),
-    )(place, metric, *pieces, first, velocity, fwd, back, both)
+    )(place, metric, regrouped, *pieces, first, velocity, fwd, back, both)
 
 
 def wall_kernel(r_ref, local_ref, element_ref, o_ref):
@@ -568,12 +586,12 @@
     ob = around(right[448:], 3)
     both = slope_table()
     first, velocity = first_modes(place, metric, points, fwd, both)
-    pieces = []
-    for piece in (own, left, right):
-        pieces += [piece, across(piece)]
+    regrouped = regroup_half((own, across(own), left, across(left)))
+    pieces = [right, across(right)]
+    oa, ob, regrouped = lax.optimization_barrier((oa, ob, regrouped))
     for piece in (oa, ob):
         pieces += [piece, across(piece)]
-    out = steps(place, metric, pieces, first, velocity, fwd, back, both)
+    out = steps(place, metric, regrouped, pieces, first, velocity, fwd, back, both)
     received = lax.all_to_all(out, "span", 0, 0, tiled=True)
 
     partial_sum = wall_sums(received, local, element)

time: 149 us -> 147 us (0.987)
  starting transfers between devices: 40.2 us -> 37.2 us
  waiting for transfers between devices: 27.9 us -> 25.5 us
  Pallas kernels: 41.1 us -> 43.2 us
  local copies, waits for them, and re-layouts: 11 us -> 12.6 us
    pallas_call x0 -> x1, Pallas kernels: none -> 5.48 us  [regroup_half(): pl.pallas_call(regroup_kernel, out_shape=jax.ShapeDtypeStruct((LINES * 12...]
    pallas_call x1, Pallas kernels: 21.9 us -> 18.4 us  [steps(): pl.pallas_call(steps_kernel, out_shape=jax.ShapeDtypeStruct((64, 4, 384),...]
    ppermute x7, waiting for transfers between devices: 15.2 us -> 12.9 us  [around(): lax.ppermute(block, 'plane', [(i, (i + step) % plane_count) for i in rang...]
    ppermute x5, starting transfers between devices: 5.36 us -> 3.46 us  [across(): return lax.ppermute(block, 'span', [(i, i ^ 1) for i in range(span_count)])]
    unnamed x46 -> x54, local copies, waits for them, and re-layouts: 9.93 us -> 11.5 us
  transfers between devices with their start and end apart: 15 -> 15, of which waited for: 7 -> 5; matrix products, arithmetic and copies ran while one was open for 5% -> 5% of each run, Pallas kernels for 8% -> 12%
where the time goes in v6:
time: 147 us; the launch traced here: 146 us
  Pallas kernels  43.2 us (29%)
  starting transfers between devices  37.2 us (25%)
  waiting for transfers between devices  25.5 us (17%)
  blocking collectives  25.4 us (17%)
  local copies, waits for them, and re-layouts  12.6 us (9%)
    all_to_all x1, blocking collectives, on_device(): received = lax.all_to_all(out, 'span', 0, 0, tiled=True)  25.4 us
    pallas_call x1, Pallas kernels, steps(): pl.pallas_call(steps_kernel, out_shape=jax.ShapeDtypeStruct((64, 4, 384),...  18.4 us
    ppermute x7, waiting for transfers between devices, around(): lax.ppermute(block, 'plane', [(i, (i + step) % plane_count) for i in rang...  12.9 us
    all_to_all x1, starting transfers between devices, on_device(): lax.all_to_all(pack_inverse(matrix, span_count // 2), 'span', 0, 0, tiled...  12 us
    unnamed x54, local copies, waits for them, and re-layouts  11.5 us
    all_to_all x1, waiting for transfers between devices, on_device(): lax.all_to_all(pack_inverse(matrix, span_count // 2), 'span', 0, 0, tiled...  7.34 us
    ppermute x7, starting transfers between devices, around(): lax.ppermute(block, 'plane', [(i, (i + step) % plane_count) for i in rang...  7.27 us
    all_to_all x1, starting transfers between devices, on_device(): points = lax.all_to_all(sent, 'span', 0, 0, tiled=True)  7.24 us
  transfers between devices with their start and end apart: 15, of which 5 were waited for; matrix products, arithmetic and copies ran while one was open for 5% of the time, Pallas kernels for 12%

profile of v6, /device:TPU:1, one launch (start us, length us, event | category | flops | bytes accessed | tf_op | source)
XLA Modules:
  0.0 146.5 jit_solution(14708883008960335851)
XLA Ops:
  0.6 0.0 copy-start
  0.7 0.9 copy-done
  1.6 0.6 copy.34
  2.2 2.0 %shard_map.140 = s32[32,32,128]{2,1,0:T(8,128)} custom-call(f32[81,81]{1,0:T(8,128)} %bitcast.20), custom_call_target="tpu_custom_call" | custom-call | tf_op jit(solution)/shard_map/pallas_call | solution.py:154
  4.2 12.0 %all-to-all-start = ((s32[32,32,128]{2,1,0:T(8,128)}), s32[32,32,128]{2,1,0:T(8,128)S(1)}, u32[]{:S(2)}, u32[]{:S(2)}) async-start(s32[32,32,128]{2,1,0:T(8,128)} %shard_map.140), calls=%async_computation | async-start | bytes 1048576 | tf_op jit(solution)/shard_map/all_to_all | solution.py:572
  16.2 0.0 copy-start.6
  16.3 0.6 copy.32
  16.9 0.0 copy-done.3
  16.9 1.4 copy.24.c0_ref.c1_ref.c2_ref
  18.3 0.8 copy.23.adj_ref
  19.1 0.0 copy-done.19
  19.1 0.6 copy.31
  19.7 3.7 %shard_map.141 = s32[64,8,384]{2,1,0:T(8,128)} custom-call(s32[3]{0:T(128)} %step_ref.1, f32[3,4,81,128]{3,2,1,0:T(8,128)} %copy.23.adj_ref, bf16[8,2,4,81,128]{4,3,2,1,0:T(8,128)(2,1)} %copy.24.c0_ref.c1_ref.c2_ref, bf16[8,2,4,81,128]{4,3,2,1,0:T(8,128)(2,1)} %copy.24.c0_ref.c1_ref.c2_ref, bf16[8,2,4,81,128]{4,3,2,1,0:T(8,128)(2,1)} %copy.24.c0_ref.c1_ref.c2_ref), custom_call_target="tpu_custom_call" | custom-call | tf_op jit(solution)/shard_map/pallas_call | solution.py:211
  23.4 0.6 pad_add_fusion.place_ref
  24.0 0.3 convolution_convert_fusion
  24.4 0.8 pad_maximum_fusion.1.back_ref
  25.1 7.3 %all-to-all-done.own_ref = s32[32,32,128]{2,1,0:T(8,128)S(1)} async-done(((s32[32,32,128]{2,1,0:T(8,128)}), s32[32,32,128]{2,1,0:T(8,128)S(1)}, u32[]{:S(2)}, u32[]{:S(2)}) %all-to-all-start) | async-done | bytes 524320 | tf_op jit(solution)/shard_map/all_to_all | solution.py:572
  32.5 7.2 %all-to-all-start.1 = ((s32[64,8,384]{2,1,0:T(8,128)}), s32[64,8,384]{2,1,0:T(8,128)S(1)}, u32[]{:S(2)}, u32[]{:S(2)}) async-start(s32[64,8,384]{2,1,0:T(8,128)} %shard_map.141), calls=%async_computation.1 | async-start | bytes 1572864 | tf_op jit(solution)/shard_map/all_to_all | solution.py:584
  39.8 2.1 %shard_map.142.own_ref = s32[896,128]{1,0:T(8,128)} custom-call(s32[32,32,128]{2,1,0:T(8,128)} %copy-done.2), custom_call_target="tpu_custom_call" | custom-call | tf_op jit(solution)/shard_map/pallas_call | solution.py:171
  41.9 1.2 collective-permute-start
  43.1 1.5 %collective-permute-start.2 = (s32[896,128]{1,0:T(8,128)}, s32[896,128]{1,0:T(8,128)S(1)}, u32[]{:S(2)}, u32[]{:S(2)}) collective-permute-start(s32[896,128]{1,0:T(8,128)} %shard_map.142.own_ref), channel_id=1, source_target_pairs={{0,3},{1,0},{2,1},{3,2},{4,7},{5,4},{6,5},{7,6},{8,11},{9,8},{10,9... | collective-permute-start | bytes 1376264 | tf_op jit(solution)/shard_map/ppermute | solution.py:563
  44.6 1.0 collective-permute-start.4
  45.6 9.4 %collective-permute-done.left_ref = s32[896,128]{1,0:T(8,128)S(1)} collective-permute-done((s32[896,128]{1,0:T(8,128)}, s32[896,128]{1,0:T(8,128)S(1)}, u32[]{:S(2)}, u32[]{:S(2)}) %collective-permute-start) | collective-permute-done | bytes 458784 | tf_op jit(solution)/shard_map/ppermute | solution.py:563
  54.9 1.3 collective-permute-start.5
  56.3 0.1 collective-permute-start.1
  56.3 0.0 collective-permute-done.2.right_ref
  56.4 2.7 %collective-permute-start.3 = (s32[448,128]{1,0:T(8,128)S(1)}, s32[448,128]{1,0:T(8,128)S(1)}, u32[]{:S(2)}, u32[]{:S(2)}) collective-permute-start(s32[448,128]{1,0:T(8,128)S(1)} %slice.19), channel_id=1, source_target_pairs={{0,3},{1,0},{2,1},{3,2},{4,7},{5,4},{6,5},{7,6},{8,11},{9,8},{10,9... | collective-permute-start | bytes 688136 | tf_op jit(solution)/shard_map/ppermute | solution.py:563
  59.1 0.6 collective-permute-start.6
  59.7 0.0 collective-permute-done.4.own2_ref
  59.7 0.0 collective-permute-done.5.left2_ref
  59.7 0.8 copy-done.7
  60.5 0.8 copy-done.8
  61.3 5.5 %shard_map.143.regrouped_ref = f32[7168,128]{1,0:T(8,128)} custom-call(s32[896,128]{1,0:T(8,128)} %shard_map.142.own_ref, s32[896,128]{1,0:T(8,128)} %copy-done.7, s32[896,128]{1,0:T(8,128)} %copy-done.4, s32[896,128]{1,0:T(8,128)} %copy-done.8), custom_call_target="tpu_custom_call" | custom-call | tf_op jit(solution)/shard_map/pallas_call | solution.py:280
  66.7 0.0 collective-permute-done.1.oa_ref
  66.8 0.0 collective-permute-done.3.ob_ref
  66.8 0.1 collective-permute-start.7
  66.9 0.5 collective-permute-start.8
  67.4 0.9 copy.27.fwd_ref
  68.3 0.0 all-to-all-done.1.r_ref
  68.3 0.9 copy-done.1
  69.2 3.4 %shard_map.144 = (f32[2,528,128]{2,1,0:T(8,128)}, f32[2,2,3,88,256]{4,3,2,1,0:T(8,128)}) custom-call(s32[2]{0:T(128)} %pad_add_fusion.place_ref, f32[2,128]{1,0:T(2,128)} %metric_ref.3, s32[64,8,384]{2,1,0:T(8,128)} %copy-done.1, bf16[768,256]{1,0:T(8,128)(2,1)} %copy.27.fwd_ref, bf16[352,88]{1,0:T(8,128)(2,1)} %constant.63.clone.both_ref), custom_call_target="tpu_custom_call" | custom-call | tf_op jit(solution)/shard_map/pallas_call | solution.py:340
  72.6 0.0 collective-permute-done.6.right2_ref
  72.6 0.0 collective-permute-done.7.oa2_ref
  72.7 0.0 collective-permute-done.8.ob2_ref
  72.7 0.7 copy-done.9
  73.4 0.1 copy-done.12
  73.5 0.1 copy-done.13
  73.6 18.4 %shard_map.145 = s32[64,4,384]{2,1,0:T(4,128)} custom-call(s32[2]{0:T(128)} %pad_add_fusion.place_ref, f32[2,128]{1,0:T(2,128)} %metric_ref.3, f32[7168,128]{1,0:T(8,128)} %shard_map.143.regrouped_ref, s32[896,128]{1,0:T(8,128)} %copy-done.5, s32[896,128]{1,0:T(8,128)} %copy-done.9, s32[448,128]{1,0:T(8,128)} %copy-done.10, s32[448,128]{1,0:T(8,128)} %copy-done.12, ...), custom_call_target="tpu_custom_call" | custom-call | tf_op jit(solution)/shard_map/pallas_call | solution.py:430
  92.0 25.4 %all_to_all.20.r_ref = s32[64,4,384]{2,1,0:T(4,128)} all-to-all(s32[64,4,384]{2,1,0:T(4,128)} %shard_map.145), channel_id=1, replica_groups=mesh['span'=64,'plane'=4] {'span'}, dimensions={0} | all-to-all | bytes 786432 | tf_op jit(solution)/shard_map/all_to_all | solution.py:595
  117.4 3.0 %shard_map.147.p0_ref = f32[4,1024]{1,0:T(4,128)} custom-call(s32[64,4,384]{2,1,0:T(4,128)} %all_to_all.20.r_ref, s32[1,2048]{1,0:T(1,128)} %bitcast.22, s32[1,2048]{1,0:T(1,128)} %bitcast.21), custom_call_target="tpu_custom_call" | custom-call | tf_op jit(solution)/shard_map/pallas_call | solution.py:471
  120.4 0.3 collective-permute-start.10
  120.7 0.9 collective-permute-start.11
  121.6 0.6 collective-permute-start.9
  122.2 2.5 %collective-permute-done.10.p2_ref = f32[4,1024]{1,0:T(4,128)S(1)} collective-permute-done((f32[4,1024]{1,0:T(4,128)}, f32[4,1024]{1,0:T(4,128)S(1)}, u32[]{:S(2)}, u32[]{:S(2)}) %collective-permute-start.10) | collective-permute-done | bytes 16416 | tf_op jit(solution)/shard_map/ppermute | solution.py:563
  124.7 0.0 collective-permute-done.11.p3_ref
  124.7 1.0 collective-permute-done.9.p1_ref
  125.7 0.6 copy-done.17
  126.3 1.5 %shard_map.148 = (f32[4,1024]{1,0:T(4,128)}, f32[64,1,128]{2,1,0:T(1,128)}) custom-call(f32[4,1024]{1,0:T(4,128)} %weight_ref.1, f32[4,1024]{1,0:T(4,128)} %shard_map.147.p0_ref, f32[4,1024]{1,0:T(4,128)} %copy-done.17, f32[4,1024]{1,0:T(4,128)} %copy-done.15, f32[4,1024]{1,0:T(4,128)} %copy-done.16), custom_call_target="tpu_custom_call" | custom-call | tf_op jit(solution)/shard_map/pallas_call | solution.py:493
  127.8 7.2 %all-to-all-start.3 = ((f32[64,1,128]{2,1,0:T(1,128)}), f32[64,1,128]{2,1,0:T(1,128)S(1)}, u32[]{:S(2)}, u32[]{:S(2)}) async-start(f32[64,1,128]{2,1,0:T(1,128)} %get-tuple-element.29), calls=%async_computation.3 | async-start | bytes 65536 | tf_op jit(solution)/shard_map/all_to_all | solution.py:600
  135.0 2.2 %shard_map.146 = f32[3,4,81,128]{3,2,1,0:T(8,128)} custom-call(s32[64,4,384]{2,1,0:T(4,128)} %all_to_all.20.r_ref), custom_call_target="tpu_custom_call" | custom-call | tf_op jit(solution)/shard_map/pallas_call | solution.py:532
  137.2 2.0 %copy.29 = f32[3,4,81,128]{3,1,2,0:T(4,128)} copy(f32[3,4,81,128]{3,2,1,0:T(8,128)} %shard_map.146) | data formatting | bytes 995328
  139.1 5.3 %all-to-all-done.3.squares_ref = f32[64,1,128]{2,1,0:T(1,128)S(1)} async-done(((f32[64,1,128]{2,1,0:T(1,128)}), f32[64,1,128]{2,1,0:T(1,128)S(1)}, u32[]{:S(2)}, u32[]{:S(2)}) %all-to-all-start.3) | async-done | bytes 32800 | tf_op jit(solution)/shard_map/all_to_all | solution.py:600
  144.4 0.6 copy-done.14
  145.0 1.5 %shard_map.149 = f32[4,256]{1,0:T(4,128)} custom-call(s32[1]{0:T(128)} %bitcast.7.plane_ref, f32[4,1024]{1,0:T(4,128)} %get-tuple-element.28.weighted_ref, f32[64,1,128]{2,1,0:T(1,128)} %copy-done.14), custom_call_target="tpu_custom_call" | custom-call | tf_op jit(solution)/shard_map/pallas_call | solution.py:513
  (42 shorter events, 0.2 us)
Async XLA Ops:
  0.6 0.9 copy-start
  0.6 15.6 %copy-start.18 = (s32[1024,2]{0,1:T(2,128)S(1)}, s32[1024,2]{0,1:T(2,128)}, u32[]{:S(2)}) copy-start(s32[1024,2]{0,1:T(2,128)} %param.18) | copy-start | bytes 24580
  0.7 16.2 %copy-start.3 = (bf16[8,2,4,81,128]{4,2,3,1,0:T(4,128)(2,1)S(1)}, bf16[8,2,4,81,128]{4,2,3,1,0:T(4,128)(2,1)}, u32[]{:S(2)}) copy-start(bf16[8,2,4,81,128]{4,2,3,1,0:T(4,128)(2,1)} %param.14) | copy-start | bytes 3981316
  4.2 28.3 %all-to-all-start = ((s32[32,32,128]{2,1,0:T(8,128)}), s32[32,32,128]{2,1,0:T(8,128)S(1)}, u32[]{:S(2)}, u32[]{:S(2)}) async-start(s32[32,32,128]{2,1,0:T(8,128)} %shard_map.140), calls=%async_computation | async-start | bytes 1048576 | tf_op jit(solution)/shard_map/all_to_all | solution.py:572
  16.2 2.0 %copy-start.6 = (f32[3,4,81,128]{3,1,2,0:T(4,128)S(1)}, f32[3,4,81,128]{3,1,2,0:T(4,128)}, u32[]{:S(2)}) copy-start(f32[3,4,81,128]{3,1,2,0:T(4,128)} %param.13) | copy-start | bytes 1492996
  16.9 2.2 %copy-start.19 = (s32[1024,2]{0,1:T(2,128)S(1)}, s32[1024,2]{0,1:T(2,128)}, u32[]{:S(2)}) copy-start(s32[1024,2]{0,1:T(2,128)} %param.19) | copy-start | bytes 24580
  19.7 4.3 %copy-start.20 = (s32[256]{0:T(256)S(1)}, s32[256]{0:T(256)}, u32[]{:S(2)}) copy-start(s32[256]{0:T(256)} %constant.61.clone) | copy-start | bytes 3076
  19.7 4.3 %copy-start.21 = (s32[256]{0:T(256)S(1)}, s32[256]{0:T(256)}, u32[]{:S(2)}) copy-start(s32[256]{0:T(256)} %constant.69) | copy-start | bytes 3076
  19.7 4.3 %copy-start.22 = (s32[256]{0:T(256)S(1)}, s32[256]{0:T(256)}, u32[]{:S(2)}) copy-start(s32[256]{0:T(256)} %constant.71) | copy-start | bytes 3076
  19.7 4.3 %copy-start.23 = (bf16[256,512]{1,0:T(8,128)(2,1)S(1)}, bf16[256,512]{1,0:T(8,128)(2,1)}, u32[]{:S(2)}) copy-start(bf16[256,512]{1,0:T(8,128)(2,1)} %constant.62.clone) | copy-start | bytes 786436
  32.5 7.3 %copy-start.2 = (s32[32,32,128]{2,1,0:T(8,128)}, s32[32,32,128]{2,1,0:T(8,128)S(1)}, u32[]{:S(2)}) copy-start(s32[32,32,128]{2,1,0:T(8,128)S(1)} %all-to-all-done.own_ref) | copy-start | bytes 1572868
  32.5 35.8 %all-to-all-start.1 = ((s32[64,8,384]{2,1,0:T(8,128)}), s32[64,8,384]{2,1,0:T(8,128)S(1)}, u32[]{:S(2)}, u32[]{:S(2)}) async-start(s32[64,8,384]{2,1,0:T(8,128)} %shard_map.141), calls=%async_computation.1 | async-start | bytes 1572864 | tf_op jit(solution)/shard_map/all_to_all | solution.py:584
  41.9 13.1 %collective-permute-start = (s32[896,128]{1,0:T(8,128)}, s32[896,128]{1,0:T(8,128)S(1)}, u32[]{:S(2)}, u32[]{:S(2)}) collective-permute-start(s32[896,128]{1,0:T(8,128)} %shard_map.142.own_ref), channel_id=1, source_target_pairs={{0,1},{1,2},{2,3},{3,0},{4,5},{5,6},{6,7},{7,4},{8,9},{9,10},{10,1... | collective-permute-start | bytes 1376264 | tf_op jit(solution)/shard_map/ppermute | solution.py:563
  43.1 13.3 %collective-permute-start.2 = (s32[896,128]{1,0:T(8,128)}, s32[896,128]{1,0:T(8,128)S(1)}, u32[]{:S(2)}, u32[]{:S(2)}) collective-permute-start(s32[896,128]{1,0:T(8,128)} %shard_map.142.own_ref), channel_id=1, source_target_pairs={{0,3},{1,0},{2,1},{3,2},{4,7},{5,4},{6,5},{7,6},{8,11},{9,8},{10,9... | collective-permute-start | bytes 1376264 | tf_op jit(solution)/shard_map/ppermute | solution.py:563
  44.6 15.1 %collective-permute-start.4 = (s32[896,128]{1,0:T(8,128)}, s32[896,128]{1,0:T(8,128)S(1)}, u32[]{:S(2)}, u32[]{:S(2)}) collective-permute-start(s32[896,128]{1,0:T(8,128)} %shard_map.142.own_ref), channel_id=1, source_target_pairs={{0,4},{4,0},{8,12},{12,8},{16,20},{20,16},{24,28},{28,24},{32,36},... | collective-permute-start | bytes 1376264 | tf_op jit(solution)/shard_map/ppermute | solution.py:568
  54.9 4.8 %copy-start.4 = (s32[896,128]{1,0:T(8,128)}, s32[896,128]{1,0:T(8,128)S(1)}, u32[]{:S(2)}) copy-start(s32[896,128]{1,0:T(8,128)S(1)} %collective-permute-done.left_ref) | copy-start | bytes 1376260
  54.9 4.7 %collective-permute-start.5 = (s32[896,128]{1,0:T(8,128)S(1)}, s32[896,128]{1,0:T(8,128)S(1)}, u32[]{:S(2)}, u32[]{:S(2)}) collective-permute-start(s32[896,128]{1,0:T(8,128)S(1)} %collective-permute-done.left_ref), channel_id=1, source_target_pairs={{0,4},{4,0},{8,12},{12,8},{16,20},{20,16},{24,28},{28,24},{32,36},... | collective-permute-start | bytes 1376264 | tf_op jit(solution)/shard_map/ppermute | solution.py:568
  56.3 10.5 %collective-permute-start.1 = (s32[448,128]{1,0:T(8,128)S(1)}, s32[448,128]{1,0:T(8,128)S(1)}, u32[]{:S(2)}, u32[]{:S(2)}) collective-permute-start(s32[448,128]{1,0:T(8,128)S(1)} %slice.18), channel_id=1, source_target_pairs={{0,1},{1,2},{2,3},{3,0},{4,5},{5,6},{6,7},{7,4},{8,9},{9,10},{10,1... | collective-permute-start | bytes 688136 | tf_op jit(solution)/shard_map/ppermute | solution.py:563
  56.4 10.4 %copy-start.5 = (s32[896,128]{1,0:T(8,128)}, s32[896,128]{1,0:T(8,128)S(1)}, u32[]{:S(2)}) copy-start(s32[896,128]{1,0:T(8,128)S(1)} %collective-permute-done.2.right_ref) | copy-start | bytes 1376260
  56.4 10.4 %collective-permute-start.3 = (s32[448,128]{1,0:T(8,128)S(1)}, s32[448,128]{1,0:T(8,128)S(1)}, u32[]{:S(2)}, u32[]{:S(2)}) collective-permute-start(s32[448,128]{1,0:T(8,128)S(1)} %slice.19), channel_id=1, source_target_pairs={{0,3},{1,0},{2,1},{3,2},{4,7},{5,4},{6,5},{7,6},{8,11},{9,8},{10,9... | collective-permute-start | bytes 688136 | tf_op jit(solution)/shard_map/ppermute | solution.py:563
  59.1 13.5 %collective-permute-start.6 = (s32[896,128]{1,0:T(8,128)S(1)}, s32[896,128]{1,0:T(8,128)S(1)}, u32[]{:S(2)}, u32[]{:S(2)}) collective-permute-start(s32[896,128]{1,0:T(8,128)S(1)} %collective-permute-done.2.right_ref), channel_id=1, source_target_pairs={{0,4},{4,0},{8,12},{12,8},{16,20},{20,16},{24,28},{28,24},{32,36},... | collective-permute-start | bytes 1376264 | tf_op jit(solution)/shard_map/ppermute | solution.py:568
  59.7 0.8 copy-start.7
  60.5 0.8 copy-start.8
  66.7 5.9 %copy-start.10 = (s32[448,128]{1,0:T(8,128)}, s32[448,128]{1,0:T(8,128)S(1)}, u32[]{:S(2)}) copy-start(s32[448,128]{1,0:T(8,128)S(1)} %collective-permute-done.1.oa_ref) | copy-start | bytes 688132
  66.8 5.9 %copy-start.11 = (s32[448,128]{1,0:T(8,128)}, s32[448,128]{1,0:T(8,128)S(1)}, u32[]{:S(2)}) copy-start(s32[448,128]{1,0:T(8,128)S(1)} %collective-permute-done.3.ob_ref) | copy-start | bytes 688132
  66.8 5.9 %collective-permute-start.7 = (s32[448,128]{1,0:T(8,128)S(1)}, s32[448,128]{1,0:T(8,128)S(1)}, u32[]{:S(2)}, u32[]{:S(2)}) collective-permute-start(s32[448,128]{1,0:T(8,128)S(1)} %collective-permute-done.1.oa_ref), channel_id=1, source_target_pairs={{0,4},{4,0},{8,12},{12,8},{16,20},{20,16},{24,28},{28,24},{32,36},... | collective-permute-start | bytes 688136 | tf_op jit(solution)/shard_map/ppermute | solution.py:568
  66.9 5.8 %collective-permute-start.8 = (s32[448,128]{1,0:T(8,128)S(1)}, s32[448,128]{1,0:T(8,128)S(1)}, u32[]{:S(2)}, u32[]{:S(2)}) collective-permute-start(s32[448,128]{1,0:T(8,128)S(1)} %collective-permute-done.3.ob_ref), channel_id=1, source_target_pairs={{0,4},{4,0},{8,12},{12,8},{16,20},{20,16},{24,28},{28,24},{32,36},... | collective-permute-start | bytes 688136 | tf_op jit(solution)/shard_map/ppermute | solution.py:568
  68.3 0.9 copy-start.1
  72.6 0.8 copy-start.9
  72.7 0.8 copy-start.12
  72.7 0.9 copy-start.13
  120.4 4.3 %collective-permute-start.10 = (f32[4,1024]{1,0:T(4,128)}, f32[4,1024]{1,0:T(4,128)S(1)}, u32[]{:S(2)}, u32[]{:S(2)}) collective-permute-start(f32[4,1024]{1,0:T(4,128)} %shard_map.147.p0_ref), channel_id=1, source_target_pairs={{0,2},{1,3},{2,0},{3,1},{4,6},{5,7},{6,4},{7,5},{8,10},{9,11},{10,... | collective-permute-start | bytes 49160 | tf_op jit(solution)/shard_map/ppermute | solution.py:563
  120.7 4.0 %collective-permute-start.11 = (f32[4,1024]{1,0:T(4,128)}, f32[4,1024]{1,0:T(4,128)S(1)}, u32[]{:S(2)}, u32[]{:S(2)}) collective-permute-start(f32[4,1024]{1,0:T(4,128)} %shard_map.147.p0_ref), channel_id=1, source_target_pairs={{0,3},{1,0},{2,1},{3,2},{4,7},{5,4},{6,5},{7,6},{8,11},{9,8},{10,9... | collective-permute-start | bytes 49160 | tf_op jit(solution)/shard_map/ppermute | solution.py:563
  121.6 4.1 %collective-permute-start.9 = (f32[4,1024]{1,0:T(4,128)}, f32[4,1024]{1,0:T(4,128)S(1)}, u32[]{:S(2)}, u32[]{:S(2)}) collective-permute-start(f32[4,1024]{1,0:T(4,128)} %shard_map.147.p0_ref), channel_id=1, source_target_pairs={{0,1},{1,2},{2,3},{3,0},{4,5},{5,6},{6,7},{7,4},{8,9},{9,10},{10,1... | collective-permute-start | bytes 49160 | tf_op jit(solution)/shard_map/ppermute | solution.py:563
  124.7 1.0 copy-start.15
  124.7 1.0 copy-start.16
  125.7 0.6 copy-start.17
  127.8 16.6 %all-to-all-start.3 = ((f32[64,1,128]{2,1,0:T(1,128)}), f32[64,1,128]{2,1,0:T(1,128)S(1)}, u32[]{:S(2)}, u32[]{:S(2)}) async-start(f32[64,1,128]{2,1,0:T(1,128)} %get-tuple-element.29), calls=%async_computation.3 | async-start | bytes 65536 | tf_op jit(solution)/shard_map/all_to_all | solution.py:600
  144.4 0.6 copy-start.14

commit v7 on v6

--- a/solution.py
+++ b/solution.py
@@ -14,7 +14,7 @@
 NSTEP = 3
 HIGHEST = lax.Precision.HIGHEST
 F32 = jnp.float32
-VMEM_BYTES = 56 * 1024 * 1024
+VMEM_BYTES = 12 * 1024 * 1024
 LEVELS = 32767.0
 SCALE_LANE = 250
 LINES = 56
@@ -70,14 +70,14 @@
     chip, lane_core, shift = (jnp.asarray(v) for v in lane_order())
     span_of = 2 * chip + lane_core + core * (1 - 2 * lane_core)
     order = 4 * span_of + (plane + shift) % 4
-    pick = jnp.where(order[:, None] == jnp.arange(256)[None, :], 1.0, 0.0).astype(jnp.bfloat16)
+    index = jnp.arange(256)
+    pick = jnp.where(order[:, None] == index[None, :], 1.0, 0.0).astype(jnp.bfloat16)
+    pick_turned = jnp.where(index[:, None] == order[None, :], 1.0, 0.0).astype(jnp.bfloat16)
     both = jnp.asarray(np.concatenate([high, low], axis=1))
     back = jnp.dot(pick, both, preferred_element_type=F32).astype(jnp.bfloat16)
-    high, low = back[:, :256], back[:, 256:]
-    return (
-        jnp.concatenate([high.T, high.T, low.T], axis=0),
-        jnp.concatenate([high, high, low], axis=0),
-    )
+    both = jnp.asarray(np.ascontiguousarray(np.concatenate([high, high, low], axis=1).T))
+    fwd = jnp.dot(both, pick_turned, preferred_element_type=F32).astype(jnp.bfloat16)
+    return fwd, jnp.concatenate([back[:, :256], back[:, :256], back[:, 256:]], axis=0)
 
 
 def slope_table():
@@ -97,8 +97,8 @@
     return pl.BlockSpec(memory_space=pltpu.SMEM)
 
 
-def params():
-    return pltpu.CompilerParams(vmem_limit_bytes=VMEM_BYTES)
+def params(size=VMEM_BYTES):
+    return pltpu.CompilerParams(vmem_limit_bytes=size)
 
 
 def pair_up(low, high):
@@ -121,8 +121,10 @@
     return (pair >> 16).astype(F32)
 
 
-def pack_inverse_kernel(h_ref, o_ref, w_ref, f_ref):
-    h = h_ref[...]
+def pack_inverse_kernel(plane_ref, h_ref, o_ref, w_ref, f_ref):
+    h = h_ref[:, 0, :]
+    for k in range(1, h_ref.shape[1]):
+        h = jnp.where(plane_ref[0] == k, h_ref[:, k, :], h)
     largest = jnp.max(jnp.abs(h), axis=1, keepdims=True)
     code = jnp.floor(largest * 2.0**30) + 1.0
     upper = jnp.floor(code * 2.0**-15)
@@ -150,15 +152,15 @@
     o_ref[...] = jnp.broadcast_to(pair[None], o_ref.shape)
 
 
-def pack_inverse(matrix, targets):
+def pack_inverse(plane, inverse, targets):
     return pl.pallas_call(
         pack_inverse_kernel,
         out_shape=jax.ShapeDtypeStruct((targets, 32, 128), jnp.int32),
-        in_specs=[vmem_spec()],
+        in_specs=[smem_spec(), vmem_spec()],
         out_specs=vmem_spec(),
         scratch_shapes=[pltpu.VMEM((128, 128), F32), pltpu.VMEM((64, 128), F32)],
         compiler_params=params(),
-    )(matrix)
+    )(plane, inverse.transpose(1, 0, 2))
 
 
 def turn_kernel(own_ref, o_ref):
@@ -268,20 +270,30 @@
     ) * (2.0**-30 / LEVELS)
 
 
-def regroup_kernel(own_ref, own2_ref, left_ref, left2_ref, o_ref):
-    def spread(k, carry):
-        spread_rows([(r, 0) for r in (own_ref, own2_ref, left_ref, left2_ref)], k, o_ref)
-        return carry
-
-    lax.fori_loop(0, 28, spread, 0, unroll=7)
+def regroup_kernel(own_ref, own2_ref, left_ref, left2_ref, o_ref, ht, sems):
+    copies = []
+    for g in range(LINES // 8):
+        for k in range(4 * g, 4 * g + 4):
+            spread_rows([(r, 0) for r in (own_ref, own2_ref, left_ref, left2_ref)], k, ht)
+        for part in range(2):
+            block = pl.ds(g * 512 + part * LINES * 64, 512)
+            copy = pltpu.make_async_copy(ht.at[block, :], o_ref.at[block, :], sems.at[g, part])
+            copy.start()
+            copies.append(copy)
+    for copy in copies:
+        copy.wait()
 
 
 def regroup_half(pieces):
     return pl.pallas_call(
         regroup_kernel,
-        out_shape=jax.ShapeDtypeStruct((LINES * 128, 128), F32),
+        out_shape=pltpu.HBM((LINES * 128, 128), F32),
         in_specs=[vmem_spec()] * 4,
-        out_specs=vmem_spec(),
+        out_specs=pl.BlockSpec(memory_space=pltpu.HBM),
+        scratch_shapes=[
+            pltpu.VMEM((LINES * 128, 128), F32),
+            pltpu.SemaphoreType.DMA((LINES // 8, 2)),
+        ],
         compiler_params=params(),
     )(*pieces)
 
@@ -430,7 +442,7 @@
     return pl.pallas_call(
         steps_kernel,
         out_shape=jax.ShapeDtypeStruct((64, 4, 384), jnp.int32),
-        in_specs=[smem_spec(), smem_spec(), pl.BlockSpec(memory_space=pl.ANY)]
+        in_specs=[smem_spec(), smem_spec(), pl.BlockSpec(memory_space=pltpu.HBM)]
         + [vmem_spec()] * (len(pieces) + 5),
         out_specs=vmem_spec(),
         scratch_shapes=[
@@ -445,7 +457,7 @@
             pltpu.VMEM((256, 256), jnp.int32),
             pltpu.SemaphoreType.DMA,
         ],
-        compiler_params=params(),
+        compiler_params=params(2 * VMEM_BYTES),
     )(place, metric, regrouped, *pieces, first, velocity, fwd, back, both)
 
 
@@ -567,10 +579,10 @@
     def across(block):
         return lax.ppermute(block, "span", [(i, i ^ 1) for i in range(span_count)])
 
-    matrix = lax.dynamic_index_in_dim(helmholtz_inverse, plane, 0, keepdims=False)
+    which = plane.reshape(1).astype(jnp.int32)
     same_core = [list(range(c, span_count, 2)) for c in range(2)]
     own = lax.all_to_all(
-        pack_inverse(matrix, span_count // 2), "span", 0, 0, tiled=True, axis_index_groups=same_core
+        pack_inverse(which, helmholtz_inverse, span_count // 2), "span", 0, 0, tiled=True, axis_index_groups=same_core
     )
     local = wall_local.T.reshape(1, 2 * wall_count)
     element = wall_element.T.reshape(1, 2 * wall_count) - plane * adjoint.shape[3]
@@ -591,6 +603,7 @@
     oa, ob, regrouped = lax.optimization_barrier((oa, ob, regrouped))
     for piece in (oa, ob):
         pieces += [piece, across(piece)]
+    regrouped = pltpu.with_memory_space_constraint(regrouped, pltpu.HBM)
     out = steps(place, metric, regrouped, pieces, first, velocity, fwd, back, both)
     received = lax.all_to_all(out, "span", 0, 0, tiled=True)
 
@@ -599,7 +612,7 @@
     weighted, square = weigh(wall_weight, parts, span_count)
     squares = lax.all_to_all(square, "span", 0, 0, tiled=True)
     gradient = share(
-        plane.reshape(1).astype(jnp.int32),
+        which,
         weighted,
         squares,
         wall_count // plane_count,

time: 147 us -> 133 us (0.905)
  Pallas kernels: 43.2 us -> 28.9 us
  local copies, waits for them, and re-layouts: 12.6 us -> 3.87 us
  waiting for transfers between devices: 25.5 us -> 33.4 us
  starting transfers between devices: 37.2 us -> 39.1 us
    unnamed x54 -> x31, local copies, waits for them, and re-layouts: 11.5 us -> 3.82 us
    all_to_all x1, waiting for transfers between devices: 7.34 us -> 11.2 us  [on_device(): lax.all_to_all(pack_inverse(which, helmholtz_inverse, span_count // 2), '...]
    all_to_all x1, waiting for transfers between devices: 5.27 us -> 8.04 us  [on_device(): squares = lax.all_to_all(square, 'span', 0, 0, tiled=True)]
    pallas_call x1, Pallas kernels: 5.48 us -> 3.45 us  [regroup_half(): pl.pallas_call(regroup_kernel, out_shape=pltpu.HBM((LINES * 128, 128), F3...]
    pallas_call x1, Pallas kernels: 18.4 us -> 16.4 us  [steps(): pl.pallas_call(steps_kernel, out_shape=jax.ShapeDtypeStruct((64, 4, 384),...]
    ppermute x7, starting transfers between devices: 7.27 us -> 9.13 us  [around(): lax.ppermute(block, 'plane', [(i, (i + step) % plane_count) for i in rang...]
    pallas_call x1, Pallas kernels: 2.12 us -> 0.31 us  [turn_own(): pl.pallas_call(turn_kernel, out_shape=jax.ShapeDtypeStruct((LINES // 8 *...]
    pallas_call x1, Pallas kernels: 2.16 us -> 0.42 us  [unpack(): pl.pallas_call(unpack_kernel, out_shape=jax.ShapeDtypeStruct((3, 4, Q, 12...]
  transfers between devices with their start and end apart: 15 -> 15, of which waited for: 5 -> 7; matrix products, arithmetic and copies ran while one was open for 5% -> 2% of each run, Pallas kernels for 12% -> 6%
where the time goes in v7:
time: 133 us; the launch traced here: 132 us
  starting transfers between devices  39.1 us (29%)
  waiting for transfers between devices  33.4 us (25%)
  Pallas kernels  28.9 us (22%)
  blocking collectives  25.3 us (19%)
  local copies, waits for them, and re-layouts  3.87 us (3%)
    all_to_all x1, blocking collectives, on_device(): received = lax.all_to_all(out, 'span', 0, 0, tiled=True)  25.3 us
    pallas_call x1, Pallas kernels, steps(): pl.pallas_call(steps_kernel, out_shape=jax.ShapeDtypeStruct((64, 4, 384),...  16.4 us
    ppermute x7, waiting for transfers between devices, around(): lax.ppermute(block, 'plane', [(i, (i + step) % plane_count) for i in rang...  14.1 us
    all_to_all x1, starting transfers between devices, on_device(): lax.all_to_all(pack_inverse(which, helmholtz_inverse, span_count // 2), '...  12 us
    all_to_all x1, waiting for transfers between devices, on_device(): lax.all_to_all(pack_inverse(which, helmholtz_inverse, span_count // 2), '...  11.2 us
    ppermute x7, starting transfers between devices, around(): lax.ppermute(block, 'plane', [(i, (i + step) % plane_count) for i in rang...  9.13 us
    all_to_all x1, waiting for transfers between devices, on_device(): squares = lax.all_to_all(square, 'span', 0, 0, tiled=True)  8.04 us
    all_to_all x1, starting transfers between devices, on_device(): points = lax.all_to_all(sent, 'span', 0, 0, tiled=True)  7.24 us
  transfers between devices with their start and end apart: 15, of which 7 were waited for; matrix products, arithmetic and copies ran while one was open for 2% of the time, Pallas kernels for 6%

profile of v7, /device:TPU:1, one launch (start us, length us, event | category | flops | bytes accessed | tf_op | source)
XLA Modules:
  0.0 132.1 jit_solution(9062492915553356545)
XLA Ops:
  0.6 0.0 copy-start.7
  0.6 0.0 copy-start.1
  0.7 0.9 copy-done.1
  1.6 1.2 shard_map.149
  2.8 12.0 %all-to-all-start = ((s32[32,32,128]{2,1,0:T(8,128)}), s32[32,32,128]{2,1,0:T(8,128)S(1)}, u32[]{:S(2)}, u32[]{:S(2)}) async-start(s32[32,32,128]{2,1,0:T(8,128)} %shard_map.149), calls=%async_computation | async-start | bytes 1048576 | tf_op jit(solution)/shard_map/all_to_all | solution.py:584
  14.9 0.0 copy-done.7
  14.9 0.0 copy-done.5
  14.9 0.0 copy-start.8
  14.9 0.0 copy-start.4
  14.9 0.2 copy.17.c0_ref.c1_ref.c2_ref
  15.2 1.1 copy.16.adj_ref
  16.2 0.0 copy-done.8
  16.3 0.1 pad_add_fusion.place_ref
  16.3 0.0 copy-done.4
  16.4 0.0 copy-start.12
  16.4 2.2 %shard_map.150 = s32[64,8,384]{2,1,0:T(8,128)} custom-call(s32[3]{0:T(128)S(1)} %copy-done.4, f32[3,4,81,128]{3,2,1,0:T(8,128)S(1)} %copy.16.adj_ref, bf16[8,2,4,81,128]{4,3,2,1,0:T(8,128)(2,1)S(1)} %copy.17.c0_ref.c1_ref.c2_ref, bf16[8,2,4,81,128]{4,3,2,1,0:T(8,128)(2,1)S(1)} %copy.17.c0_ref.c1_ref.c2_ref, ...), custom_call_target="tpu_custom_call" | custom-call | tf_op jit(solution)/shard_map/pallas_call | solution.py:213
  18.6 0.0 copy-done.9
  18.6 0.0 copy-done.10
  18.7 0.3 convolution_convert_fusion.1
  19.0 0.6 copy-done.6
  19.6 0.3 fusion.fwd_ref
  19.9 11.2 %all-to-all-done.own_ref = s32[32,32,128]{2,1,0:T(8,128)S(1)} async-done(((s32[32,32,128]{2,1,0:T(8,128)}), s32[32,32,128]{2,1,0:T(8,128)S(1)}, u32[]{:S(2)}, u32[]{:S(2)}) %all-to-all-start) | async-done | bytes 524320 | tf_op jit(solution)/shard_map/all_to_all | solution.py:584
  31.1 7.2 %all-to-all-start.1 = ((s32[64,8,384]{2,1,0:T(8,128)}), s32[64,8,384]{2,1,0:T(8,128)S(1)}, u32[]{:S(2)}, u32[]{:S(2)}) async-start(s32[64,8,384]{2,1,0:T(8,128)} %shard_map.150), calls=%async_computation.1 | async-start | bytes 1572864 | tf_op jit(solution)/shard_map/all_to_all | solution.py:596
  38.4 0.3 shard_map.151.own_ref
  38.7 1.3 collective-permute-start
  40.0 1.5 %collective-permute-start.2 = (s32[896,128]{1,0:T(8,128)S(1)}, s32[896,128]{1,0:T(8,128)S(1)}, u32[]{:S(2)}, u32[]{:S(2)}) collective-permute-start(s32[896,128]{1,0:T(8,128)S(1)} %shard_map.151.own_ref), channel_id=1, source_target_pairs={{0,3},{1,0},{2,1},{3,2},{4,7},{5,4},{6,5},{7,6},{8,11},{9,8},{10,9... | collective-permute-start | bytes 1376264 | tf_op jit(solution)/shard_map/ppermute | solution.py:575
  41.4 1.0 collective-permute-start.4
  42.5 9.2 %collective-permute-done.left_ref = s32[896,128]{1,0:T(8,128)S(1)} collective-permute-done((s32[896,128]{1,0:T(8,128)S(1)}, s32[896,128]{1,0:T(8,128)S(1)}, u32[]{:S(2)}, u32[]{:S(2)}) %collective-permute-start) | collective-permute-done | bytes 458784 | tf_op jit(solution)/shard_map/ppermute | solution.py:575
  51.6 1.3 collective-permute-start.5
  52.9 0.1 collective-permute-start.1
  53.0 0.0 collective-permute-done.2.right_ref
  53.1 0.0 copy-start
  53.1 0.0 copy-start.3
  53.1 2.7 %collective-permute-start.3 = (s32[448,128]{1,0:T(8,128)S(1)}, s32[448,128]{1,0:T(8,128)}, u32[]{:S(2)}, u32[]{:S(2)}) collective-permute-start(s32[448,128]{1,0:T(8,128)S(1)} %slice.20), channel_id=1, source_target_pairs={{0,3},{1,0},{2,1},{3,2},{4,7},{5,4},{6,5},{7,6},{8,11},{9,8},{10,9... | collective-permute-start | bytes 688136 | tf_op jit(solution)/shard_map/ppermute | solution.py:575
  55.8 0.6 collective-permute-start.6
  56.4 0.0 collective-permute-done.4.own2_ref
  56.4 0.0 collective-permute-done.5.left2_ref
  56.4 3.5 %shard_map.152.regrouped_ref = f32[7168,128]{1,0:T(8,128)} custom-call(s32[896,128]{1,0:T(8,128)S(1)} %shard_map.151.own_ref, s32[896,128]{1,0:T(8,128)S(1)} %collective-permute-done.4.own2_ref, s32[896,128]{1,0:T(8,128)S(1)} %collective-permute-done.left_ref, s32[896,128]{1,0:T(8,128)S(1)} %collective-permute-done.5.left2_ref), custom_call_target="tpu_custom_call" | custom-call | tf_op jit(solution)/shard_map/pallas_call | solution.py:288
  59.8 1.6 %collective-permute-done.1.oa_ref = s32[448,128]{1,0:T(8,128)S(1)} collective-permute-done((s32[448,128]{1,0:T(8,128)S(1)}, s32[448,128]{1,0:T(8,128)S(1)}, u32[]{:S(2)}, u32[]{:S(2)}) %collective-permute-start.1) | collective-permute-done | bytes 229408 | tf_op jit(solution)/shard_map/ppermute | solution.py:575
  61.4 0.0 collective-permute-done.3.ob_ref
  61.5 0.8 collective-permute-start.7
  62.2 0.0 collective-permute-start.8
  62.2 0.0 all-to-all-done.1.r_ref
  62.2 0.0 copy-done.3
  62.3 1.9 %shard_map.153 = (f32[2,528,128]{2,1,0:T(8,128)S(1)}, f32[2,2,3,88,256]{4,3,2,1,0:T(8,128)S(1)}) custom-call(s32[2]{0:T(128)S(1)} %pad_add_fusion.place_ref, f32[2,128]{1,0:T(2,128)S(1)} %copy-done.3, s32[64,8,384]{2,1,0:T(8,128)S(1)} %all-to-all-done.1.r_ref, bf16[768,256]{1,0:T(8,128)(2,1)S(1)} %fusion.fwd_ref, bf16[352,88]{1,0:T(8,128)(2,1)S(1)} %copy-done), custom_call_target="tpu_custom_call" | custom-call | tf_op jit(solution)/shard_map/pallas_call | solution.py:352
  64.2 0.0 collective-permute-done.6.right2_ref
  64.2 0.0 collective-permute-done.7.oa2_ref
  64.2 0.0 collective-permute-done.8.ob2_ref
  64.2 0.0 copy-start.2
  64.2 16.4 %shard_map.154 = s32[64,4,384]{2,1,0:T(4,128)S(1)} custom-call(s32[2]{0:T(128)S(1)} %pad_add_fusion.place_ref, f32[2,128]{1,0:T(2,128)S(1)} %copy-done.3, f32[7168,128]{1,0:T(8,128)} %shard_map.152.regrouped_ref, s32[896,128]{1,0:T(8,128)S(1)} %collective-permute-done.2.right_ref, s32[896,128]{1,0:T(8,128)S(1)} %collective-permute-done.6.right2_ref, ...), custom_call_target="tpu_custom_call" | custom-call | tf_op jit(solution)/shard_map/pallas_call | solution.py:442
  80.7 25.3 %all_to_all.20.r_ref = s32[64,4,384]{2,1,0:T(4,128)S(1)} all-to-all(s32[64,4,384]{2,1,0:T(4,128)S(1)} %shard_map.154), channel_id=1, replica_groups=mesh['span'=64,'plane'=4] {'span'}, dimensions={0} | all-to-all | bytes 786432 | tf_op jit(solution)/shard_map/all_to_all | solution.py:608
  106.0 1.5 %shard_map.156.p0_ref = f32[4,1024]{1,0:T(4,128)S(1)} custom-call(s32[64,4,384]{2,1,0:T(4,128)S(1)} %all_to_all.20.r_ref, s32[1,2048]{1,0:T(1,128)S(1)} %bitcast.19, s32[1,2048]{1,0:T(1,128)S(1)} %bitcast.18), custom_call_target="tpu_custom_call" | custom-call | tf_op jit(solution)/shard_map/pallas_call | solution.py:483
  107.4 1.6 %collective-permute-start.10 = (f32[4,1024]{1,0:T(4,128)S(1)}, f32[4,1024]{1,0:T(4,128)S(1)}, u32[]{:S(2)}, u32[]{:S(2)}) collective-permute-start(f32[4,1024]{1,0:T(4,128)S(1)} %shard_map.156.p0_ref), channel_id=1, source_target_pairs={{0,2},{1,3},{2,0},{3,1},{4,6},{5,7},{6,4},{7,5},{8,10},{9,11},{10,... | collective-permute-start | bytes 49160 | tf_op jit(solution)/shard_map/ppermute | solution.py:575
  109.0 1.5 %collective-permute-start.11 = (f32[4,1024]{1,0:T(4,128)S(1)}, f32[4,1024]{1,0:T(4,128)S(1)}, u32[]{:S(2)}, u32[]{:S(2)}) collective-permute-start(f32[4,1024]{1,0:T(4,128)S(1)} %shard_map.156.p0_ref), channel_id=1, source_target_pairs={{0,3},{1,0},{2,1},{3,2},{4,7},{5,4},{6,5},{7,6},{8,11},{9,8},{10,9... | collective-permute-start | bytes 49160 | tf_op jit(solution)/shard_map/ppermute | solution.py:575
  110.5 0.5 collective-permute-start.9
  111.0 0.6 collective-permute-done.10.p2_ref
  111.6 1.0 collective-permute-done.11.p3_ref
  112.6 1.7 %collective-permute-done.9.p1_ref = f32[4,1024]{1,0:T(4,128)S(1)} collective-permute-done((f32[4,1024]{1,0:T(4,128)S(1)}, f32[4,1024]{1,0:T(4,128)S(1)}, u32[]{:S(2)}, u32[]{:S(2)}) %collective-permute-start.9) | collective-permute-done | bytes 16416 | tf_op jit(solution)/shard_map/ppermute | solution.py:575
  114.3 0.7 shard_map.157
  115.0 7.0 %all-to-all-start.3 = ((f32[64,1,128]{2,1,0:T(1,128)}), f32[64,1,128]{2,1,0:T(1,128)S(1)}, u32[]{:S(2)}, u32[]{:S(2)}) async-start(f32[64,1,128]{2,1,0:T(1,128)} %get-tuple-element.29), calls=%async_computation.3 | async-start | bytes 65536 | tf_op jit(solution)/shard_map/all_to_all | solution.py:613
  122.1 0.4 shard_map.155
  122.5 0.9 copy.21
  123.4 8.0 %all-to-all-done.3.squares_ref = f32[64,1,128]{2,1,0:T(1,128)S(1)} async-done(((f32[64,1,128]{2,1,0:T(1,128)}), f32[64,1,128]{2,1,0:T(1,128)S(1)}, u32[]{:S(2)}, u32[]{:S(2)}) %all-to-all-start.3) | async-done | bytes 32800 | tf_op jit(solution)/shard_map/all_to_all | solution.py:613
  131.4 0.7 shard_map.158
  (17 shorter events, 0.1 us)
Async XLA Ops:
  0.6 14.2 %copy-start.7 = (s32[1024,2]{0,1:T(2,128)S(1)}, s32[1024,2]{0,1:T(2,128)}, u32[]{:S(2)}) copy-start(s32[1024,2]{0,1:T(2,128)} %param.19) | copy-start | bytes 24580
  0.6 0.9 copy-start.1
  1.6 13.3 %copy-start.5 = (bf16[8,2,4,81,128]{4,2,3,1,0:T(4,128)(2,1)S(1)}, bf16[8,2,4,81,128]{4,2,3,1,0:T(4,128)(2,1)}, u32[]{:S(2)}) copy-start(bf16[8,2,4,81,128]{4,2,3,1,0:T(4,128)(2,1)} %param.15) | copy-start | bytes 3981316
  2.8 28.3 %all-to-all-start = ((s32[32,32,128]{2,1,0:T(8,128)}), s32[32,32,128]{2,1,0:T(8,128)S(1)}, u32[]{:S(2)}, u32[]{:S(2)}) async-start(s32[32,32,128]{2,1,0:T(8,128)} %shard_map.149), calls=%async_computation | async-start | bytes 1048576 | tf_op jit(solution)/shard_map/all_to_all | solution.py:584
  14.9 1.3 %copy-start.8 = (s32[1024,2]{0,1:T(2,128)S(1)}, s32[1024,2]{0,1:T(2,128)}, u32[]{:S(2)}) copy-start(s32[1024,2]{0,1:T(2,128)} %param.20) | copy-start | bytes 24580
  14.9 1.4 %copy-start.4 = (s32[3]{0:T(128)S(1)}, s32[3]{0:T(128)}, u32[]{:S(2)}) copy-start(s32[3]{0:T(128)} %step_ref.1) | copy-start | bytes 40
  16.3 2.3 %copy-start.9 = (s32[256]{0:T(256)S(1)}, s32[256]{0:T(256)}, u32[]{:S(2)}) copy-start(s32[256]{0:T(256)} %constant.59.clone) | copy-start | bytes 3076
  16.3 2.3 %copy-start.10 = (s32[256]{0:T(256)S(1)}, s32[256]{0:T(256)}, u32[]{:S(2)}) copy-start(s32[256]{0:T(256)} %constant.68) | copy-start | bytes 3076
  16.4 2.3 %copy-start.11 = (s32[256]{0:T(256)S(1)}, s32[256]{0:T(256)}, u32[]{:S(2)}) copy-start(s32[256]{0:T(256)} %constant.70) | copy-start | bytes 3076
  16.4 2.3 %copy-start.12 = (bf16[256,512]{1,0:T(8,128)(2,1)S(1)}, bf16[256,512]{1,0:T(8,128)(2,1)}, u32[]{:S(2)}) copy-start(bf16[256,512]{1,0:T(8,128)(2,1)} %constant.60.clone) | copy-start | bytes 786436
  18.6 1.0 copy-start.6
  31.1 31.1 %all-to-all-start.1 = ((s32[64,8,384]{2,1,0:T(8,128)}), s32[64,8,384]{2,1,0:T(8,128)S(1)}, u32[]{:S(2)}, u32[]{:S(2)}) async-start(s32[64,8,384]{2,1,0:T(8,128)} %shard_map.150), calls=%async_computation.1 | async-start | bytes 1572864 | tf_op jit(solution)/shard_map/all_to_all | solution.py:596
  38.7 12.9 %collective-permute-start = (s32[896,128]{1,0:T(8,128)S(1)}, s32[896,128]{1,0:T(8,128)S(1)}, u32[]{:S(2)}, u32[]{:S(2)}) collective-permute-start(s32[896,128]{1,0:T(8,128)S(1)} %shard_map.151.own_ref), channel_id=1, source_target_pairs={{0,1},{1,2},{2,3},{3,0},{4,5},{5,6},{6,7},{7,4},{8,9},{9,10},{10,1... | collective-permute-start | bytes 1376264 | tf_op jit(solution)/shard_map/ppermute | solution.py:575
  40.0 13.0 %collective-permute-start.2 = (s32[896,128]{1,0:T(8,128)S(1)}, s32[896,128]{1,0:T(8,128)S(1)}, u32[]{:S(2)}, u32[]{:S(2)}) collective-permute-start(s32[896,128]{1,0:T(8,128)S(1)} %shard_map.151.own_ref), channel_id=1, source_target_pairs={{0,3},{1,0},{2,1},{3,2},{4,7},{5,4},{6,5},{7,6},{8,11},{9,8},{10,9... | collective-permute-start | bytes 1376264 | tf_op jit(solution)/shard_map/ppermute | solution.py:575
  41.4 14.9 %collective-permute-start.4 = (s32[896,128]{1,0:T(8,128)S(1)}, s32[896,128]{1,0:T(8,128)S(1)}, u32[]{:S(2)}, u32[]{:S(2)}) collective-permute-start(s32[896,128]{1,0:T(8,128)S(1)} %shard_map.151.own_ref), channel_id=1, source_target_pairs={{0,4},{4,0},{8,12},{12,8},{16,20},{20,16},{24,28},{28,24},{32,36},... | collective-permute-start | bytes 1376264 | tf_op jit(solution)/shard_map/ppermute | solution.py:580
  51.6 4.8 %collective-permute-start.5 = (s32[896,128]{1,0:T(8,128)S(1)}, s32[896,128]{1,0:T(8,128)S(1)}, u32[]{:S(2)}, u32[]{:S(2)}) collective-permute-start(s32[896,128]{1,0:T(8,128)S(1)} %collective-permute-done.left_ref), channel_id=1, source_target_pairs={{0,4},{4,0},{8,12},{12,8},{16,20},{20,16},{24,28},{28,24},{32,36},... | collective-permute-start | bytes 1376264 | tf_op jit(solution)/shard_map/ppermute | solution.py:580
  52.9 8.5 %collective-permute-start.1 = (s32[448,128]{1,0:T(8,128)S(1)}, s32[448,128]{1,0:T(8,128)S(1)}, u32[]{:S(2)}, u32[]{:S(2)}) collective-permute-start(s32[448,128]{1,0:T(8,128)S(1)} %slice.19), channel_id=1, source_target_pairs={{0,1},{1,2},{2,3},{3,0},{4,5},{5,6},{6,7},{7,4},{8,9},{9,10},{10,1... | collective-permute-start | bytes 688136 | tf_op jit(solution)/shard_map/ppermute | solution.py:575
  53.1 9.2 %copy-start = (bf16[352,88]{1,0:T(8,128)(2,1)S(1)}, bf16[352,88]{1,0:T(8,128)(2,1)}, u32[]{:S(2)}) copy-start(bf16[352,88]{1,0:T(8,128)(2,1)} %constant.62.clone.both_ref) | copy-start | bytes 185860
  53.1 9.2 %copy-start.3 = (f32[2,128]{1,0:T(2,128)S(1)}, f32[2,128]{1,0:T(2,128)}, u32[]{:S(2)}) copy-start(f32[2,128]{1,0:T(2,128)} %metric_ref.3) | copy-start | bytes 3076
  53.1 8.4 %collective-permute-start.3 = (s32[448,128]{1,0:T(8,128)S(1)}, s32[448,128]{1,0:T(8,128)}, u32[]{:S(2)}, u32[]{:S(2)}) collective-permute-start(s32[448,128]{1,0:T(8,128)S(1)} %slice.20), channel_id=1, source_target_pairs={{0,3},{1,0},{2,1},{3,2},{4,7},{5,4},{6,5},{7,6},{8,11},{9,8},{10,9... | collective-permute-start | bytes 688136 | tf_op jit(solution)/shard_map/ppermute | solution.py:575
  55.8 8.4 %collective-permute-start.6 = (s32[896,128]{1,0:T(8,128)S(1)}, s32[896,128]{1,0:T(8,128)S(1)}, u32[]{:S(2)}, u32[]{:S(2)}) collective-permute-start(s32[896,128]{1,0:T(8,128)S(1)} %collective-permute-done.2.right_ref), channel_id=1, source_target_pairs={{0,4},{4,0},{8,12},{12,8},{16,20},{20,16},{24,28},{28,24},{32,36},... | collective-permute-start | bytes 1376264 | tf_op jit(solution)/shard_map/ppermute | solution.py:580
  61.5 2.7 %collective-permute-start.7 = (s32[448,128]{1,0:T(8,128)S(1)}, s32[448,128]{1,0:T(8,128)S(1)}, u32[]{:S(2)}, u32[]{:S(2)}) collective-permute-start(s32[448,128]{1,0:T(8,128)S(1)} %collective-permute-done.1.oa_ref), channel_id=1, source_target_pairs={{0,4},{4,0},{8,12},{12,8},{16,20},{20,16},{24,28},{28,24},{32,36},... | collective-permute-start | bytes 688136 | tf_op jit(solution)/shard_map/ppermute | solution.py:580
  62.2 2.0 %collective-permute-start.8 = (s32[448,128]{1,0:T(8,128)}, s32[448,128]{1,0:T(8,128)S(1)}, u32[]{:S(2)}, u32[]{:S(2)}) collective-permute-start(s32[448,128]{1,0:T(8,128)} %collective-permute-done.3.ob_ref), channel_id=1, source_target_pairs={{0,4},{4,0},{8,12},{12,8},{16,20},{20,16},{24,28},{28,24},{32,36},... | collective-permute-start | bytes 688136 | tf_op jit(solution)/shard_map/ppermute | solution.py:580
  64.2 50.1 %copy-start.2 = (f32[4,1024]{1,0:T(4,128)S(1)}, f32[4,1024]{1,0:T(4,128)}, u32[]{:S(2)}) copy-start(f32[4,1024]{1,0:T(4,128)} %weight_ref.1) | copy-start | bytes 49156
  107.4 4.2 %collective-permute-start.10 = (f32[4,1024]{1,0:T(4,128)S(1)}, f32[4,1024]{1,0:T(4,128)S(1)}, u32[]{:S(2)}, u32[]{:S(2)}) collective-permute-start(f32[4,1024]{1,0:T(4,128)S(1)} %shard_map.156.p0_ref), channel_id=1, source_target_pairs={{0,2},{1,3},{2,0},{3,1},{4,6},{5,7},{6,4},{7,5},{8,10},{9,11},{10,... | collective-permute-start | bytes 49160 | tf_op jit(solution)/shard_map/ppermute | solution.py:575
  109.0 3.6 %collective-permute-start.11 = (f32[4,1024]{1,0:T(4,128)S(1)}, f32[4,1024]{1,0:T(4,128)S(1)}, u32[]{:S(2)}, u32[]{:S(2)}) collective-permute-start(f32[4,1024]{1,0:T(4,128)S(1)} %shard_map.156.p0_ref), channel_id=1, source_target_pairs={{0,3},{1,0},{2,1},{3,2},{4,7},{5,4},{6,5},{7,6},{8,11},{9,8},{10,9... | collective-permute-start | bytes 49160 | tf_op jit(solution)/shard_map/ppermute | solution.py:575
  110.5 3.8 %collective-permute-start.9 = (f32[4,1024]{1,0:T(4,128)S(1)}, f32[4,1024]{1,0:T(4,128)S(1)}, u32[]{:S(2)}, u32[]{:S(2)}) collective-permute-start(f32[4,1024]{1,0:T(4,128)S(1)} %shard_map.156.p0_ref), channel_id=1, source_target_pairs={{0,1},{1,2},{2,3},{3,0},{4,5},{5,6},{6,7},{7,4},{8,9},{9,10},{10,1... | collective-permute-start | bytes 49160 | tf_op jit(solution)/shard_map/ppermute | solution.py:575
  115.0 16.4 %all-to-all-start.3 = ((f32[64,1,128]{2,1,0:T(1,128)}), f32[64,1,128]{2,1,0:T(1,128)S(1)}, u32[]{:S(2)}, u32[]{:S(2)}) async-start(f32[64,1,128]{2,1,0:T(1,128)} %get-tuple-element.29), calls=%async_computation.3 | async-start | bytes 65536 | tf_op jit(solution)/shard_map/all_to_all | solution.py:613

commit v8 on v7

--- a/solution.py
+++ b/solution.py
@@ -164,15 +164,14 @@
 
 
 def turn_kernel(own_ref, o_ref):
-    for g in range(LINES // 8):
-        lines = [own_ref[:, 4 * g + b, :] for b in range(4)]
-        o_ref[g * 128 : (g + 1) * 128, :] = jnp.concatenate(lines, axis=0).T
+    for k in range(LINES // 2):
+        o_ref[k] = own_ref[:, k, :]
 
 
 def turn_own(own):
     return pl.pallas_call(
         turn_kernel,
-        out_shape=jax.ShapeDtypeStruct((LINES // 8 * 128, 128), jnp.int32),
+        out_shape=jax.ShapeDtypeStruct((LINES // 2, 32, 128), jnp.int32),
         in_specs=[vmem_spec()],
         out_specs=vmem_spec(),
         compiler_params=params(),
@@ -236,31 +235,11 @@
     )
 
 
-def regroup(blocks):
-    lane = lax.broadcasted_iota(jnp.int32, blocks[0].shape, 1)
-
-    def exchange(a, b, keep, width):
-        return jnp.where(keep, a, pltpu.roll(b, width, 1)), jnp.where(
-            keep, pltpu.roll(a, 128 - width, 1), b
-        )
-
-    low = lane < 64
-    p0, p2 = exchange(blocks[0], blocks[2], low, 64)
-    p1, p3 = exchange(blocks[1], blocks[3], low, 64)
-    even = (lane & 32) == 0
-    p0, p1 = exchange(p0, p1, even, 32)
-    p2, p3 = exchange(p2, p3, even, 32)
-    return p0, p1, p2, p3
-
-
-def spread_rows(pieces, k, ht):
-    blocks = regroup([ref[pl.ds(pl.multiple_of((k - f) * 32, 32), 32), :] for ref, f in pieces])
-    start = (k >> 2) * 512 + (k & 3) * 32
-    for b in range(4):
-        row = pl.multiple_of(start + b * 128, 32)
-        ht[pl.ds(row, 32), :] = low_of(blocks[b])
-        row = pl.multiple_of(start + b * 128 + LINES * 64, 32)
-        ht[pl.ds(row, 32), :] = high_of(blocks[b])
+def spread_line(pieces, k, ht):
+    pair = jnp.concatenate([ref[k - f] for ref, f in pieces], axis=0).T
+    ht[k * 128 : (k + 1) * 128, :] = low_of(pair)
+    row = (k + LINES // 2) * 128
+    ht[row : row + 128, :] = high_of(pair)
 
 
 def row_scales(ht, rows):
@@ -274,7 +253,7 @@
     copies = []
     for g in range(LINES // 8):
         for k in range(4 * g, 4 * g + 4):
-            spread_rows([(r, 0) for r in (own_ref, own2_ref, left_ref, left2_ref)], k, ht)
+            spread_line([(r, 0) for r in (own_ref, own2_ref, left_ref, left2_ref)], k, ht)
         for part in range(2):
             block = pl.ds(g * 512 + part * LINES * 64, 512)
             copy = pltpu.make_async_copy(ht.at[block, :], o_ref.at[block, :], sems.at[g, part])
@@ -372,14 +351,10 @@
     load.start()
     halves = (ht0, ht1)
     scales = (rows0, rows1)
-    for first, far in ((0, (oa_ref, oa2_ref)), (14, (ob_ref, ob2_ref))):
-
-        def spread(k, carry, first=first, far=far):
-            near = [(right_ref, 0), (right2_ref, 0)]
-            spread_rows(near + [(ref, first) for ref in far], k, ht1)
-            return carry
-
-        lax.fori_loop(first, first + 14, spread, 0, unroll=7)
+    for k in range(LINES // 2):
+        first, far = (0, (oa_ref, oa2_ref)) if k < 14 else (14, (ob_ref, ob2_ref))
+        near = [(right_ref, 0), (right2_ref, 0)]
+        spread_line(near + [(ref, first) for ref in far], k, ht1)
     load.wait()
     row_scales(ht0, rows0)
     row_scales(ht1, rows1)
@@ -594,8 +569,8 @@
     left = around(own, 1)
     right = around(own, 3)
     points = lax.all_to_all(sent, "span", 0, 0, tiled=True)
-    oa = around(left[:448], 1)
-    ob = around(right[448:], 3)
+    oa = around(left[:14], 1)
+    ob = around(right[14:], 3)
     both = slope_table()
     first, velocity = first_modes(place, metric, points, fwd, both)
     regrouped = regroup_half((own, across(own), left, across(left)))

time: 133 us -> 133 us (level)
  waiting for transfers between devices: 33.4 us -> 34.8 us
    ppermute x7, waiting for transfers between devices: 14.1 us -> 15.5 us  [around(): lax.ppermute(block, 'plane', [(i, (i + step) % plane_count) for i in rang...]
    pallas_call x1, Pallas kernels: 3.45 us -> 2.05 us  [regroup_half(): pl.pallas_call(regroup_kernel, out_shape=pltpu.HBM((LINES * 128, 128), F3...]
  transfers between devices with their start and end apart: 15 -> 15, of which waited for: 7 -> 7; matrix products, arithmetic and copies ran while one was open for 2% -> 2% of each run, Pallas kernels for 6% -> 5%
where the time goes in v8:
time: 133 us; the launch traced here: 132 us
  starting transfers between devices  39.1 us (29%)
  waiting for transfers between devices  34.8 us (26%)
  Pallas kernels  27.7 us (21%)
  blocking collectives  25.3 us (19%)
  local copies, waits for them, and re-layouts  3.87 us (3%)
    all_to_all x1, blocking collectives, on_device(): received = lax.all_to_all(out, 'span', 0, 0, tiled=True)  25.3 us
    pallas_call x1, Pallas kernels, steps(): pl.pallas_call(steps_kernel, out_shape=jax.ShapeDtypeStruct((64, 4, 384),...  16.7 us
    ppermute x7, waiting for transfers between devices, around(): lax.ppermute(block, 'plane', [(i, (i + step) % plane_count) for i in rang...  15.5 us
    all_to_all x1, starting transfers between devices, on_device(): lax.all_to_all(pack_inverse(which, helmholtz_inverse, span_count // 2), '...  12 us
    all_to_all x1, waiting for transfers between devices, on_device(): lax.all_to_all(pack_inverse(which, helmholtz_inverse, span_count // 2), '...  11.2 us
    ppermute x7, starting transfers between devices, around(): lax.ppermute(block, 'plane', [(i, (i + step) % plane_count) for i in rang...  9.14 us
    all_to_all x1, waiting for transfers between devices, on_device(): squares = lax.all_to_all(square, 'span', 0, 0, tiled=True)  8.04 us
    all_to_all x1, starting transfers between devices, on_device(): points = lax.all_to_all(sent, 'span', 0, 0, tiled=True)  7.24 us
  transfers between devices with their start and end apart: 15, of which 7 were waited for; matrix products, arithmetic and copies ran while one was open for 2% of the time, Pallas kernels for 5%

profile of v8, /device:TPU:1, one launch (start us, length us, event | category | flops | bytes accessed | tf_op | source)
XLA Modules:
  0.0 132.3 jit_solution(17766912903723541285)
XLA Ops:
  0.6 0.0 copy-start.7
  0.6 0.0 copy-start.1
  0.7 0.9 copy-done.1
  1.6 1.2 shard_map.149
  2.8 12.0 %all-to-all-start = ((s32[32,32,128]{2,1,0:T(8,128)}), s32[32,32,128]{2,1,0:T(8,128)S(1)}, u32[]{:S(2)}, u32[]{:S(2)}) async-start(s32[32,32,128]{2,1,0:T(8,128)} %shard_map.149), calls=%async_computation | async-start | bytes 1048576 | tf_op jit(solution)/shard_map/all_to_all | solution.py:559
  14.9 0.0 copy-done.7
  14.9 0.0 copy-done.5
  14.9 0.0 copy-start.8
  14.9 0.0 copy-start.4
  14.9 0.2 copy.17.c0_ref.c1_ref.c2_ref
  15.2 1.1 copy.16.adj_ref
  16.2 0.0 copy-done.8
  16.3 0.1 pad_add_fusion.place_ref
  16.3 0.0 copy-done.4
  16.4 0.0 copy-start.12
  16.4 2.2 %shard_map.150 = s32[64,8,384]{2,1,0:T(8,128)} custom-call(s32[3]{0:T(128)S(1)} %copy-done.4, f32[3,4,81,128]{3,2,1,0:T(8,128)S(1)} %copy.16.adj_ref, bf16[8,2,4,81,128]{4,3,2,1,0:T(8,128)(2,1)S(1)} %copy.17.c0_ref.c1_ref.c2_ref, bf16[8,2,4,81,128]{4,3,2,1,0:T(8,128)(2,1)S(1)} %copy.17.c0_ref.c1_ref.c2_ref, ...), custom_call_target="tpu_custom_call" | custom-call | tf_op jit(solution)/shard_map/pallas_call | solution.py:212
  18.6 0.0 copy-done.9
  18.6 0.0 copy-done.10
  18.6 0.0 copy-done.11
  18.7 0.3 convolution_convert_fusion.1
  19.0 0.6 copy-done.6
  19.6 0.3 fusion.fwd_ref
  19.9 11.2 %all-to-all-done.own_ref = s32[32,32,128]{2,1,0:T(8,128)S(1)} async-done(((s32[32,32,128]{2,1,0:T(8,128)}), s32[32,32,128]{2,1,0:T(8,128)S(1)}, u32[]{:S(2)}, u32[]{:S(2)}) %all-to-all-start) | async-done | bytes 524320 | tf_op jit(solution)/shard_map/all_to_all | solution.py:559
  31.1 7.2 %all-to-all-start.1 = ((s32[64,8,384]{2,1,0:T(8,128)}), s32[64,8,384]{2,1,0:T(8,128)S(1)}, u32[]{:S(2)}, u32[]{:S(2)}) async-start(s32[64,8,384]{2,1,0:T(8,128)} %shard_map.150), calls=%async_computation.1 | async-start | bytes 1572864 | tf_op jit(solution)/shard_map/all_to_all | solution.py:571
  38.4 0.3 shard_map.151.own_ref
  38.6 1.3 collective-permute-start
  39.9 1.5 %collective-permute-start.2 = (s32[28,32,128]{2,1,0:T(8,128)S(1)}, s32[28,32,128]{2,1,0:T(8,128)S(1)}, u32[]{:S(2)}, u32[]{:S(2)}) collective-permute-start(s32[28,32,128]{2,1,0:T(8,128)S(1)} %shard_map.151.own_ref), channel_id=1, source_target_pairs={{0,3},{1,0},{2,1},{3,2},{4,7},{5,4},{6,5},{7,6},{8,11},{9,8},{10,9... | collective-permute-start | bytes 1376264 | tf_op jit(solution)/shard_map/ppermute | solution.py:550
  41.4 1.0 collective-permute-start.4
  42.4 9.2 %collective-permute-done.left_ref = s32[28,32,128]{2,1,0:T(8,128)S(1)} collective-permute-done((s32[28,32,128]{2,1,0:T(8,128)S(1)}, s32[28,32,128]{2,1,0:T(8,128)S(1)}, u32[]{:S(2)}, u32[]{:S(2)}) %collective-permute-start) | collective-permute-done | bytes 458784 | tf_op jit(solution)/shard_map/ppermute | solution.py:550
  51.6 1.3 collective-permute-start.5
  52.9 0.1 collective-permute-start.1
  53.0 0.0 collective-permute-done.2.right_ref
  53.0 0.0 copy-start
  53.0 0.0 copy-start.3
  53.0 2.7 %collective-permute-start.3 = (s32[14,32,128]{2,1,0:T(8,128)S(1)}, s32[14,32,128]{2,1,0:T(8,128)}, u32[]{:S(2)}, u32[]{:S(2)}) collective-permute-start(s32[14,32,128]{2,1,0:T(8,128)S(1)} %slice.20), channel_id=1, source_target_pairs={{0,3},{1,0},{2,1},{3,2},{4,7},{5,4},{6,5},{7,6},{8,11},{9,8},{10,9... | collective-permute-start | bytes 688136 | tf_op jit(solution)/shard_map/ppermute | solution.py:550
  55.8 0.6 collective-permute-start.6
  56.3 0.0 collective-permute-done.4.own2_ref
  56.3 0.0 collective-permute-done.5.left2_ref
  56.3 2.1 %shard_map.152.regrouped_ref = f32[7168,128]{1,0:T(8,128)} custom-call(s32[28,32,128]{2,1,0:T(8,128)S(1)} %shard_map.151.own_ref, s32[28,32,128]{2,1,0:T(8,128)S(1)} %collective-permute-done.4.own2_ref, s32[28,32,128]{2,1,0:T(8,128)S(1)} %collective-permute-done.left_ref, s32[28,32,128]{2,1,0:T(8,128)S(1)} %collective-permute-done.5.left2_ref), custom_call_target="tpu_custom_call" | custom-call | tf_op jit(solution)/shard_map/pallas_call | solution.py:267
  58.4 3.0 %collective-permute-done.1.oa_ref = s32[14,32,128]{2,1,0:T(8,128)S(1)} collective-permute-done((s32[14,32,128]{2,1,0:T(8,128)S(1)}, s32[14,32,128]{2,1,0:T(8,128)S(1)}, u32[]{:S(2)}, u32[]{:S(2)}) %collective-permute-start.1) | collective-permute-done | bytes 229408 | tf_op jit(solution)/shard_map/ppermute | solution.py:550
  61.4 0.0 collective-permute-done.3.ob_ref
  61.4 0.8 collective-permute-start.7
  62.2 0.0 collective-permute-start.8
  62.2 0.0 all-to-all-done.1.r_ref
  62.2 1.9 %shard_map.153 = (f32[2,528,128]{2,1,0:T(8,128)S(1)}, f32[2,2,3,88,256]{4,3,2,1,0:T(8,128)S(1)}) custom-call(s32[2]{0:T(128)S(1)} %pad_add_fusion.place_ref, f32[2,128]{1,0:T(2,128)S(1)} %copy-done.3, s32[64,8,384]{2,1,0:T(8,128)S(1)} %all-to-all-done.1.r_ref, bf16[768,256]{1,0:T(8,128)(2,1)S(1)} %fusion.fwd_ref, bf16[352,88]{1,0:T(8,128)(2,1)S(1)} %copy-done), custom_call_target="tpu_custom_call" | custom-call | tf_op jit(solution)/shard_map/pallas_call | solution.py:331
  64.1 0.0 collective-permute-done.6.right2_ref
  64.1 0.0 collective-permute-done.7.oa2_ref
  64.1 0.0 collective-permute-done.8.ob2_ref
  64.2 0.0 copy-start.2
  64.2 16.7 %shard_map.154 = s32[64,4,384]{2,1,0:T(4,128)S(1)} custom-call(s32[2]{0:T(128)S(1)} %pad_add_fusion.place_ref, f32[2,128]{1,0:T(2,128)S(1)} %copy-done.3, f32[7168,128]{1,0:T(8,128)} %shard_map.152.regrouped_ref, s32[28,32,128]{2,1,0:T(8,128)S(1)} %collective-permute-done.2.right_ref, s32[28,32,128]{2,1,0:T(8,128)S(1)} %collective-permute-done.6.right2_ref, ...), custom_call_target="tpu_custom_call" | custom-call | tf_op jit(solution)/shard_map/pallas_call | solution.py:417
  80.8 25.3 %all_to_all.20.r_ref = s32[64,4,384]{2,1,0:T(4,128)S(1)} all-to-all(s32[64,4,384]{2,1,0:T(4,128)S(1)} %shard_map.154), channel_id=1, replica_groups=mesh['span'=64,'plane'=4] {'span'}, dimensions={0} | all-to-all | bytes 786432 | tf_op jit(solution)/shard_map/all_to_all | solution.py:583
  106.1 1.5 %shard_map.156.p0_ref = f32[4,1024]{1,0:T(4,128)S(1)} custom-call(s32[64,4,384]{2,1,0:T(4,128)S(1)} %all_to_all.20.r_ref, s32[1,2048]{1,0:T(1,128)S(1)} %bitcast.19, s32[1,2048]{1,0:T(1,128)S(1)} %bitcast.18), custom_call_target="tpu_custom_call" | custom-call | tf_op jit(solution)/shard_map/pallas_call | solution.py:458
  107.6 1.6 %collective-permute-start.10 = (f32[4,1024]{1,0:T(4,128)S(1)}, f32[4,1024]{1,0:T(4,128)S(1)}, u32[]{:S(2)}, u32[]{:S(2)}) collective-permute-start(f32[4,1024]{1,0:T(4,128)S(1)} %shard_map.156.p0_ref), channel_id=1, source_target_pairs={{0,2},{1,3},{2,0},{3,1},{4,6},{5,7},{6,4},{7,5},{8,10},{9,11},{10,... | collective-permute-start | bytes 49160 | tf_op jit(solution)/shard_map/ppermute | solution.py:550
  109.1 1.5 %collective-permute-start.11 = (f32[4,1024]{1,0:T(4,128)S(1)}, f32[4,1024]{1,0:T(4,128)S(1)}, u32[]{:S(2)}, u32[]{:S(2)}) collective-permute-start(f32[4,1024]{1,0:T(4,128)S(1)} %shard_map.156.p0_ref), channel_id=1, source_target_pairs={{0,3},{1,0},{2,1},{3,2},{4,7},{5,4},{6,5},{7,6},{8,11},{9,8},{10,9... | collective-permute-start | bytes 49160 | tf_op jit(solution)/shard_map/ppermute | solution.py:550
  110.7 0.5 collective-permute-start.9
  111.2 0.6 collective-permute-done.10.p2_ref
  111.8 1.0 collective-permute-done.11.p3_ref
  112.8 1.7 %collective-permute-done.9.p1_ref = f32[4,1024]{1,0:T(4,128)S(1)} collective-permute-done((f32[4,1024]{1,0:T(4,128)S(1)}, f32[4,1024]{1,0:T(4,128)S(1)}, u32[]{:S(2)}, u32[]{:S(2)}) %collective-permute-start.9) | collective-permute-done | bytes 16416 | tf_op jit(solution)/shard_map/ppermute | solution.py:550
  114.5 0.7 shard_map.157
  115.2 7.0 %all-to-all-start.3 = ((f32[64,1,128]{2,1,0:T(1,128)}), f32[64,1,128]{2,1,0:T(1,128)S(1)}, u32[]{:S(2)}, u32[]{:S(2)}) async-start(f32[64,1,128]{2,1,0:T(1,128)} %get-tuple-element.29), calls=%async_computation.3 | async-start | bytes 65536 | tf_op jit(solution)/shard_map/all_to_all | solution.py:588
  122.2 0.4 shard_map.155
  122.7 0.9 copy.21
  123.6 8.0 %all-to-all-done.3.squares_ref = f32[64,1,128]{2,1,0:T(1,128)S(1)} async-done(((f32[64,1,128]{2,1,0:T(1,128)}), f32[64,1,128]{2,1,0:T(1,128)S(1)}, u32[]{:S(2)}, u32[]{:S(2)}) %all-to-all-start.3) | async-done | bytes 32800 | tf_op jit(solution)/shard_map/all_to_all | solution.py:588
  131.6 0.7 shard_map.158
  (17 shorter events, 0.1 us)
Async XLA Ops:
  0.6 14.2 %copy-start.7 = (s32[1024,2]{0,1:T(2,128)S(1)}, s32[1024,2]{0,1:T(2,128)}, u32[]{:S(2)}) copy-start(s32[1024,2]{0,1:T(2,128)} %param.19) | copy-start | bytes 24580
  0.6 0.9 copy-start.1
  1.6 13.3 %copy-start.5 = (bf16[8,2,4,81,128]{4,2,3,1,0:T(4,128)(2,1)S(1)}, bf16[8,2,4,81,128]{4,2,3,1,0:T(4,128)(2,1)}, u32[]{:S(2)}) copy-start(bf16[8,2,4,81,128]{4,2,3,1,0:T(4,128)(2,1)} %param.15) | copy-start | bytes 3981316
  2.8 28.3 %all-to-all-start = ((s32[32,32,128]{2,1,0:T(8,128)}), s32[32,32,128]{2,1,0:T(8,128)S(1)}, u32[]{:S(2)}, u32[]{:S(2)}) async-start(s32[32,32,128]{2,1,0:T(8,128)} %shard_map.149), calls=%async_computation | async-start | bytes 1048576 | tf_op jit(solution)/shard_map/all_to_all | solution.py:559
  14.9 1.3 %copy-start.8 = (s32[1024,2]{0,1:T(2,128)S(1)}, s32[1024,2]{0,1:T(2,128)}, u32[]{:S(2)}) copy-start(s32[1024,2]{0,1:T(2,128)} %param.20) | copy-start | bytes 24580
  14.9 1.4 %copy-start.4 = (s32[3]{0:T(128)S(1)}, s32[3]{0:T(128)}, u32[]{:S(2)}) copy-start(s32[3]{0:T(128)} %step_ref.1) | copy-start | bytes 40
  16.3 2.3 %copy-start.9 = (s32[256]{0:T(256)S(1)}, s32[256]{0:T(256)}, u32[]{:S(2)}) copy-start(s32[256]{0:T(256)} %constant.59.clone) | copy-start | bytes 3076
  16.3 2.3 %copy-start.10 = (s32[256]{0:T(256)S(1)}, s32[256]{0:T(256)}, u32[]{:S(2)}) copy-start(s32[256]{0:T(256)} %constant.68) | copy-start | bytes 3076
  16.4 2.3 %copy-start.11 = (s32[256]{0:T(256)S(1)}, s32[256]{0:T(256)}, u32[]{:S(2)}) copy-start(s32[256]{0:T(256)} %constant.70) | copy-start | bytes 3076
  16.4 2.3 %copy-start.12 = (bf16[256,512]{1,0:T(8,128)(2,1)S(1)}, bf16[256,512]{1,0:T(8,128)(2,1)}, u32[]{:S(2)}) copy-start(bf16[256,512]{1,0:T(8,128)(2,1)} %constant.60.clone) | copy-start | bytes 786436
  18.6 1.0 copy-start.6
  31.1 31.1 %all-to-all-start.1 = ((s32[64,8,384]{2,1,0:T(8,128)}), s32[64,8,384]{2,1,0:T(8,128)S(1)}, u32[]{:S(2)}, u32[]{:S(2)}) async-start(s32[64,8,384]{2,1,0:T(8,128)} %shard_map.150), calls=%async_computation.1 | async-start | bytes 1572864 | tf_op jit(solution)/shard_map/all_to_all | solution.py:571
  38.6 12.9 %collective-permute-start = (s32[28,32,128]{2,1,0:T(8,128)S(1)}, s32[28,32,128]{2,1,0:T(8,128)S(1)}, u32[]{:S(2)}, u32[]{:S(2)}) collective-permute-start(s32[28,32,128]{2,1,0:T(8,128)S(1)} %shard_map.151.own_ref), channel_id=1, source_target_pairs={{0,1},{1,2},{2,3},{3,0},{4,5},{5,6},{6,7},{7,4},{8,9},{9,10},{10,1... | collective-permute-start | bytes 1376264 | tf_op jit(solution)/shard_map/ppermute | solution.py:550
  39.9 13.0 %collective-permute-start.2 = (s32[28,32,128]{2,1,0:T(8,128)S(1)}, s32[28,32,128]{2,1,0:T(8,128)S(1)}, u32[]{:S(2)}, u32[]{:S(2)}) collective-permute-start(s32[28,32,128]{2,1,0:T(8,128)S(1)} %shard_map.151.own_ref), channel_id=1, source_target_pairs={{0,3},{1,0},{2,1},{3,2},{4,7},{5,4},{6,5},{7,6},{8,11},{9,8},{10,9... | collective-permute-start | bytes 1376264 | tf_op jit(solution)/shard_map/ppermute | solution.py:550
  41.4 14.9 %collective-permute-start.4 = (s32[28,32,128]{2,1,0:T(8,128)S(1)}, s32[28,32,128]{2,1,0:T(8,128)S(1)}, u32[]{:S(2)}, u32[]{:S(2)}) collective-permute-start(s32[28,32,128]{2,1,0:T(8,128)S(1)} %shard_map.151.own_ref), channel_id=1, source_target_pairs={{0,4},{4,0},{8,12},{12,8},{16,20},{20,16},{24,28},{28,24},{32,36},... | collective-permute-start | bytes 1376264 | tf_op jit(solution)/shard_map/ppermute | solution.py:555
  51.6 4.8 %collective-permute-start.5 = (s32[28,32,128]{2,1,0:T(8,128)S(1)}, s32[28,32,128]{2,1,0:T(8,128)S(1)}, u32[]{:S(2)}, u32[]{:S(2)}) collective-permute-start(s32[28,32,128]{2,1,0:T(8,128)S(1)} %collective-permute-done.left_ref), channel_id=1, source_target_pairs={{0,4},{4,0},{8,12},{12,8},{16,20},{20,16},{24,28},{28,24},{32,36},... | collective-permute-start | bytes 1376264 | tf_op jit(solution)/shard_map/ppermute | solution.py:555
  52.9 8.5 %collective-permute-start.1 = (s32[14,32,128]{2,1,0:T(8,128)S(1)}, s32[14,32,128]{2,1,0:T(8,128)S(1)}, u32[]{:S(2)}, u32[]{:S(2)}) collective-permute-start(s32[14,32,128]{2,1,0:T(8,128)S(1)} %slice.19), channel_id=1, source_target_pairs={{0,1},{1,2},{2,3},{3,0},{4,5},{5,6},{6,7},{7,4},{8,9},{9,10},{10,1... | collective-permute-start | bytes 688136 | tf_op jit(solution)/shard_map/ppermute | solution.py:550
  53.0 9.2 %copy-start = (bf16[352,88]{1,0:T(8,128)(2,1)S(1)}, bf16[352,88]{1,0:T(8,128)(2,1)}, u32[]{:S(2)}) copy-start(bf16[352,88]{1,0:T(8,128)(2,1)} %constant.62.clone.both_ref) | copy-start | bytes 185860
  53.0 9.2 %copy-start.3 = (f32[2,128]{1,0:T(2,128)S(1)}, f32[2,128]{1,0:T(2,128)}, u32[]{:S(2)}) copy-start(f32[2,128]{1,0:T(2,128)} %metric_ref.3) | copy-start | bytes 3076
  53.0 8.4 %collective-permute-start.3 = (s32[14,32,128]{2,1,0:T(8,128)S(1)}, s32[14,32,128]{2,1,0:T(8,128)}, u32[]{:S(2)}, u32[]{:S(2)}) collective-permute-start(s32[14,32,128]{2,1,0:T(8,128)S(1)} %slice.20), channel_id=1, source_target_pairs={{0,3},{1,0},{2,1},{3,2},{4,7},{5,4},{6,5},{7,6},{8,11},{9,8},{10,9... | collective-permute-start | bytes 688136 | tf_op jit(solution)/shard_map/ppermute | solution.py:550
  55.8 8.4 %collective-permute-start.6 = (s32[28,32,128]{2,1,0:T(8,128)S(1)}, s32[28,32,128]{2,1,0:T(8,128)S(1)}, u32[]{:S(2)}, u32[]{:S(2)}) collective-permute-start(s32[28,32,128]{2,1,0:T(8,128)S(1)} %collective-permute-done.2.right_ref), channel_id=1, source_target_pairs={{0,4},{4,0},{8,12},{12,8},{16,20},{20,16},{24,28},{28,24},{32,36},... | collective-permute-start | bytes 1376264 | tf_op jit(solution)/shard_map/ppermute | solution.py:555
  61.4 2.7 %collective-permute-start.7 = (s32[14,32,128]{2,1,0:T(8,128)S(1)}, s32[14,32,128]{2,1,0:T(8,128)S(1)}, u32[]{:S(2)}, u32[]{:S(2)}) collective-permute-start(s32[14,32,128]{2,1,0:T(8,128)S(1)} %collective-permute-done.1.oa_ref), channel_id=1, source_target_pairs={{0,4},{4,0},{8,12},{12,8},{16,20},{20,16},{24,28},{28,24},{32,36},... | collective-permute-start | bytes 688136 | tf_op jit(solution)/shard_map/ppermute | solution.py:555
  62.2 2.0 %collective-permute-start.8 = (s32[14,32,128]{2,1,0:T(8,128)}, s32[14,32,128]{2,1,0:T(8,128)S(1)}, u32[]{:S(2)}, u32[]{:S(2)}) collective-permute-start(s32[14,32,128]{2,1,0:T(8,128)} %collective-permute-done.3.ob_ref), channel_id=1, source_target_pairs={{0,4},{4,0},{8,12},{12,8},{16,20},{20,16},{24,28},{28,24},{32,36},... | collective-permute-start | bytes 688136 | tf_op jit(solution)/shard_map/ppermute | solution.py:555
  64.2 50.3 %copy-start.2 = (f32[4,1024]{1,0:T(4,128)S(1)}, f32[4,1024]{1,0:T(4,128)}, u32[]{:S(2)}) copy-start(f32[4,1024]{1,0:T(4,128)} %weight_ref.1) | copy-start | bytes 49156
  107.6 4.2 %collective-permute-start.10 = (f32[4,1024]{1,0:T(4,128)S(1)}, f32[4,1024]{1,0:T(4,128)S(1)}, u32[]{:S(2)}, u32[]{:S(2)}) collective-permute-start(f32[4,1024]{1,0:T(4,128)S(1)} %shard_map.156.p0_ref), channel_id=1, source_target_pairs={{0,2},{1,3},{2,0},{3,1},{4,6},{5,7},{6,4},{7,5},{8,10},{9,11},{10,... | collective-permute-start | bytes 49160 | tf_op jit(solution)/shard_map/ppermute | solution.py:550
  109.1 3.6 %collective-permute-start.11 = (f32[4,1024]{1,0:T(4,128)S(1)}, f32[4,1024]{1,0:T(4,128)S(1)}, u32[]{:S(2)}, u32[]{:S(2)}) collective-permute-start(f32[4,1024]{1,0:T(4,128)S(1)} %shard_map.156.p0_ref), channel_id=1, source_target_pairs={{0,3},{1,0},{2,1},{3,2},{4,7},{5,4},{6,5},{7,6},{8,11},{9,8},{10,9... | collective-permute-start | bytes 49160 | tf_op jit(solution)/shard_map/ppermute | solution.py:550
  110.7 3.8 %collective-permute-start.9 = (f32[4,1024]{1,0:T(4,128)S(1)}, f32[4,1024]{1,0:T(4,128)S(1)}, u32[]{:S(2)}, u32[]{:S(2)}) collective-permute-start(f32[4,1024]{1,0:T(4,128)S(1)} %shard_map.156.p0_ref), channel_id=1, source_target_pairs={{0,1},{1,2},{2,3},{3,0},{4,5},{5,6},{6,7},{7,4},{8,9},{9,10},{10,1... | collective-permute-start | bytes 49160 | tf_op jit(solution)/shard_map/ppermute | solution.py:550
  115.2 16.4 %all-to-all-start.3 = ((f32[64,1,128]{2,1,0:T(1,128)}), f32[64,1,128]{2,1,0:T(1,128)S(1)}, u32[]{:S(2)}, u32[]{:S(2)}) async-start(f32[64,1,128]{2,1,0:T(1,128)} %get-tuple-element.29), calls=%async_computation.3 | async-start | bytes 65536 | tf_op jit(solution)/shard_map/all_to_all | solution.py:588
